TPU v7x, 32 devices: a whole 2x2x4 slice. The times are simulated.
32 devices in a mesh: member: 2 (over y), seq: 16 (over z, x, core).
Axes of the slice: x: 2, y: 2, z: 4, core: 2. Of those that a mesh axis runs over, the one named last changes fastest.
Arguments:
- hidden: bfloat16 [2, 6144, 2880], P('member', 'seq'), may hold values from -6 to 6
- segments: int32 [6144], replicated, may hold values from 0 to 31, never falling along the last dimension, each value on 1 to 768 neighbouring positions
- pre_gain: float32 [2, 2880], P('member'), may hold values from 0.5 to 1.5
- w_query: bfloat16 [2, 2880, 2048], P('member', 'seq'), may hold values from -3 to 3
- w_key: bfloat16 [2, 2880, 256], P('member', 'seq'), may hold values from -3 to 3
- w_value: bfloat16 [2, 2880, 256], P('member', 'seq'), may hold values from -0.109375 to 0.109375
- w_output: bfloat16 [2, 2048, 2880], P('member', 'seq'), may hold values from -0.125 to 0.125
- post_gain: float32 [2, 2880], P('member'), may hold values from 0.5 to 1.5
- final_gain: float32 [2, 2880], P('member'), may hold values from 0.5 to 1.5
- w_judge: bfloat16 [2, 2880, 128], P('member'), may hold values from -0.21875 to 0.21875
Outputs:
- residual_out: bfloat16 [2, 6144, 2880], P('member', 'seq')
- logits: float32 [6144, 128], P('seq')
Inputs may be any that keep to these rules, and one draw needn't show every extreme that they name: `segments`: segment numbers never fall from one token to the next; every number is used, each names 1 to 768 consecutive tokens, and one names exactly 768.
All inputs are finite; a program needn't handle non-finite values.
Results may differ from a plain program's by a relative error of at most 0.014.
Values may be sent and summed in bfloat16 or wider, within the bound.
No kernel may reach another device: no remote copies, remote signals or barrier semaphores. Data moves between devices by JAX's collectives and lax.ppermute only.
A program may use at most 128 MiB of HBM per device.

v0:
```python
import math

import jax
import jax.numpy as jnp
from jax import lax
from jax.sharding import PartitionSpec as P

QH = 32
KVH = 4
HD = 64
WINDOW = 128


epsilon = 1e-06
softcap = 50.0
rope_base = 10000.0


def from_behind(block, axis, distance):
    devices = range(lax.axis_size(axis))
    route = [(i - distance, i) for i in devices if i - distance in devices]
    return lax.ppermute(block, axis, route)


def rms_norm(inputs, scale_gain):
    values = inputs.astype(jnp.float32)
    return (
        values * lax.rsqrt(jnp.mean(values * values, axis=-1, keepdims=True) + epsilon) * scale_gain
    )


def rotate(inputs, positions):
    head_size = inputs.shape[-1]
    half_dim = head_size // 2
    frequency = jnp.exp(
        jnp.arange(half_dim, dtype=jnp.float32) * (-2.0 * math.log(rope_base) / head_size)
    )
    angles = positions.astype(jnp.float32)[:, None] * frequency[None, :]
    cosine_term = jnp.cos(angles)[:, None, :]
    sine_term = jnp.sin(angles)[:, None, :]
    lower_half = inputs[..., :half_dim]
    upper_half = inputs[..., half_dim:]
    return jnp.concatenate(
        [
            lower_half * cosine_term - upper_half * sine_term,
            upper_half * cosine_term + lower_half * sine_term,
        ],
        axis=-1,
    )


def attend_heads(block_queries, block_keys, block_values, seg_query, seg_key):
    query_count = block_queries.shape[0]
    key_count = block_keys.shape[0]
    head_span = QH // KVH * HD
    distance = (
        jnp.arange(query_count, dtype=jnp.int32)[:, None]
        + (key_count - query_count)
        - jnp.arange(key_count, dtype=jnp.int32)[None, :]
    )
    allowed = (distance >= 0) & (distance < WINDOW) & (seg_query[:, None] == seg_key[None, :])

    def one_head(head_index):
        query_head = lax.dynamic_slice_in_dim(
            block_queries, head_index * head_span, head_span, 1
        ).reshape(query_count, QH // KVH, HD)
        key_head = lax.dynamic_slice_in_dim(block_keys, head_index * HD, HD, 1)
        value_head = lax.dynamic_slice_in_dim(block_values, head_index * HD, HD, 1)
        scores = jnp.einsum("qgd,kd->gqk", query_head, key_head, preferred_element_type=jnp.float32)
        scores = softcap * jnp.tanh(scores / softcap)
        expanded = jnp.where(allowed[None], jnp.exp(scores), 0.0)
        weights = (expanded / jnp.sum(expanded, axis=-1, keepdims=True)).astype(jnp.bfloat16)
        head_out = jnp.einsum(
            "gqk,kd->qgd", weights, value_head, preferred_element_type=jnp.float32
        )
        return head_out.astype(jnp.bfloat16).reshape(query_count, head_span)

    per_head = lax.map(one_head, jnp.arange(KVH, dtype=jnp.int32))
    return per_head.transpose(1, 0, 2).reshape(query_count, KVH * head_span)


def body(
    hidden, segments, pre_gain, w_query, w_key, w_value, w_output, post_gain, final_gain, w_judge
):
    tok_rows = hidden.shape[1]
    dev_index = lax.axis_index("seq")
    row_first = dev_index * tok_rows
    own_rows = hidden[0]
    normed = rms_norm(own_rows, pre_gain[0]).astype(jnp.bfloat16)
    earlier = from_behind(normed[tok_rows - WINDOW :], "seq", 1)
    kv_input = jnp.concatenate([earlier, normed], axis=0)
    kv_count = kv_input.shape[0]
    queries = jnp.dot(
        normed,
        lax.all_gather(w_query[0], "seq", axis=0, tiled=True),
        preferred_element_type=jnp.float32,
    )
    key_rows = jnp.dot(
        kv_input,
        lax.all_gather(w_key[0], "seq", axis=0, tiled=True),
        preferred_element_type=jnp.float32,
    )
    val_rows = jnp.dot(
        kv_input,
        lax.all_gather(w_value[0], "seq", axis=0, tiled=True),
        preferred_element_type=jnp.float32,
    )
    query_positions = row_first + jnp.arange(tok_rows, dtype=jnp.int32)
    key_positions = row_first - (kv_count - tok_rows) + jnp.arange(kv_count, dtype=jnp.int32)
    queries = (
        (rotate(queries.reshape(tok_rows, QH, HD), query_positions) * (1.0 / math.sqrt(HD)))
        .astype(jnp.bfloat16)
        .reshape(tok_rows, QH * HD)
    )
    key_rows = (
        rotate(key_rows.reshape(kv_count, KVH, HD), key_positions)
        .astype(jnp.bfloat16)
        .reshape(kv_count, KVH * HD)
    )
    val_rows = val_rows.astype(jnp.bfloat16)
    seg_own = lax.dynamic_slice_in_dim(segments, row_first, tok_rows, 0)
    seg_prior = lax.dynamic_slice_in_dim(segments, jnp.maximum(row_first - WINDOW, 0), WINDOW, 0)
    seg_prior = jnp.where(dev_index > 0, seg_prior, -1)
    seg_keys = jnp.concatenate([seg_prior, seg_own], axis=0)
    block_rows = min(tok_rows, 512)

    def one_block(block_number):
        return attend_heads(queries, key_rows, val_rows, seg_own, seg_keys)

    attended = lax.map(one_block, jnp.arange(tok_rows // block_rows, dtype=jnp.int32)).reshape(
        tok_rows, QH * HD
    )
    projected = jnp.dot(
        attended,
        lax.all_gather(w_output[0], "seq", axis=0, tiled=True),
        preferred_element_type=jnp.float32,
    )
    updated = (own_rows.astype(jnp.float32) + rms_norm(projected, post_gain[0])).astype(
        jnp.bfloat16
    )
    closing = rms_norm(updated, final_gain[0]).astype(jnp.bfloat16)
    verdict = jnp.dot(closing, w_judge[0], preferred_element_type=jnp.float32)
    summed_verdict = lax.psum(verdict.astype(jnp.bfloat16), "member").astype(jnp.float32)
    return (updated[None], summed_verdict / lax.axis_size("member"))


def solution(mesh):
    return jax.shard_map(
        body,
        mesh=mesh,
        in_specs=(
            P("member", "seq", None),
            P(),
            P("member", None),
            P("member", "seq", None),
            P("member", "seq", None),
            P("member", "seq", None),
            P("member", "seq", None),
            P("member", None),
            P("member", None),
            P("member", None, None),
        ),
        out_specs=(P("member", "seq", None), P("seq", None)),
        check_vma=False,
    )
```

profile of v0, /device:TPU:0, one launch (start us, length us, event | category | flops | bytes accessed | tf_op | source)
XLA Modules:
  0.0 372.0 jit_solution(8620353155111887067)
XLA Ops:
  7.2 1.9 copy.22
  9.2 1.7 copy.23
  11.0 3.4 copy.24
  15.6 0.6 fusion.29
  16.2 1.3 copy-done.2
  17.6 0.9 slice.20
  18.5 3.2 collective-permute-start
  21.7 0.6 reduce.1
  22.4 0.6 reduce.2
  23.0 0.8 dynamic_slice.19
  23.8 0.8 broadcast_select_fusion
  25.2 33.5 %all-gather.9.cloned.1.call-done = bf16[1,2880,256]{2,0,1:T(2,128)(2,1)} async-done(((bf16[1,180,256]{2,0,1:T(2,128)(2,1)}), bf16[1,2880,256]{2,0,1:T(2,128)(2,1)}) %all-gather.9.cloned.1.call-update) | async-done | bytes 1474576 | tf_op jit(solution)/shard_map/all_gather | solution.py:105
  58.7 3.8 %fusion.49 = bf16[512,256]{1,0:T(8,128)(2,1)S(1)} fusion(bf16[1,2880,256]{2,0,1:T(2,128)(2,1)} %all-gather.9.cloned.1.call-done, bf16[384,2880]{0,1:T(8,128)(2,1)} %copy-done.2, bf16[128,2880]{0,1:T(8,128)(2,1)} %collective-permute-done), kind=kOutput, calls=%fused_computation.60 | convolution fusion | flops 761004032 | bytes 4685824 | tf_op jit(solution)/shard_map/dot_general | solution.py:103
  62.4 0.8 copy.26
  63.3 40.8 %all-gather.11.cloned.1.call-done = bf16[1,2880,256]{2,0,1:T(2,128)(2,1)} async-done(((bf16[1,180,256]{2,0,1:T(2,128)(2,1)}), bf16[1,2880,256]{2,0,1:T(2,128)(2,1)}) %all-gather.11.cloned.1.call-update) | async-done | bytes 1474576 | tf_op jit(solution)/shard_map/all_gather | solution.py:100
  104.0 3.8 %fusion.43 = f32[512,256]{0,1:T(8,128)S(1)} fusion(bf16[384,2880]{0,1:T(8,128)(2,1)} %copy-done.2, bf16[128,2880]{0,1:T(8,128)(2,1)} %collective-permute-done, bf16[1,2880,256]{2,0,1:T(2,128)(2,1)} %all-gather.11.cloned.1.call-done), kind=kOutput, calls=%fused_computation.52 | convolution fusion | flops 760872960 | bytes 4947968 | tf_op jit(solution)/shard_map/dot_general | solution.py:98
  107.9 0.7 pad_maximum_fusion.5
  108.6 116.6 %all-gather.13.cloned.1.call-done = bf16[1,2880,2048]{2,0,1:T(2,128)(2,1)} async-done(((bf16[1,180,2048]{2,0,1:T(2,128)(2,1)}), bf16[1,2880,2048]{2,0,1:T(2,128)(2,1)}) %all-gather.13.cloned.1.call-update) | async-done | bytes 11796496 | tf_op jit(solution)/shard_map/all_gather | solution.py:95
  225.2 50.9 %copy.31 = bf16[1,2880,2048]{1,2,0:T(8,128)(2,1)} copy(bf16[1,2880,2048]{2,0,1:T(2,128)(2,1)} %all-gather.13.cloned.1.call-done) | data formatting | bytes 23592960 | tf_op jit(solution)/shard_map/dot_general | solution.py:93
  276.0 9.7 %fusion.35 = f32[384,32,64]{0,2,1:T(8,128)S(1)} fusion(bf16[32,64,2880]{2,1,0:T(8,128)(2,1)} %bitcast.94, bf16[1,384,2880]{1,2,0:T(8,128)(2,1)S(1)} %copy-done.1, f32[2880]{0:T(1024)S(1)} %reduce, f32[384]{0:T(512)S(1)} %add_rsqrt_fusion.2), kind=kOutput, calls=%fused_computation.46 | convolution fusion | flops 4534272000 | bytes 17167104 | tf_op jit(solution)/shard_map/dot_general | solution.py:93
  286.2 1.5 fusion.33
  287.7 40.2 %while.18 = (s32[]{:T(128)}, bf16[4,384,512]{1,2,0:T(8,128)(2,1)}, s32[4]{0:T(128)S(1)}, bf16[512,256]{0,1:T(8,128)(2,1)}, bf16[512,256]{0,1:T(8,128)(2,1)}, /*i...) while((s32[]{:T(128)}, bf16[4,384,512]{1,2,0:T(8,128)(2,1)}, ...), condition=%wide.region_3.4_spmd.clone, body=%wide.region_1.3_spmd.clone.sunk | while | flops 418182144 | bytes 15693069 | solution.py:78
  288.0 0.6 dynamic_slice.44
  289.3 1.0 constant_dynamic-slice_fusion.2
  291.0 3.0 fusion.70
  294.0 3.0 fusion.71
  297.0 0.8 constant_dynamic-update-slice_fusion.2
  298.1 0.6 dynamic_slice.44
  299.3 1.0 constant_dynamic-slice_fusion.2
  301.0 3.0 fusion.70
  304.0 3.0 fusion.71
  307.0 0.8 constant_dynamic-update-slice_fusion.2
  308.1 0.6 dynamic_slice.44
  309.4 1.0 constant_dynamic-slice_fusion.2
  311.1 3.0 fusion.70
  314.1 3.0 fusion.71
  317.1 0.8 constant_dynamic-update-slice_fusion.2
  318.2 0.6 dynamic_slice.44
  319.4 1.0 constant_dynamic-slice_fusion.2
  321.1 3.0 fusion.70
  324.1 3.0 fusion.71
  327.1 0.8 constant_dynamic-update-slice_fusion.2
  327.9 9.7 %multiply_reduce_fusion = (f32[384]{0:T(512)S(1)}, f32[384,2880]{0,1:T(8,128)S(1)}) fusion(bf16[384,2048]{0,1:T(8,128)(2,1)} %bitcast.101, bf16[1,2048,2880]{1,2,0:T(8,128)(2,1)} %all-gather.15.cloned.1.call-done), kind=kOutput, calls=%fused_computation.41 | convolution fusion | flops 4532059648 | bytes 17794560 | tf_op jit(solution)/shard_map/dot_general | solution.py:133
  337.6 1.5 fusion.24
  339.1 1.3 copy-done.3
  340.5 2.1 fusion.52
  342.6 21.3 %all-reduce.2.cloned.1.call-done = bf16[384,128]{1,0:T(8,128)(2,1)} async-done(((bf16[384,128]{1,0:T(8,128)(2,1)}), bf16[384,128]{1,0:T(8,128)(2,1)}) %all-reduce.2.cloned.1.call-update) | async-done | bytes 98320 | tf_op jit(solution)/shard_map/psum | solution.py:143
  363.8 1.6 convert_multiply_fusion.3
  (48 shorter events, 3.7 us)
Async XLA Ops:
  7.2 333.3 %copy-start = (bf16[1,2880,128]{2,1,0:T(8,128)(2,1)S(1)}, bf16[1,2880,128]{2,1,0:T(8,128)(2,1)}, u32[]{:S(2)}) copy-start(bf16[1,2880,128]{2,1,0:T(8,128)(2,1)} %param.21) | copy-start | bytes 2211844
  7.2 7.8 %copy-start.6 = (f32[1,2880]{1,0:T(1,128)S(1)}, f32[1,2880]{1,0:T(1,128)}, u32[]{:S(2)}) copy-start(f32[1,2880]{1,0:T(1,128)} %param.14) | copy-start | bytes 34564
  7.2 7.9 %copy-start.1 = (bf16[1,384,2880]{1,2,0:T(8,128)(2,1)S(1)}, bf16[1,384,2880]{1,2,0:T(8,128)(2,1)}, u32[]{:S(2)}) copy-start(bf16[1,384,2880]{1,2,0:T(8,128)(2,1)} %param.12) | copy-start | bytes 6635524
  7.2 51.5 %all-gather.9.cloned.1.call-start = ((), (), s32[]{:S(2)}) async-start(), calls=%async_computation.1 | async-start | bytes 3133440 | tf_op jit(solution)/shard_map/all_gather | solution.py:105
  9.1 94.9 %all-gather.11.cloned.1.call-start = ((), (), s32[]{:S(2)}) async-start(), calls=%async_computation.2 | async-start | bytes 3133440 | tf_op jit(solution)/shard_map/all_gather | solution.py:100
  10.9 214.3 %all-gather.13.cloned.1.call-start = ((), (), s32[]{:S(2)}) async-start(), calls=%async_computation.3 | async-start | bytes 25067520 | tf_op jit(solution)/shard_map/all_gather | solution.py:95
  14.4 313.5 %all-gather.15.cloned.1.call-start = ((), (), s32[]{:S(2)}) async-start(), calls=%async_computation.4 | async-start | bytes 12533760 | tf_op jit(solution)/shard_map/all_gather | solution.py:135
  15.0 348.9 %all-reduce.2.cloned.1.call-start = ((), (), s32[]{:S(2)}) async-start(), calls=%async_computation | async-start | bytes 196608 | tf_op jit(solution)/shard_map/psum | solution.py:143
  15.6 6.1 %copy-start.7 = (f32[1,2880]{1,0:T(1,128)S(1)}, f32[1,2880]{1,0:T(1,128)}, u32[]{:S(2)}) copy-start(f32[1,2880]{1,0:T(1,128)} %param.19) | copy-start | bytes 34564
  15.6 6.8 %copy-start.8 = (f32[1,2880]{1,0:T(1,128)S(1)}, f32[1,2880]{1,0:T(1,128)}, u32[]{:S(2)}) copy-start(f32[1,2880]{1,0:T(1,128)} %param.20) | copy-start | bytes 34564
  16.2 1.4 copy-start.2
  18.5 6.7 %collective-permute-start = (bf16[128,2880]{0,1:T(8,128)(2,1)}, bf16[128,2880]{0,1:T(8,128)(2,1)}, u32[]{:S(2)}, u32[]{:S(2)}) collective-permute-start(bf16[128,2880]{0,1:T(8,128)(2,1)} %slice.20), channel_id=1, source_target_pairs={{0,1},{1,2},{2,3},{3,4},{4,5},{5,6},{6,7},{7,8},{8,9},{9,10},{10,1... | collective-permute-start | bytes 2211848 | tf_op jit(solution)/shard_map/ppermute | solution.py:22
  327.9 9.7 %copy-start.4 = (f32[2880]{0:T(1024)S(1)}, f32[2880]{0:T(1024)}, u32[]{:S(2)}) copy-start(f32[2880]{0:T(1024)} %reduce.1) | copy-start | bytes 34564
  337.6 2.9 copy-start.5
  339.1 1.4 copy-start.3
Sparse Core Ops, SparseCore 0:
  10.8 47.8 all-gather.8
  60.8 43.1 all-gather.10
  105.6 119.5 all-gather.12
  227.2 98.9 all-gather.14
  342.7 21.0 all-reduce.1
where the time goes:
time: 374 us; the launch traced here: 372 us
  waiting for transfers between devices  213 us (57%)
  local copies, waits for them, and re-layouts  72.8 us (19%)
  matrix products  53 us (14%)
  between operations  14 us (4%)
  other arithmetic  10.8 us (3%)
  loops' own time  5.3 us (1%)
    all_gather x1, waiting for transfers between devices, body(): lax.all_gather(w_query[0], 'seq', axis=0, tiled=True)  117 us
    dot_general x1, local copies, waits for them, and re-layouts, body(): jnp.dot(normed, lax.all_gather(w_query[0], 'seq', axis=0, tiled=True), pr...  50.9 us
    all_gather x1, waiting for transfers between devices, body(): lax.all_gather(w_key[0], 'seq', axis=0, tiled=True)  40.8 us
    all_gather x1, waiting for transfers between devices, body(): lax.all_gather(w_value[0], 'seq', axis=0, tiled=True)  33.5 us
    psum x1, waiting for transfers between devices, body(): lax.psum(verdict.astype(jnp.bfloat16), 'member').astype(jnp.float32)  21.3 us
    dot_general x4, matrix products, one_head(): jnp.einsum('qgd,kd->gqk', query_head, key_head, preferred_element_type=jn...  12 us
    dot_general x4, matrix products, one_head(): jnp.einsum('gqk,kd->qgd', weights, value_head, preferred_element_type=jnp...  11.9 us
    unnamed x22, local copies, waits for them, and re-layouts  10.5 us
  transfers between devices with their start and end apart: 6, of which 4 were waited for; matrix products, arithmetic and copies ran while one was open for 31% of the time, Pallas kernels for 0%

commit v1 on v0

v1 whole, which is shorter than its diff:
```python
import functools
import math

import jax
import jax.numpy as jnp
from jax import lax
from jax.experimental import pallas as pl
from jax.experimental.pallas import tpu as pltpu
from jax.sharding import PartitionSpec as P

QH = 32
KVH = 4
HD = 64
WINDOW = 128
CORES = 2
GROUP = 4
LANES = 128
ROWS = 128

epsilon = 1e-06
softcap = 50.0
rope_base = 10000.0
VMEM_LIMIT = 48 * 1024 * 1024


def pieces(total, step):
    return [(at, min(step, total - at)) for at in range(0, total, step)]


def accumulate(x_refs, w_refs, prior, at, size):
    total = prior
    for x_ref, w_ref in zip(x_refs, w_refs):
        x = x_ref[0] if len(x_ref.shape) == 3 else x_ref[...]
        part = jnp.dot(x, w_ref[:, at : at + size], preferred_element_type=jnp.float32)
        total = part if total is None else total + part
    return total


def rotated(block, cosine, sine):
    lane = lax.broadcasted_iota(jnp.int32, block.shape, 1)
    half = HD // 2
    other = jnp.where(
        lane % HD < half, pltpu.roll(block, LANES - half, 1), pltpu.roll(block, half, 1)
    )
    return block * cosine + other * sine


def qkv_kernel(first, last, _, *refs):
    x_refs, w_refs, refs = refs[:GROUP], refs[GROUP : 2 * GROUP], refs[2 * GROUP :]
    acc_ref = None
    if not first:
        acc_ref, refs = refs[0], refs[1:]
    if last:
        cos_ref, sin_ref, q_ref, kv_ref = refs
        q_wide, k_wide = QH * HD, KVH * HD
        cosine, sine = cos_ref[...], sin_ref[...]
    else:
        (out_ref,) = refs
    for at, size in pieces(w_refs[0].shape[1], 4 * LANES):
        prior = None if first else acc_ref[:, at : at + size]
        total = accumulate(x_refs, w_refs, prior, at, size)
        if not last:
            out_ref[:, at : at + size] = total
            continue
        for low in range(0, size, LANES):
            block = total[:, low : low + LANES]
            column = at + low
            if column < q_wide:
                block = rotated(block, cosine, sine) * (1.0 / math.sqrt(HD))
                q_ref[:, column : column + LANES] = block.astype(jnp.bfloat16)
                continue
            column = column - q_wide
            if column < k_wide:
                block = rotated(block, cosine, sine)
            kv_ref[:, column : column + LANES] = block.astype(jnp.bfloat16)


def qkv_group(indices, chunks, units, acc, tables):
    _, rows, depth = chunks.shape
    wide = units[0].shape[1]
    first, last = acc is None, tables is not None
    x_specs = [
        pl.BlockSpec((1, ROWS, depth), lambda m, ids, k=k: (ids[k], m, 0))
        for k in range(GROUP)
    ]
    w_specs = [pl.BlockSpec((depth, wide), lambda m, ids: (0, 0)) for _ in units]
    rows_spec = lambda width: pl.BlockSpec((ROWS, width), lambda m, ids: (m, 0))
    operands, specs, aliases = [chunks] * GROUP + list(units), x_specs + w_specs, {}
    if not first:
        operands.append(acc)
        specs.append(rows_spec(wide))
    if last:
        operands += list(tables)
        specs += [rows_spec(LANES)] * 2
        kv_wide = 2 * KVH * HD
        out_shape = (
            jax.ShapeDtypeStruct((rows, wide - kv_wide), jnp.bfloat16),
            jax.ShapeDtypeStruct((rows, kv_wide), jnp.bfloat16),
        )
        out_specs = (rows_spec(wide - kv_wide), rows_spec(kv_wide))
    else:
        out_shape = jax.ShapeDtypeStruct((rows, wide), jnp.float32)
        out_specs = rows_spec(wide)
        if not first:
            aliases = {1 + 2 * GROUP: 0}
    return pl.pallas_call(
        functools.partial(qkv_kernel, first, last),
        grid_spec=pltpu.PrefetchScalarGridSpec(
            num_scalar_prefetch=1, grid=(rows // ROWS,), in_specs=specs, out_specs=out_specs
        ),
        out_shape=out_shape,
        input_output_aliases=aliases,
        compiler_params=pltpu.CompilerParams(vmem_limit_bytes=VMEM_LIMIT),
        cost_estimate=pl.CostEstimate(
            flops=2 * rows * depth * wide * GROUP,
            bytes_accessed=2 * GROUP * depth * wide + 8 * rows * wide,
            transcendentals=0,
        ),
    )(indices, *operands)


def attend_kernel(q_ref, before_ref, own_ref, seg_q_ref, seg_before_ref, seg_own_ref, out_ref):
    rows = q_ref.shape[0]
    count = 2 * rows
    distance = (
        lax.broadcasted_iota(jnp.int32, (rows, count), 0)
        + rows
        - lax.broadcasted_iota(jnp.int32, (rows, count), 1)
    )
    seg_keys = jnp.concatenate([seg_before_ref[...], seg_own_ref[...]], axis=1)
    allowed = (distance >= 0) & (distance < WINDOW) & (seg_q_ref[...] == seg_keys)
    keys = jnp.concatenate([before_ref[...], own_ref[...]], axis=0)
    span = QH // KVH
    for g in range(KVH):
        key = keys[:, g * HD : (g + 1) * HD]
        value = keys[:, (KVH + g) * HD : (KVH + g + 1) * HD]
        for pair in range(span // 2):
            outs = []
            for side in range(2):
                h = g * span + 2 * pair + side
                query = q_ref[:, h * HD : (h + 1) * HD]
                scores = lax.dot_general(
                    query, key, (((1,), (1,)), ((), ())), preferred_element_type=jnp.float32
                )
                expanded = jnp.exp(softcap * jnp.tanh(scores * (1.0 / softcap)))
                expanded = jnp.where(allowed, expanded, 0.0)
                total = jnp.sum(expanded, axis=1, keepdims=True)
                mixed = jnp.dot(
                    expanded.astype(jnp.bfloat16), value, preferred_element_type=jnp.float32
                )
                outs.append(mixed / total)
            at = (g * span + 2 * pair) * HD
            out_ref[:, at : at + 2 * HD] = jnp.concatenate(outs, axis=1).astype(jnp.bfloat16)


def attend(queries, keys_values, seg_q, seg_keys):
    rows, wide = queries.shape
    kv_wide = keys_values.shape[1]
    return pl.pallas_call(
        attend_kernel,
        grid=(rows // ROWS,),
        in_specs=[
            pl.BlockSpec((ROWS, wide), lambda m: (m, 0)),
            pl.BlockSpec((ROWS, kv_wide), lambda m: (m, 0)),
            pl.BlockSpec((ROWS, kv_wide), lambda m: (m + 1, 0)),
            pl.BlockSpec((ROWS, 1), lambda m: (m, 0)),
            pl.BlockSpec((1, ROWS), lambda m: (0, m)),
            pl.BlockSpec((1, ROWS), lambda m: (0, m + 1)),
        ],
        out_specs=pl.BlockSpec((ROWS, wide), lambda m: (m, 0)),
        out_shape=jax.ShapeDtypeStruct((rows, wide), jnp.bfloat16),
        compiler_params=pltpu.CompilerParams(vmem_limit_bytes=VMEM_LIMIT),
        cost_estimate=pl.CostEstimate(
            flops=8 * rows * ROWS * wide,
            bytes_accessed=4 * rows * wide,
            transcendentals=4 * rows * ROWS * QH,
        ),
    )(queries, keys_values, keys_values, seg_q, seg_keys, seg_keys)


def out_kernel(first, last, _, *refs):
    x_refs, w_refs, refs = refs[:GROUP], refs[GROUP : 2 * GROUP], refs[2 * GROUP :]
    acc_ref = None
    if not first:
        acc_ref, refs = refs[0], refs[1:]
    if last:
        hidden_ref, post_ref, final_ref, judge_ref, updated_ref, verdict_ref, total_ref = refs
    else:
        (total_ref,) = refs
    width = w_refs[0].shape[1]
    square = None
    for at, size in pieces(width, 4 * LANES):
        prior = None if first else acc_ref[:, at : at + size]
        total = accumulate(x_refs, w_refs, prior, at, size)
        total_ref[:, at : at + size] = total
        if last:
            part = jnp.sum(total * total, axis=1, keepdims=True)
            square = part if square is None else square + part
    if not last:
        return
    scale = lax.rsqrt(square * (1.0 / width) + epsilon)
    square = None
    for at, size in pieces(width, 4 * LANES):
        cols = slice(at, at + size)
        updated = hidden_ref[:, cols].astype(jnp.float32) + (
            total_ref[:, cols] * scale * post_ref[:, cols]
        )
        updated = updated.astype(jnp.bfloat16)
        updated_ref[:, cols] = updated
        updated = updated.astype(jnp.float32)
        part = jnp.sum(updated * updated, axis=1, keepdims=True)
        square = part if square is None else square + part
    scale = lax.rsqrt(square * (1.0 / width) + epsilon)
    verdict = None
    for at, size in pieces(width, 4 * LANES):
        cols = slice(at, at + size)
        closing = updated_ref[:, cols].astype(jnp.float32) * scale * final_ref[:, cols]
        part = jnp.dot(
            closing.astype(jnp.bfloat16), judge_ref[cols, :], preferred_element_type=jnp.float32
        )
        verdict = part if verdict is None else verdict + part
    verdict_ref[...] = verdict.astype(jnp.bfloat16)


def out_group(indices, attended, units, acc, closing):
    rows = attended.shape[0]
    depth, wide = units[0].shape
    first, last = acc is None, closing is not None
    if depth % LANES:
        attended = attended.reshape(rows, -1, depth).transpose(1, 0, 2)
        x_specs = [
            pl.BlockSpec((1, ROWS, depth), lambda m, ids, k=k: (ids[k], m, 0))
            for k in range(GROUP)
        ]
    else:
        x_specs = [
            pl.BlockSpec((ROWS, depth), lambda m, ids, k=k: (m, ids[k])) for k in range(GROUP)
        ]
    w_specs = [pl.BlockSpec((depth, wide), lambda m, ids: (0, 0)) for _ in units]
    rows_spec = lambda width: pl.BlockSpec((ROWS, width), lambda m, ids: (m, 0))
    operands, specs = [attended] * GROUP + list(units), x_specs + w_specs
    aliases, scratch = {}, []
    if not first:
        operands.append(acc)
        specs.append(rows_spec(wide))
    if last:
        hidden, post_gain, final_gain, judge = closing
        operands += [hidden, post_gain, final_gain, judge]
        whole = lambda array: pl.BlockSpec(array.shape, lambda m, ids: (0, 0))
        specs += [rows_spec(wide), whole(post_gain), whole(final_gain), whole(judge)]
        out_shape = (
            jax.ShapeDtypeStruct((rows, wide), jnp.bfloat16),
            jax.ShapeDtypeStruct((rows, judge.shape[1]), jnp.bfloat16),
        )
        out_specs = (rows_spec(wide), rows_spec(judge.shape[1]))
        scratch = [pltpu.VMEM((ROWS, wide), jnp.float32)]
    else:
        out_shape = jax.ShapeDtypeStruct((rows, wide), jnp.float32)
        out_specs = rows_spec(wide)
        if not first:
            aliases = {1 + 2 * GROUP: 0}
    return pl.pallas_call(
        functools.partial(out_kernel, first, last),
        grid_spec=pltpu.PrefetchScalarGridSpec(
            num_scalar_prefetch=1,
            grid=(rows // ROWS,),
            in_specs=specs,
            out_specs=out_specs,
            scratch_shapes=scratch,
        ),
        out_shape=out_shape,
        input_output_aliases=aliases,
        compiler_params=pltpu.CompilerParams(vmem_limit_bytes=VMEM_LIMIT),
        cost_estimate=pl.CostEstimate(
            flops=2 * rows * depth * wide * GROUP,
            bytes_accessed=2 * GROUP * depth * wide + 8 * rows * wide,
            transcendentals=0,
        ),
    )(indices, *operands)


def move(block, route):
    return lax.ppermute(block, "seq", route)


class Plane:
    def __init__(self):
        self.index = lax.axis_index("seq")
        self.z = self.index // (2 * CORES)
        ends = lambda z: z in (0, 3)
        middle = lambda z: z in (1, 2)
        self.core = self.route(lambda z, x, c: (z, x, 1 - c))
        self.x_all = self.route(lambda z, x, c: (z, 1 - x, c))
        self.x_end = self.route(lambda z, x, c: (z, 1 - x, c) if ends(z) else None)
        self.x_mid = self.route(lambda z, x, c: (z, 1 - x, c) if middle(z) else None)
        self.z_pair = self.route(lambda z, x, c: (z ^ 1, x, c))
        self.z_mid = self.route(lambda z, x, c: (3 - z, x, c) if middle(z) else None)
        self.z_out = self.route(lambda z, x, c: (z ^ 1, x, c) if middle(z) else None)

    @staticmethod
    def route(target):
        route = []
        for i in range(4 * 2 * CORES):
            to = target(i // (2 * CORES), i // CORES % 2, i % CORES)
            if to is not None:
                route.append((i, (to[0] * 2 + to[1]) * CORES + to[2]))
        return route

    def gather(self, own, by_z):
        side = move(own, self.x_all)
        near = move(own, self.z_pair)
        inner = move(own, self.z_mid)
        far = move(near, self.z_mid)
        side_inner = move(side, self.z_mid)
        from_inner = move(inner, self.z_out)
        from_far = move(far, self.z_out)
        third = inner + from_inner
        fourth = far + from_far
        if by_z:
            side_near = move(near, self.x_mid) + move(side, self.z_out)
        else:
            side_near = move(near, self.x_all)
        side_third = side_inner + move(from_inner, self.x_end)
        side_fourth = move(fourth, self.x_all)
        found = [[own, side], [near, side_near], [third, side_third], [fourth, side_fourth]]
        return [pair + [move(unit, self.core) for unit in pair] for pair in found]

    def sources(self):
        i = self.index
        at_end = (self.z == 0) | (self.z == 3)
        step = 2 * CORES
        flips = [0, step, jnp.where(at_end, 2 * step, 3 * step), jnp.where(at_end, 3 * step, 2 * step)]
        return [
            jnp.stack([i ^ f, i ^ f ^ CORES, i ^ f ^ 1, i ^ f ^ CORES ^ 1]).astype(jnp.int32)
            for f in flips
        ]


def gather_whole(own):
    count = lax.axis_size("seq")
    whole = lax.all_gather(own, "seq", axis=0)
    return [[whole[i + k] for k in range(GROUP)] for i in range(0, count, GROUP)]


def body(
    structured,
    hidden, segments, pre_gain, w_query, w_key, w_value, w_output, post_gain, final_gain, w_judge,
):
    own_rows = hidden[0]
    tok_rows, width = own_rows.shape
    shards = lax.axis_size("seq")
    dev_index = lax.axis_index("seq")
    row_first = dev_index * tok_rows

    unit_in = jnp.concatenate([w_query[0], w_key[0], w_value[0]], axis=1)
    unit_out = w_output[0]
    if structured:
        plane = Plane()
        groups_in = plane.gather(unit_in, True)
        groups_out = plane.gather(unit_out, False)
        sources = plane.sources()
    else:
        groups_in, groups_out = gather_whole(unit_in), gather_whole(unit_out)
        sources = [jnp.arange(i, i + GROUP, dtype=jnp.int32) for i in range(0, shards, GROUP)]

    values = own_rows.astype(jnp.float32)
    normed = values * lax.rsqrt(jnp.mean(values * values, axis=-1, keepdims=True) + epsilon)
    normed = (normed * pre_gain[0]).astype(jnp.bfloat16)
    chunks = normed.reshape(tok_rows, shards, width // shards).transpose(1, 0, 2)

    half = HD // 2
    lane = jnp.arange(LANES, dtype=jnp.int32)
    frequency = jnp.exp((lane % half).astype(jnp.float32) * (-2.0 * math.log(rope_base) / HD))
    positions = row_first + jnp.arange(tok_rows, dtype=jnp.int32)
    angles = positions.astype(jnp.float32)[:, None] * frequency[None, :]
    tables = (jnp.cos(angles), jnp.where(lane % HD < half, -1.0, 1.0) * jnp.sin(angles))

    acc = None
    for k, (ids, units) in enumerate(zip(sources, groups_in)):
        end = k == len(sources) - 1
        acc = qkv_group(ids, chunks, units, acc, tables if end else None)
    queries, keys_values = acc

    line = [(i, i + 1) for i in range(shards - 1)]
    before = lax.ppermute(keys_values[tok_rows - WINDOW :], "seq", line)
    keys_values = jnp.concatenate([before, keys_values], axis=0)
    seg_own = lax.dynamic_slice_in_dim(segments, row_first, tok_rows, 0)
    seg_prior = lax.dynamic_slice_in_dim(segments, jnp.maximum(row_first - WINDOW, 0), WINDOW, 0)
    seg_prior = jnp.where(dev_index > 0, seg_prior, -1)
    seg_keys = jnp.concatenate([seg_prior, seg_own])[None, :]
    attended = attend(queries, keys_values, seg_own[:, None], seg_keys)

    closing = (own_rows, post_gain, final_gain, w_judge[0])
    acc = None
    for k, (ids, units) in enumerate(zip(sources, groups_out)):
        end = k == len(sources) - 1
        acc = out_group(ids, attended, units, acc, closing if end else None)
    updated, verdict = acc

    members = lax.axis_size("member")
    summed = verdict.astype(jnp.float32)
    for step in range(1, members):
        ring = [(i, (i + step) % members) for i in range(members)]
        summed = summed + lax.ppermute(verdict, "member", ring).astype(jnp.float32)
    return updated[None], summed / members


def solution(mesh):
    across = mesh.shape["member"]
    structured = across == 2 and mesh.shape["seq"] == 4 * across * CORES
    return jax.shard_map(
        functools.partial(body, structured),
        mesh=mesh,
        in_specs=(
            P("member", "seq", None),
            P(),
            P("member", None),
            P("member", "seq", None),
            P("member", "seq", None),
            P("member", "seq", None),
            P("member", "seq", None),
            P("member", None),
            P("member", None),
            P("member", None, None),
        ),
        out_specs=(P("member", "seq", None), P("seq", None)),
        check_vma=False,
    )
```

time: 374 us -> 306 us (0.82)
  waiting for transfers between devices: 213 us -> 117 us
  Pallas kernels: 0 us -> 63.3 us
  matrix products: 53 us -> 0 us
  starting transfers between devices: 3.43 us -> 36.7 us
  other arithmetic: 10.8 us -> 26.8 us
  local copies, waits for them, and re-layouts: 72.8 us -> 58.6 us
  between operations: 14 us -> 1.35 us
  loops' own time: 5.3 us -> 0 us
    all_gather x4 -> x0, waiting for transfers between devices: 191 us -> none  [the longest x1 117 us: body(): lax.all_gather(w_query[0], 'seq', axis=0, tiled=True)]
    ppermute x1 -> x39, waiting for transfers between devices: 0.01 us -> 117 us  [the longest x37 117 us: move(): return lax.ppermute(block, 'seq', route)]
    pallas_call x0 -> x9, Pallas kernels: none -> 63.3 us  [the longest x4 27.9 us: qkv_group(): pl.pallas_call(functools.partial(qkv_kernel, first, last), grid_spec=pltp...]
    dot_general x13 -> x0, matrix products: 53 us -> none  [the longest x4 12 us: one_head(): jnp.einsum('qgd,kd->gqk', query_head, key_head, preferred_element_type=jn...]
    dot_general x1 -> x0, local copies, waits for them, and re-layouts: 50.9 us -> none  [body(): jnp.dot(normed, lax.all_gather(w_query[0], 'seq', axis=0, tiled=True), pr...]
    ppermute x1 -> x39, starting transfers between devices: 3.23 us -> 36.7 us  [the longest x37 32.2 us: move(): return lax.ppermute(block, 'seq', route)]
    ppermute x0 -> x12, local copies, waits for them, and re-layouts: none -> 22.8 us  [move(): return lax.ppermute(block, 'seq', route)]
    psum x1 -> x0, waiting for transfers between devices: 21.3 us -> none  [body(): lax.psum(verdict.astype(jnp.bfloat16), 'member').astype(jnp.float32)]
  transfers between devices with their start and end apart: 6 -> 39, of which waited for: 4 -> 8; matrix products, arithmetic and copies ran while one was open for 31% -> 26% of each run, Pallas kernels for 0% -> 9%
where the time goes in v1:
time: 306 us; the launch traced here: 304 us
  waiting for transfers between devices  117 us (38%)
  Pallas kernels  63.3 us (21%)
  local copies, waits for them, and re-layouts  58.6 us (19%)
  starting transfers between devices  36.7 us (12%)
  other arithmetic  26.8 us (9%)
    ppermute x37, waiting for transfers between devices, move(): return lax.ppermute(block, 'seq', route)  117 us
    ppermute x37, starting transfers between devices, move(): return lax.ppermute(block, 'seq', route)  32.2 us
    pallas_call x4, Pallas kernels, qkv_group(): pl.pallas_call(functools.partial(qkv_kernel, first, last), grid_spec=pltp...  27.9 us
    pallas_call x4, Pallas kernels, out_group(): pl.pallas_call(functools.partial(out_kernel, first, last), grid_spec=pltp...  27.6 us
    ppermute x12, local copies, waits for them, and re-layouts, move(): return lax.ppermute(block, 'seq', route)  22.8 us
    unnamed x87, local copies, waits for them, and re-layouts  16.9 us
    convert_element_type x2, local copies, waits for them, and re-layouts, body(): values = own_rows.astype(jnp.float32)  10.6 us
    pallas_call x1, Pallas kernels, attend(): pl.pallas_call(attend_kernel, grid=(rows // ROWS,), in_specs=[pl.BlockSpe...  7.8 us
  transfers between devices with their start and end apart: 39, of which 8 were waited for; matrix products, arithmetic and copies ran while one was open for 26% of the time, Pallas kernels for 9%

profile of v1, /device:TPU:0, one launch (start us, length us, event | category | flops | bytes accessed | tf_op | source)
XLA Modules:
  0.0 303.8 jit_solution(6712564754093561745)
XLA Ops:
  0.6 3.0 collective-permute-start.28
  3.6 1.6 collective-permute-start.20
  7.1 14.1 %collective-permute-done.28 = bf16[128,2880]{0,1:T(8,128)(2,1)S(1)} collective-permute-done((bf16[128,2880]{0,1:T(8,128)(2,1)}, bf16[128,2880]{0,1:T(8,128)(2,1)S(1)}, u32[]{:S(2)}, u32[]{:S(2)}) %collective-permute-start.28) | collective-permute-done | bytes 737312 | tf_op jit(solution)/shard_map/ppermute | solution.py:283
  21.2 2.1 collective-permute-start
  25.7 14.9 %collective-permute-done.8.refs_5_ = bf16[180,2560]{1,0:T(8,128)(2,1)} collective-permute-done((bf16[180,2560]{1,0:T(8,128)(2,1)S(1)}, bf16[180,2560]{1,0:T(8,128)(2,1)}, u32[]{:S(2)}, u32[]{:S(2)}) %collective-permute-start.8) | collective-permute-done | bytes 921632 | tf_op jit(solution)/shard_map/ppermute | solution.py:283
  40.6 1.7 collective-permute-start.33
  46.1 12.2 %collective-permute-done.33 = bf16[128,2880]{0,1:T(8,128)(2,1)S(1)} collective-permute-done((bf16[128,2880]{0,1:T(8,128)(2,1)S(1)}, bf16[128,2880]{0,1:T(8,128)(2,1)S(1)}, u32[]{:S(2)}, u32[]{:S(2)}) %collective-permute-start.33) | collective-permute-done | bytes 737312 | tf_op jit(solution)/shard_map/ppermute | solution.py:283
  60.3 6.7 %collective-permute-done.27 = bf16[128,2880]{0,1:T(8,128)(2,1)} collective-permute-done((bf16[128,2880]{0,1:T(8,128)(2,1)S(1)}, bf16[128,2880]{0,1:T(8,128)(2,1)}, u32[]{:S(2)}, u32[]{:S(2)}) %collective-permute-start.27) | collective-permute-done | bytes 737312 | tf_op jit(solution)/shard_map/ppermute | solution.py:283
  67.0 1.5 collective-permute-start.21
  71.8 21.4 %collective-permute-done.7 = bf16[180,2560]{1,0:T(8,128)(2,1)} collective-permute-done((bf16[180,2560]{1,0:T(8,128)(2,1)S(1)}, bf16[180,2560]{1,0:T(8,128)(2,1)}, u32[]{:S(2)}, u32[]{:S(2)}) %collective-permute-start.7) | collective-permute-done | bytes 921632 | tf_op jit(solution)/shard_map/ppermute | solution.py:283
  93.2 1.6 collective-permute-start.9
  94.8 18.4 %collective-permute-done.2 = bf16[180,2560]{1,0:T(8,128)(2,1)S(1)} collective-permute-done((bf16[180,2560]{1,0:T(8,128)(2,1)S(1)}, bf16[180,2560]{1,0:T(8,128)(2,1)S(1)}, u32[]{:S(2)}, u32[]{:S(2)}) %collective-permute-start.2) | collective-permute-done | bytes 921632 | tf_op jit(solution)/shard_map/ppermute | solution.py:283
  114.2 2.4 collective-permute-start.10
  118.2 10.6 %collective-permute-done.14 = bf16[180,2560]{1,0:T(8,128)(2,1)} collective-permute-done((bf16[180,2560]{1,0:T(8,128)(2,1)}, bf16[180,2560]{1,0:T(8,128)(2,1)}, u32[]{:S(2)}, u32[]{:S(2)}) %collective-permute-start.14) | collective-permute-done | bytes 921632 | tf_op jit(solution)/shard_map/ppermute | solution.py:283
  129.4 1.7 add.74.refs_5_
  131.1 3.4 %collective-permute-start.30 = (bf16[128,2880]{0,1:T(8,128)(2,1)}, bf16[128,2880]{0,1:T(8,128)(2,1)}, u32[]{:S(2)}, u32[]{:S(2)}) collective-permute-start(bf16[128,2880]{0,1:T(8,128)(2,1)} %collective-permute-done.27), channel_id=1, source_target_pairs={{0,2},{1,3},{2,0},{3,1},{12,14},{13,15},{14,12},{15,13},{16,18},{1... | collective-permute-start | bytes 2211848 | tf_op jit(solution)/shard_map/ppermute | solution.py:283
  136.0 4.2 %copy.55 = bf16[1,384,2880]{2,1,0:T(8,128)(2,1)} copy(bf16[1,384,2880]{1,2,0:T(8,128)(2,1)} %param.10) | data formatting | bytes 4423680 | tf_op args[0]
  140.2 2.2 multiply_reduce_fusion
  142.4 1.7 add.72.refs_4_
  144.8 2.6 add.73.refs_5_
  147.4 18.7 %collective-permute-done.30 = bf16[128,2880]{0,1:T(8,128)(2,1)} collective-permute-done((bf16[128,2880]{0,1:T(8,128)(2,1)}, bf16[128,2880]{0,1:T(8,128)(2,1)}, u32[]{:S(2)}, u32[]{:S(2)}) %collective-permute-start.30) | collective-permute-done | bytes 737312 | tf_op jit(solution)/shard_map/ppermute | solution.py:283
  166.7 2.4 add.80
  169.7 4.4 %reshape.54 = f32[384,16,180]{0,2,1:T(8,128)} reshape(bf16[1,384,2880]{1,2,0:T(8,128)(2,1)} %param.10) | data formatting | bytes 6635520 | tf_op jit(solution)/shard_map/convert_element_type | solution.py:366
  174.1 6.2 %copy.56 = f32[384,16,180]{2,0,1:T(8,128)} copy(f32[384,16,180]{0,2,1:T(8,128)} %reshape.54) | data formatting | bytes 8847360 | tf_op jit(solution)/shard_map/convert_element_type | solution.py:366
  180.5 5.5 %fusion.refs_0_.refs_1_.refs_2_.refs_3_ = bf16[16,384,180]{2,1,0:T(8,128)(2,1)} fusion(f32[384,16,180]{2,0,1:T(8,128)} %copy.56, f32[16,180]{1,0:T(8,128)S(1)} %mul.60, f32[384]{0:T(512)S(1)} %add_rsqrt_fusion), kind=kLoop, calls=%fused_computation.2 | loop fusion | flops 3317760 | bytes 6648576 | tf_op jit(solution)/shard_map/transpose | solution.py:369
  187.0 2.2 add.81
  189.2 2.2 add.82
  192.5 6.3 %shard_map.113.refs_8_ = f32[384,2560]{1,0:T(8,128)} custom-call(s32[4]{0:T(128)S(1)} %pad_add_fusion.4._, bf16[16,384,180]{2,1,0:T(8,128)(2,1)} %fusion.refs_0_.refs_1_.refs_2_.refs_3_, bf16[16,384,180]{2,1,0:T(8,128)(2,1)} %fusion.refs_0_.refs_1_.refs_2_.refs_3_, bf16[16,384,180]{2,1,0:T(8,128)(2,1)} %fusion.refs_0_.refs_1_.refs_2_.refs_3_, ...), custom_call_target="tpu_custom_call" | custom-call | flops 1415577600 | bytes 11550720 | tf_op jit(solution)/shard_map/pallas_call | solution.py:106
  198.7 7.5 %shard_map.114.refs_8_ = f32[384,2560]{1,0:T(8,128)} custom-call(s32[4]{0:T(128)S(1)} %pad_add_fusion.3._, bf16[16,384,180]{2,1,0:T(8,128)(2,1)} %fusion.refs_0_.refs_1_.refs_2_.refs_3_, bf16[16,384,180]{2,1,0:T(8,128)(2,1)} %fusion.refs_0_.refs_1_.refs_2_.refs_3_, ...), custom_call_target="tpu_custom_call", output_to_operand_aliasing={{}: (9, {})} | custom-call | flops 1415577600 | bytes 11550720 | tf_op jit(solution)/shard_map/pallas_call | solution.py:106
  206.2 7.8 %shard_map.115.refs_8_ = f32[384,2560]{1,0:T(8,128)} custom-call(s32[4]{0:T(128)S(1)} %pad_add_fusion.2._, bf16[16,384,180]{2,1,0:T(8,128)(2,1)} %fusion.refs_0_.refs_1_.refs_2_.refs_3_, bf16[16,384,180]{2,1,0:T(8,128)(2,1)} %fusion.refs_0_.refs_1_.refs_2_.refs_3_, ...), custom_call_target="tpu_custom_call", output_to_operand_aliasing={{}: (9, {})} | custom-call | flops 1415577600 | bytes 11550720 | tf_op jit(solution)/shard_map/pallas_call | solution.py:106
  214.0 6.4 %shard_map.116 = (bf16[384,2048]{1,0:T(8,128)(2,1)S(1)}, bf16[384,512]{1,0:T(8,128)(2,1)S(1)}) custom-call(s32[4]{0:T(128)S(1)} %pad_add_fusion.1._, bf16[16,384,180]{2,1,0:T(8,128)(2,1)} %fusion.refs_0_.refs_1_.refs_2_.refs_3_, bf16[16,384,180]{2,1,0:T(8,128)(2,1)} %fusion.refs_0_.refs_1_.refs_2_.refs_3_, ...), custom_call_target="tpu_custom_call" | custom-call | flops 1415577600 | bytes 11550720 | tf_op jit(solution)/shard_map/pallas_call | solution.py:106
  222.1 2.9 collective-permute-start.19
  225.8 2.3 copy.58
  229.7 2.3 copy.63.refs_5_
  231.9 2.3 copy.66.refs_4_
  235.4 2.3 copy.70.refs_4_
  237.7 2.4 copy.67.refs_5_
  240.0 2.3 copy.65.refs_7_
  242.3 2.3 copy.68.refs_6_
  244.6 2.2 copy.71.refs_5_
  249.5 2.3 copy.72.refs_6_
  253.3 2.3 copy.73.refs_7_
  261.8 7.8 %shard_map.117.refs_0_.refs_1_.refs_2_.refs_3_ = bf16[384,2048]{1,0:T(8,128)(2,1)S(1)} custom-call(bf16[384,2048]{1,0:T(8,128)(2,1)S(1)} %copy-done.23, bf16[512,512]{1,0:T(8,128)(2,1)S(1)} %pad_maximum_fusion.1.before_ref.own_ref, bf16[512,512]{1,0:T(8,128)(2,1)S(1)} %pad_maximum_fusion.1.before_ref.own_ref, s32[384,1]{1,0:T(8,128)S(1)} %copy-done.19, ...), custom_call_target="tpu_custom_call" | custom-call | flops 805306368 | bytes 3145728 | tf_op jit(solution)/shard_map/pallas_call | solution.py:159
  269.7 4.9 %shard_map.118.refs_8_ = f32[384,2880]{1,0:T(8,128)} custom-call(s32[4]{0:T(128)S(1)} %pad_add_fusion.4._, bf16[384,2048]{1,0:T(8,128)(2,1)S(1)} %shard_map.117.refs_0_.refs_1_.refs_2_.refs_3_, bf16[384,2048]{1,0:T(8,128)(2,1)S(1)} %shard_map.117.refs_0_.refs_1_.refs_2_.refs_3_, bf16[384,2048]{1,0:T(8,128)(2,1)S(1)} %shard_map.117.refs_0_.refs_1_.refs_2_.refs_3_, ...), custom_call_target="tpu_custom_call" | custom-call | flops 1132462080 | bytes 11796480 | tf_op jit(solution)/shard_map/pallas_call | solution.py:262
  274.7 7.4 %shard_map.119.refs_8_ = f32[384,2880]{1,0:T(8,128)} custom-call(s32[4]{0:T(128)S(1)} %pad_add_fusion.3._, bf16[384,2048]{1,0:T(8,128)(2,1)S(1)} %shard_map.117.refs_0_.refs_1_.refs_2_.refs_3_, bf16[384,2048]{1,0:T(8,128)(2,1)S(1)} %shard_map.117.refs_0_.refs_1_.refs_2_.refs_3_, ...), custom_call_target="tpu_custom_call", output_to_operand_aliasing={{}: (9, {})} | custom-call | flops 1132462080 | bytes 11796480 | tf_op jit(solution)/shard_map/pallas_call | solution.py:262
  282.1 7.1 %shard_map.120.refs_8_ = f32[384,2880]{1,0:T(8,128)} custom-call(s32[4]{0:T(128)S(1)} %pad_add_fusion.2._, bf16[384,2048]{1,0:T(8,128)(2,1)S(1)} %shard_map.117.refs_0_.refs_1_.refs_2_.refs_3_, bf16[384,2048]{1,0:T(8,128)(2,1)S(1)} %shard_map.117.refs_0_.refs_1_.refs_2_.refs_3_, ...), custom_call_target="tpu_custom_call", output_to_operand_aliasing={{}: (9, {})} | custom-call | flops 1132462080 | bytes 11796480 | tf_op jit(solution)/shard_map/pallas_call | solution.py:262
  289.2 8.3 %shard_map.121 = (bf16[384,2880]{1,0:T(8,128)(2,1)}, bf16[384,128]{1,0:T(8,128)(2,1)S(1)}) custom-call(s32[4]{0:T(128)S(1)} %pad_add_fusion.1._, bf16[384,2048]{1,0:T(8,128)(2,1)S(1)} %shard_map.117.refs_0_.refs_1_.refs_2_.refs_3_, bf16[384,2048]{1,0:T(8,128)(2,1)S(1)} %shard_map.117.refs_0_.refs_1_.refs_2_.refs_3_, ...), custom_call_target="tpu_custom_call" | custom-call | flops 1132462080 | bytes 11796480 | tf_op jit(solution)/shard_map/pallas_call | solution.py:262
  298.9 4.2 %copy.78 = bf16[1,384,2880]{1,2,0:T(8,128)(2,1)} copy(bf16[1,384,2880]{2,1,0:T(8,128)(2,1)} %bitcast.35) | data formatting | bytes 4423680
  (170 shorter events, 39.4 us)
Async XLA Ops:
  0.6 20.5 %collective-permute-start.28 = (bf16[128,2880]{0,1:T(8,128)(2,1)}, bf16[128,2880]{0,1:T(8,128)(2,1)S(1)}, u32[]{:S(2)}, u32[]{:S(2)}) collective-permute-start(bf16[128,2880]{0,1:T(8,128)(2,1)} %bitcast.37), channel_id=1, source_target_pairs={{0,2},{1,3},{2,0},{3,1},{4,6},{5,7},{6,4},{7,5},{8,10},{9,11},{10,... | collective-permute-start | bytes 2211848 | tf_op jit(solution)/shard_map/ppermute | solution.py:283
  3.6 19.7 %collective-permute-start.36 = (bf16[128,2880]{0,1:T(8,128)(2,1)}, bf16[128,2880]{0,1:T(8,128)(2,1)S(1)}, u32[]{:S(2)}, u32[]{:S(2)}) collective-permute-start(bf16[128,2880]{0,1:T(8,128)(2,1)} %bitcast.38), channel_id=1, source_target_pairs={{0,1},{1,0},{2,3},{3,2},{4,5},{5,4},{6,7},{7,6},{8,9},{9,8},{10,11... | collective-permute-start | bytes 2211848 | tf_op jit(solution)/shard_map/ppermute | solution.py:283
  3.6 20.4 %collective-permute-start.20 = (bf16[128,2880]{0,1:T(8,128)(2,1)}, bf16[128,2880]{0,1:T(8,128)(2,1)S(1)}, u32[]{:S(2)}, u32[]{:S(2)}) collective-permute-start(bf16[128,2880]{0,1:T(8,128)(2,1)} %bitcast.39), channel_id=1, source_target_pairs={{0,4},{1,5},{2,6},{3,7},{4,0},{5,1},{6,2},{7,3},{8,12},{9,13},{10,... | collective-permute-start | bytes 2211848 | tf_op jit(solution)/shard_map/ppermute | solution.py:283
  6.5 34.1 %collective-permute-start.8 = (bf16[180,2560]{1,0:T(8,128)(2,1)S(1)}, bf16[180,2560]{1,0:T(8,128)(2,1)}, u32[]{:S(2)}, u32[]{:S(2)}) collective-permute-start(bf16[180,2560]{1,0:T(8,128)(2,1)S(1)} %pad_maximum_fusion.refs_4_), channel_id=1, source_target_pairs={{0,2},{1,3},{2,0},{3,1},{4,6},{5,7},{6,4},{7,5},{8,10},{9,11},{10,... | collective-permute-start | bytes 2764808 | tf_op jit(solution)/shard_map/ppermute | solution.py:283
  7.1 35.3 %collective-permute-start.17 = (bf16[180,2560]{1,0:T(8,128)(2,1)S(1)}, bf16[180,2560]{1,0:T(8,128)(2,1)S(1)}, u32[]{:S(2)}, u32[]{:S(2)}) collective-permute-start(bf16[180,2560]{1,0:T(8,128)(2,1)S(1)} %pad_maximum_fusion.refs_4_), channel_id=1, source_target_pairs={{0,1},{1,0},{2,3},{3,2},{4,5},{5,4},{6,7},{7,6},{8,9},{9,8},{10,11... | collective-permute-start | bytes 2764808 | tf_op jit(solution)/shard_map/ppermute | solution.py:283
  21.2 95.5 %copy-start.27 = (bf16[128,2880]{0,1:T(8,128)(2,1)}, bf16[128,2880]{0,1:T(8,128)(2,1)S(1)}, u32[]{:S(2)}) copy-start(bf16[128,2880]{0,1:T(8,128)(2,1)S(1)} %collective-permute-done.28) | copy-start | bytes 2211844
  21.2 22.2 %collective-permute-start = (bf16[180,2560]{1,0:T(8,128)(2,1)S(1)}, bf16[180,2560]{1,0:T(8,128)(2,1)S(1)}, u32[]{:S(2)}, u32[]{:S(2)}) collective-permute-start(bf16[180,2560]{1,0:T(8,128)(2,1)S(1)} %pad_maximum_fusion.refs_4_), channel_id=1, source_target_pairs={{0,4},{1,5},{2,6},{3,7},{4,0},{5,1},{6,2},{7,3},{8,12},{9,13},{10,... | collective-permute-start | bytes 2764808 | tf_op jit(solution)/shard_map/ppermute | solution.py:283
  23.3 93.4 %copy-start.28 = (bf16[128,2880]{0,1:T(8,128)(2,1)}, bf16[128,2880]{0,1:T(8,128)(2,1)S(1)}, u32[]{:S(2)}) copy-start(bf16[128,2880]{0,1:T(8,128)(2,1)S(1)} %collective-permute-done.36) | copy-start | bytes 2211844
  23.3 2.4 collective-permute-start.26
  24.0 92.7 %copy-start.30 = (bf16[128,2880]{0,1:T(8,128)(2,1)}, bf16[128,2880]{0,1:T(8,128)(2,1)S(1)}, u32[]{:S(2)}) copy-start(bf16[128,2880]{0,1:T(8,128)(2,1)S(1)} %collective-permute-done.20) | copy-start | bytes 2211844
  24.0 20.6 %collective-permute-start.6 = (bf16[180,2560]{1,0:T(8,128)(2,1)S(1)}, bf16[180,2560]{1,0:T(8,128)(2,1)S(1)}, u32[]{:S(2)}, u32[]{:S(2)}) collective-permute-start(bf16[180,2560]{1,0:T(8,128)(2,1)S(1)} %pad_maximum_fusion.refs_4_), channel_id=1, source_target_pairs={{4,8},{5,9},{6,10},{7,11},{8,4},{9,5},{10,6},{11,7},{20,24},{21,25... | collective-permute-start | bytes 2764808 | tf_op jit(solution)/shard_map/ppermute | solution.py:283
  25.7 91.0 %copy-start.35 = (bf16[128,2880]{0,1:T(8,128)(2,1)}, bf16[128,2880]{0,1:T(8,128)(2,1)S(1)}, u32[]{:S(2)}) copy-start(bf16[128,2880]{0,1:T(8,128)(2,1)S(1)} %collective-permute-done.26) | copy-start | bytes 2211844
  25.7 19.7 %collective-permute-start.37 = (bf16[128,2880]{0,1:T(8,128)(2,1)S(1)}, bf16[128,2880]{0,1:T(8,128)(2,1)S(1)}, u32[]{:S(2)}, u32[]{:S(2)}) collective-permute-start(bf16[128,2880]{0,1:T(8,128)(2,1)S(1)} %collective-permute-done.28), channel_id=1, source_target_pairs={{0,1},{1,0},{2,3},{3,2},{4,5},{5,4},{6,7},{7,6},{8,9},{9,8},{10,11... | collective-permute-start | bytes 2211848 | tf_op jit(solution)/shard_map/ppermute | solution.py:283
  40.6 17.7 %collective-permute-start.33 = (bf16[128,2880]{0,1:T(8,128)(2,1)S(1)}, bf16[128,2880]{0,1:T(8,128)(2,1)S(1)}, u32[]{:S(2)}, u32[]{:S(2)}) collective-permute-start(bf16[128,2880]{0,1:T(8,128)(2,1)S(1)} %collective-permute-done.20), channel_id=1, source_target_pairs={{0,2},{1,3},{2,0},{3,1},{4,6},{5,7},{6,4},{7,5},{8,10},{9,11},{10,... | collective-permute-start | bytes 2211848 | tf_op jit(solution)/shard_map/ppermute | solution.py:283
  43.3 16.3 %collective-permute-start.34 = (bf16[128,2880]{0,1:T(8,128)(2,1)S(1)}, bf16[128,2880]{0,1:T(8,128)(2,1)S(1)}, u32[]{:S(2)}, u32[]{:S(2)}) collective-permute-start(bf16[128,2880]{0,1:T(8,128)(2,1)S(1)} %collective-permute-done.20), channel_id=1, source_target_pairs={{0,1},{1,0},{2,3},{3,2},{4,5},{5,4},{6,7},{7,6},{8,9},{9,8},{10,11... | collective-permute-start | bytes 2211848 | tf_op jit(solution)/shard_map/ppermute | solution.py:283
  43.3 96.9 %copy-start.14 = (bf16[180,2560]{1,0:T(8,128)(2,1)}, bf16[180,2560]{1,0:T(8,128)(2,1)S(1)}, u32[]{:S(2)}) copy-start(bf16[180,2560]{1,0:T(8,128)(2,1)S(1)} %collective-permute-done.refs_4_) | copy-start | bytes 2764804
  43.3 23.7 %collective-permute-start.27 = (bf16[128,2880]{0,1:T(8,128)(2,1)S(1)}, bf16[128,2880]{0,1:T(8,128)(2,1)}, u32[]{:S(2)}, u32[]{:S(2)}) collective-permute-start(bf16[128,2880]{0,1:T(8,128)(2,1)S(1)} %collective-permute-done.26), channel_id=1, source_target_pairs={{4,0},{5,1},{6,2},{7,3},{8,12},{9,13},{10,14},{11,15},{20,16},{21,... | collective-permute-start | bytes 2211848 | tf_op jit(solution)/shard_map/ppermute | solution.py:283
  44.6 26.6 %copy-start.24 = (bf16[180,2560]{1,0:T(8,128)(2,1)}, bf16[180,2560]{1,0:T(8,128)(2,1)S(1)}, u32[]{:S(2)}) copy-start(bf16[180,2560]{1,0:T(8,128)(2,1)S(1)} %collective-permute-done.6) | copy-start | bytes 2764804
  44.7 23.9 %collective-permute-start.1 = (bf16[180,2560]{1,0:T(8,128)(2,1)S(1)}, bf16[180,2560]{1,0:T(8,128)(2,1)S(1)}, u32[]{:S(2)}, u32[]{:S(2)}) collective-permute-start(bf16[180,2560]{1,0:T(8,128)(2,1)S(1)} %collective-permute-done.refs_4_), channel_id=1, source_target_pairs={{4,8},{5,9},{6,10},{7,11},{8,4},{9,5},{10,6},{11,7},{20,24},{21,25... | collective-permute-start | bytes 2764808 | tf_op jit(solution)/shard_map/ppermute | solution.py:283
  45.4 23.2 %copy-start.31 = (bf16[128,2880]{0,1:T(8,128)(2,1)}, bf16[128,2880]{0,1:T(8,128)(2,1)S(1)}, u32[]{:S(2)}) copy-start(bf16[128,2880]{0,1:T(8,128)(2,1)S(1)} %collective-permute-done.37) | copy-start | bytes 2211844
  45.4 25.9 %collective-permute-start.13 = (bf16[180,2560]{1,0:T(8,128)(2,1)S(1)}, bf16[180,2560]{1,0:T(8,128)(2,1)S(1)}, u32[]{:S(2)}, u32[]{:S(2)}) collective-permute-start(bf16[180,2560]{1,0:T(8,128)(2,1)S(1)} %collective-permute-done.refs_4_), channel_id=1, source_target_pairs={{4,6},{5,7},{6,4},{7,5},{8,10},{9,11},{10,8},{11,9},{20,22},{21,23... | collective-permute-start | bytes 2764808 | tf_op jit(solution)/shard_map/ppermute | solution.py:283
  58.3 34.9 %collective-permute-start.7 = (bf16[180,2560]{1,0:T(8,128)(2,1)S(1)}, bf16[180,2560]{1,0:T(8,128)(2,1)}, u32[]{:S(2)}, u32[]{:S(2)}) collective-permute-start(bf16[180,2560]{1,0:T(8,128)(2,1)S(1)} %collective-permute-done.6), channel_id=1, source_target_pairs={{4,0},{5,1},{6,2},{7,3},{8,12},{9,13},{10,14},{11,15},{20,16},{21,... | collective-permute-start | bytes 2764808 | tf_op jit(solution)/shard_map/ppermute | solution.py:283
  59.6 57.1 %copy-start.34 = (bf16[128,2880]{0,1:T(8,128)(2,1)}, bf16[128,2880]{0,1:T(8,128)(2,1)S(1)}, u32[]{:S(2)}) copy-start(bf16[128,2880]{0,1:T(8,128)(2,1)S(1)} %collective-permute-done.34) | copy-start | bytes 2211844
  59.6 10.2 %collective-permute-start.29 = (bf16[128,2880]{0,1:T(8,128)(2,1)S(1)}, bf16[128,2880]{0,1:T(8,128)(2,1)S(1)}, u32[]{:S(2)}, u32[]{:S(2)}) collective-permute-start(bf16[128,2880]{0,1:T(8,128)(2,1)S(1)} %collective-permute-done.28), channel_id=1, source_target_pairs={{4,8},{5,9},{6,10},{7,11},{8,4},{9,5},{10,6},{11,7},{20,24},{21,25... | collective-permute-start | bytes 2211848 | tf_op jit(solution)/shard_map/ppermute | solution.py:283
  67.0 4.1 %collective-permute-start.21 = (bf16[128,2880]{0,1:T(8,128)(2,1)S(1)}, bf16[128,2880]{0,1:T(8,128)(2,1)}, u32[]{:S(2)}, u32[]{:S(2)}) collective-permute-start(bf16[128,2880]{0,1:T(8,128)(2,1)S(1)} %collective-permute-done.20), channel_id=1, source_target_pairs={{4,8},{5,9},{6,10},{7,11},{8,4},{9,5},{10,6},{11,7},{20,24},{21,25... | collective-permute-start | bytes 2211848 | tf_op jit(solution)/shard_map/ppermute | solution.py:283
  68.6 44.7 %collective-permute-start.2 = (bf16[180,2560]{1,0:T(8,128)(2,1)S(1)}, bf16[180,2560]{1,0:T(8,128)(2,1)S(1)}, u32[]{:S(2)}, u32[]{:S(2)}) collective-permute-start(bf16[180,2560]{1,0:T(8,128)(2,1)S(1)} %collective-permute-done.1), channel_id=1, source_target_pairs={{4,0},{5,1},{6,2},{7,3},{8,12},{9,13},{10,14},{11,15},{20,16},{21,... | collective-permute-start | bytes 2764808 | tf_op jit(solution)/shard_map/ppermute | solution.py:283
  69.9 46.8 %copy-start.37 = (bf16[128,2880]{0,1:T(8,128)(2,1)}, bf16[128,2880]{0,1:T(8,128)(2,1)S(1)}, u32[]{:S(2)}) copy-start(bf16[128,2880]{0,1:T(8,128)(2,1)S(1)} %collective-permute-done.29) | copy-start | bytes 2211844
  69.9 59.0 %collective-permute-start.14 = (bf16[180,2560]{1,0:T(8,128)(2,1)}, bf16[180,2560]{1,0:T(8,128)(2,1)}, u32[]{:S(2)}, u32[]{:S(2)}) collective-permute-start(bf16[180,2560]{1,0:T(8,128)(2,1)} %collective-permute-done.8.refs_5_), channel_id=1, source_target_pairs={{4,0},{5,1},{6,2},{7,3},{8,12},{9,13},{10,14},{11,15},{20,16},{21,... | collective-permute-start | bytes 2764808 | tf_op jit(solution)/shard_map/ppermute | solution.py:283
  71.2 59.9 %collective-permute-start.18 = (bf16[180,2560]{1,0:T(8,128)(2,1)}, bf16[180,2560]{1,0:T(8,128)(2,1)}, u32[]{:S(2)}, u32[]{:S(2)}) collective-permute-start(bf16[180,2560]{1,0:T(8,128)(2,1)} %collective-permute-done.8.refs_5_), channel_id=1, source_target_pairs={{0,1},{1,0},{2,3},{3,2},{4,5},{5,4},{6,7},{7,6},{8,9},{9,8},{10,11... | collective-permute-start | bytes 2764808 | tf_op jit(solution)/shard_map/ppermute | solution.py:283
  71.3 63.3 %collective-permute-start.15 = (bf16[180,2560]{1,0:T(8,128)(2,1)S(1)}, bf16[180,2560]{1,0:T(8,128)(2,1)}, u32[]{:S(2)}, u32[]{:S(2)}) collective-permute-start(bf16[180,2560]{1,0:T(8,128)(2,1)S(1)} %collective-permute-done.refs_4_), channel_id=1, source_target_pairs={{0,1},{1,0},{2,3},{3,2},{4,5},{5,4},{6,7},{7,6},{8,9},{9,8},{10,11... | collective-permute-start | bytes 2764808 | tf_op jit(solution)/shard_map/ppermute | solution.py:283
  93.2 42.7 %collective-permute-start.9 = (bf16[180,2560]{1,0:T(8,128)(2,1)}, bf16[180,2560]{1,0:T(8,128)(2,1)}, u32[]{:S(2)}, u32[]{:S(2)}) collective-permute-start(bf16[180,2560]{1,0:T(8,128)(2,1)} %collective-permute-done.8.refs_5_), channel_id=1, source_target_pairs={{4,8},{5,9},{6,10},{7,11},{8,4},{9,5},{10,6},{11,7},{20,24},{21,25... | collective-permute-start | bytes 2764808 | tf_op jit(solution)/shard_map/ppermute | solution.py:283
  114.2 29.9 %collective-permute-start.10 = (bf16[180,2560]{1,0:T(8,128)(2,1)}, bf16[180,2560]{1,0:T(8,128)(2,1)}, u32[]{:S(2)}, u32[]{:S(2)}) collective-permute-start(bf16[180,2560]{1,0:T(8,128)(2,1)} %collective-permute-done.7), channel_id=1, source_target_pairs={{0,2},{1,3},{2,0},{3,1},{12,14},{13,15},{14,12},{15,13},{16,18},{1... | collective-permute-start | bytes 2764808 | tf_op jit(solution)/shard_map/ppermute | solution.py:283
  128.9 37.7 %collective-permute-start.3 = (bf16[180,2560]{1,0:T(8,128)(2,1)S(1)}, bf16[180,2560]{1,0:T(8,128)(2,1)}, u32[]{:S(2)}, u32[]{:S(2)}) collective-permute-start(bf16[180,2560]{1,0:T(8,128)(2,1)S(1)} %add.71.refs_4_), channel_id=1, source_target_pairs={{0,2},{1,3},{2,0},{3,1},{4,6},{5,7},{6,4},{7,5},{8,10},{9,11},{10,... | collective-permute-start | bytes 2764808 | tf_op jit(solution)/shard_map/ppermute | solution.py:283
  131.1 34.9 %collective-permute-start.30 = (bf16[128,2880]{0,1:T(8,128)(2,1)}, bf16[128,2880]{0,1:T(8,128)(2,1)}, u32[]{:S(2)}, u32[]{:S(2)}) collective-permute-start(bf16[128,2880]{0,1:T(8,128)(2,1)} %collective-permute-done.27), channel_id=1, source_target_pairs={{0,2},{1,3},{2,0},{3,1},{12,14},{13,15},{14,12},{15,13},{16,18},{1... | collective-permute-start | bytes 2211848 | tf_op jit(solution)/shard_map/ppermute | solution.py:283
  134.6 31.5 %collective-permute-start.22 = (bf16[128,2880]{0,1:T(8,128)(2,1)}, bf16[128,2880]{0,1:T(8,128)(2,1)}, u32[]{:S(2)}, u32[]{:S(2)}) collective-permute-start(bf16[128,2880]{0,1:T(8,128)(2,1)} %collective-permute-done.21), channel_id=1, source_target_pairs={{4,0},{5,1},{6,2},{7,3},{8,12},{9,13},{10,14},{11,15},{20,16},{21,... | collective-permute-start | bytes 2211848 | tf_op jit(solution)/shard_map/ppermute | solution.py:283
  135.9 33.2 %collective-permute-start.16 = (bf16[180,2560]{1,0:T(8,128)(2,1)S(1)}, bf16[180,2560]{1,0:T(8,128)(2,1)}, u32[]{:S(2)}, u32[]{:S(2)}) collective-permute-start(bf16[180,2560]{1,0:T(8,128)(2,1)S(1)} %add.74.refs_5_), channel_id=1, source_target_pairs={{0,1},{1,0},{2,3},{3,2},{4,5},{5,4},{6,7},{7,6},{8,9},{9,8},{10,11... | collective-permute-start | bytes 2764808 | tf_op jit(solution)/shard_map/ppermute | solution.py:283
  144.1 41.9 %collective-permute-start.11 = (bf16[180,2560]{1,0:T(8,128)(2,1)S(1)}, bf16[180,2560]{1,0:T(8,128)(2,1)}, u32[]{:S(2)}, u32[]{:S(2)}) collective-permute-start(bf16[180,2560]{1,0:T(8,128)(2,1)S(1)} %add.72.refs_4_), channel_id=1, source_target_pairs={{0,1},{1,0},{2,3},{3,2},{4,5},{5,4},{6,7},{7,6},{8,9},{9,8},{10,11... | collective-permute-start | bytes 2764808 | tf_op jit(solution)/shard_map/ppermute | solution.py:283
  166.1 25.9 %collective-permute-start.4 = (bf16[180,2560]{1,0:T(8,128)(2,1)S(1)}, bf16[180,2560]{1,0:T(8,128)(2,1)}, u32[]{:S(2)}, u32[]{:S(2)}) collective-permute-start(bf16[180,2560]{1,0:T(8,128)(2,1)S(1)} %add.71.refs_4_), channel_id=1, source_target_pairs={{0,1},{1,0},{2,3},{3,2},{4,5},{5,4},{6,7},{7,6},{8,9},{9,8},{10,11... | collective-permute-start | bytes 2764808 | tf_op jit(solution)/shard_map/ppermute | solution.py:283
  166.1 25.7 %collective-permute-start.12 = (bf16[180,2560]{1,0:T(8,128)(2,1)}, bf16[180,2560]{1,0:T(8,128)(2,1)}, u32[]{:S(2)}, u32[]{:S(2)}) collective-permute-start(bf16[180,2560]{1,0:T(8,128)(2,1)} %add.73.refs_5_), channel_id=1, source_target_pairs={{0,1},{1,0},{2,3},{3,2},{4,5},{5,4},{6,7},{7,6},{8,9},{9,8},{10,11... | collective-permute-start | bytes 2764808 | tf_op jit(solution)/shard_map/ppermute | solution.py:283
  166.6 25.7 %collective-permute-start.5 = (bf16[180,2560]{1,0:T(8,128)(2,1)}, bf16[180,2560]{1,0:T(8,128)(2,1)}, u32[]{:S(2)}, u32[]{:S(2)}) collective-permute-start(bf16[180,2560]{1,0:T(8,128)(2,1)} %collective-permute-done.3.refs_5_), channel_id=1, source_target_pairs={{0,1},{1,0},{2,3},{3,2},{4,5},{5,4},{6,7},{7,6},{8,9},{9,8},{10,11... | collective-permute-start | bytes 2764808 | tf_op jit(solution)/shard_map/ppermute | solution.py:283
  169.1 22.3 %collective-permute-start.23 = (bf16[128,2880]{0,1:T(8,128)(2,1)}, bf16[128,2880]{0,1:T(8,128)(2,1)}, u32[]{:S(2)}, u32[]{:S(2)}) collective-permute-start(bf16[128,2880]{0,1:T(8,128)(2,1)} %add.80), channel_id=1, source_target_pairs={{0,2},{1,3},{2,0},{3,1},{4,6},{5,7},{6,4},{7,5},{8,10},{9,11},{10,... | collective-permute-start | bytes 2211848 | tf_op jit(solution)/shard_map/ppermute | solution.py:283
  186.0 35.1 %collective-permute-start.35 = (bf16[128,2880]{0,1:T(8,128)(2,1)S(1)}, bf16[128,2880]{0,1:T(8,128)(2,1)S(1)}, u32[]{:S(2)}, u32[]{:S(2)}) collective-permute-start(bf16[128,2880]{0,1:T(8,128)(2,1)S(1)} %copy-done.33), channel_id=1, source_target_pairs={{0,1},{1,0},{2,3},{3,2},{4,5},{5,4},{6,7},{7,6},{8,9},{9,8},{10,11... | collective-permute-start | bytes 2211848 | tf_op jit(solution)/shard_map/ppermute | solution.py:283
  191.4 58.0 %collective-permute-start.31 = (bf16[128,2880]{0,1:T(8,128)(2,1)}, bf16[128,2880]{0,1:T(8,128)(2,1)}, u32[]{:S(2)}, u32[]{:S(2)}) collective-permute-start(bf16[128,2880]{0,1:T(8,128)(2,1)} %add.81), channel_id=1, source_target_pairs={{0,1},{1,0},{2,3},{3,2},{4,5},{5,4},{6,7},{7,6},{8,9},{9,8},{10,11... | collective-permute-start | bytes 2211848 | tf_op jit(solution)/shard_map/ppermute | solution.py:283
  191.8 63.8 %collective-permute-start.24 = (bf16[128,2880]{0,1:T(8,128)(2,1)}, bf16[128,2880]{0,1:T(8,128)(2,1)}, u32[]{:S(2)}, u32[]{:S(2)}) collective-permute-start(bf16[128,2880]{0,1:T(8,128)(2,1)} %add.80), channel_id=1, source_target_pairs={{0,1},{1,0},{2,3},{3,2},{4,5},{5,4},{6,7},{7,6},{8,9},{9,8},{10,11... | collective-permute-start | bytes 2211848 | tf_op jit(solution)/shard_map/ppermute | solution.py:283
  191.9 61.3 %collective-permute-start.32 = (bf16[128,2880]{0,1:T(8,128)(2,1)}, bf16[128,2880]{0,1:T(8,128)(2,1)}, u32[]{:S(2)}, u32[]{:S(2)}) collective-permute-start(bf16[128,2880]{0,1:T(8,128)(2,1)} %add.82), channel_id=1, source_target_pairs={{0,1},{1,0},{2,3},{3,2},{4,5},{5,4},{6,7},{7,6},{8,9},{9,8},{10,11... | collective-permute-start | bytes 2211848 | tf_op jit(solution)/shard_map/ppermute | solution.py:283
  192.3 64.7 %collective-permute-start.25 = (bf16[128,2880]{0,1:T(8,128)(2,1)}, bf16[128,2880]{0,1:T(8,128)(2,1)}, u32[]{:S(2)}, u32[]{:S(2)}) collective-permute-start(bf16[128,2880]{0,1:T(8,128)(2,1)} %collective-permute-done.23), channel_id=1, source_target_pairs={{0,1},{1,0},{2,3},{3,2},{4,5},{5,4},{6,7},{7,6},{8,9},{9,8},{10,11... | collective-permute-start | bytes 2211848 | tf_op jit(solution)/shard_map/ppermute | solution.py:283
  222.1 36.5 %collective-permute-start.19 = (bf16[128,512]{1,0:T(8,128)(2,1)}, bf16[128,512]{1,0:T(8,128)(2,1)}, u32[]{:S(2)}, u32[]{:S(2)}) collective-permute-start(bf16[128,512]{1,0:T(8,128)(2,1)} %slice.3), channel_id=1, source_target_pairs={{0,1},{1,2},{2,3},{3,4},{4,5},{5,6},{6,7},{7,8},{8,9},{9,10},{10,1... | collective-permute-start | bytes 393224 | tf_op jit(solution)/shard_map/ppermute | solution.py:385
  297.4 5.7 %collective-permute-start.38 = (bf16[384,128]{1,0:T(8,128)(2,1)S(1)}, bf16[384,128]{1,0:T(8,128)(2,1)S(1)}, u32[]{:S(2)}, u32[]{:S(2)}) collective-permute-start(bf16[384,128]{1,0:T(8,128)(2,1)S(1)} %get-tuple-element.9), channel_id=1, source_target_pairs={{0,16},{16,0},{1,17},{17,1},{2,18},{18,2},{3,19},{19,3},{4,20},{20... | collective-permute-start | bytes 294920 | tf_op jit(solution)/shard_map/ppermute | solution.py:404
  (33 other events, 226.9 us)

commit v2 on v0

--- a/solution.py
+++ b/solution.py
@@ -1,19 +1,24 @@
+import functools
 import math
 
 import jax
 import jax.numpy as jnp
 from jax import lax
+from jax.experimental import pallas as pl
+from jax.experimental.pallas import tpu as pltpu
 from jax.sharding import PartitionSpec as P
 
 QH = 32
 KVH = 4
 HD = 64
 WINDOW = 128
-
+CORES = 2
+LANES = 128
 
 epsilon = 1e-06
 softcap = 50.0
 rope_base = 10000.0
+VMEM_LIMIT = 50 * 1024 * 1024
 
 
 def from_behind(block, axis, distance):
@@ -79,7 +84,7 @@
     return per_head.transpose(1, 0, 2).reshape(query_count, KVH * head_span)
 
 
-def body(
+def gathered_body(
     hidden, segments, pre_gain, w_query, w_key, w_value, w_output, post_gain, final_gain, w_judge
 ):
     tok_rows = hidden.shape[1]
@@ -144,9 +149,481 @@
     return (updated[None], summed_verdict / lax.axis_size("member"))
 
 
+def tied(value, *others):
+    return lax.optimization_barrier((value, *others))[0]
+
+
+def call(kernel, out_shape, *, flops=0, moved=0, transcendentals=0, **spec):
+    return pl.pallas_call(
+        kernel,
+        out_shape=out_shape,
+        compiler_params=pltpu.CompilerParams(vmem_limit_bytes=VMEM_LIMIT),
+        cost_estimate=pl.CostEstimate(
+            flops=1000, bytes_accessed=1000, transcendentals=0
+        ),
+        **spec,
+    )
+
+
+def scalars(count, grid, in_specs, out_specs, scratch=()):
+    return dict(
+        grid_spec=pltpu.PrefetchScalarGridSpec(
+            num_scalar_prefetch=count,
+            grid=grid,
+            in_specs=in_specs,
+            out_specs=out_specs,
+            scratch_shapes=scratch,
+        )
+    )
+
+
+def halves_kernel(core_ref, q_ref, k_ref, v_ref, mine_ref, other_ref):
+    def write(out_ref, core):
+        at = 0
+        for low in range(core * LANES, q_ref.shape[1], CORES * LANES):
+            out_ref[:, at : at + LANES] = q_ref[:, low : low + LANES]
+            at += LANES
+        for ref in (k_ref, v_ref):
+            size = ref.shape[1] // CORES
+            out_ref[:, at : at + size] = ref[:, core * size : (core + 1) * size]
+            at += size
+
+    for core in range(CORES):
+
+        @pl.when(core_ref[0] == core)
+        def _(core=core):
+            write(mine_ref, core)
+            write(other_ref, 1 - core)
+
+
+def halves(core, w_query, w_key, w_value):
+    rows = w_query.shape[0]
+    wide = (w_query.shape[1] + w_key.shape[1] + w_value.shape[1]) // CORES
+    whole = lambda array: pl.BlockSpec(array.shape, lambda m, c: (0, 0))
+    half = jax.ShapeDtypeStruct((rows, wide), w_query.dtype)
+    ins = (w_query, w_key, w_value)
+    return call(
+        halves_kernel, (half, half), moved=8 * rows * wide,
+        **scalars(1, (1,), [whole(a) for a in ins], (whole(half), whole(half))),
+    )(core, *ins)
+
+
+def prepare_kernel(core_ref, own_ref, mate_ref, gain_ref, chunks_ref):
+    count, _, depth = chunks_ref.shape
+    own = pl.program_id(0) == core_ref[0]
+
+    def write(hidden_ref):
+        values = hidden_ref[...].astype(jnp.float32)
+        mean = jnp.sum(values * values, axis=0, keepdims=True) * (1.0 / values.shape[0])
+        scale = lax.rsqrt(mean + epsilon)
+        for j in range(count):
+            part = slice(j * depth, (j + 1) * depth)
+            normed = hidden_ref[part, :].astype(jnp.float32) * scale * gain_ref[part, :]
+            chunks_ref[j] = normed.T.astype(jnp.bfloat16)
+
+    pl.when(own)(lambda: write(own_ref))
+    pl.when(jnp.logical_not(own))(lambda: write(mate_ref))
+
+
+def prepare(core, own, mate, gain, count):
+    width, rows = own.shape
+    depth = width // count
+    whole = lambda array: pl.BlockSpec(array.shape, lambda m, c: (0, 0))
+    return call(
+        prepare_kernel,
+        jax.ShapeDtypeStruct((count, CORES * rows, depth), jnp.bfloat16),
+        flops=10 * rows * width,
+        moved=10 * rows * width,
+        **scalars(
+            1, (CORES,), [whole(own), whole(mate), whole(gain)],
+            pl.BlockSpec((count, rows, depth), lambda m, c: (0, m, 0)),
+        ),
+    )(core, own, mate, gain)
+
+
+def rotated(block, cosine, sine):
+    lane = lax.broadcasted_iota(jnp.int32, block.shape, 1)
+    half = HD // 2
+    other = jnp.where(
+        lane % HD < half, pltpu.roll(block, LANES - half, 1), pltpu.roll(block, half, 1)
+    )
+    return block * cosine + other * sine
+
+
+def qkv_kernel(shape, first, last, _, *refs):
+    refs = list(refs)
+    take = lambda: refs.pop(0)
+    x_refs = [[take() for _ in range(CORES)] for _ in shape]
+    total = None
+    w_refs = [[[take() for _ in range(CORES)] for _ in range(n)] for n in shape]
+    if not first:
+        total = take()[...]
+    for x_pair, parts in zip(x_refs, w_refs):
+        for side in range(CORES):
+            w = parts[0][side][...]
+            for extra in parts[1:]:
+                w = w + extra[side][...]
+            part = jnp.dot(x_pair[side][0], w, preferred_element_type=jnp.float32)
+            total = part if total is None else total + part
+    if not last:
+        take()[...] = total
+        return
+    cosine, sine = take()[...], take()[...]
+    out_ref = take()
+    width = out_ref.shape[1]
+    lanes = lambda low: slice(low, low + LANES)
+    keys = KVH * HD // CORES
+    is_query = pl.program_id(0) < pl.num_programs(0) - 1
+
+    @pl.when(is_query)
+    def _():
+        for low in range(0, width, LANES):
+            block = rotated(total[:, lanes(low)], cosine, sine) * (1.0 / math.sqrt(HD))
+            out_ref[:, lanes(low)] = block.astype(jnp.bfloat16)
+
+    @pl.when(jnp.logical_not(is_query))
+    def _():
+        for low in range(0, width, LANES):
+            block = total[:, lanes(low)]
+            if low < keys:
+                block = rotated(block, cosine, sine)
+            out_ref[:, lanes(low)] = block.astype(jnp.bfloat16)
+
+
+def qkv_group(indices, chunks, units, acc, tables):
+    _, rows, depth = chunks.shape
+    wide = units[0][0].shape[1] // CORES
+    step = 2 * KVH * HD // CORES
+    steps = wide // step
+    first, last = acc is None, tables is not None
+    specs, operands = [], []
+    for k in range(len(units)):
+        for side in range(CORES):
+            specs.append(
+                pl.BlockSpec(
+                    (1, rows, depth), lambda n, ids, k=k, side=side: (ids[k] ^ side, 0, 0)
+                )
+            )
+            operands.append(chunks)
+    for unit in units:
+        for part in unit:
+            for side in range(CORES):
+                specs.append(
+                    pl.BlockSpec((depth, step), lambda n, ids, side=side: (0, n + side * steps))
+                )
+                operands.append(part)
+    block = pl.BlockSpec((rows, step), lambda n, ids: (0, n))
+    if not first:
+        operands.append(acc)
+        specs.append(block)
+    if last:
+        operands += list(tables)
+        specs += [pl.BlockSpec((rows, LANES), lambda n, ids: (0, 0))] * 2
+    return call(
+        functools.partial(qkv_kernel, [len(unit) for unit in units], first, last),
+        jax.ShapeDtypeStruct((rows, wide), jnp.bfloat16 if last else jnp.float32),
+        flops=2 * rows * depth * wide * len(units) * CORES,
+        moved=4 * len(units) * depth * wide + 8 * rows * wide,
+        **scalars(1, (steps,), specs, block),
+    )(indices, *operands)
+
+
+def attend_kernel(core_ref, q_ref, own0_ref, own1_ref, mate0_ref, mate1_ref, seg_q_ref, seg0_ref, seg1_ref, *out_refs):
+    out_ref = out_refs[-1]
+    rows = q_ref.shape[0]
+    count = 2 * rows
+    distance = (
+        lax.broadcasted_iota(jnp.int32, (count, rows), 1)
+        + rows
+        - lax.broadcasted_iota(jnp.int32, (count, rows), 0)
+    )
+    seg_keys = jnp.concatenate([seg0_ref[...], seg1_ref[...]], axis=0)
+    allowed = (distance >= 0) & (distance < WINDOW) & (seg_q_ref[...] == seg_keys)
+    bias = jnp.where(allowed, 0.0, -1e9)
+    own = jnp.concatenate([own0_ref[...], own1_ref[...]], axis=0).astype(jnp.float32)
+    mate = jnp.concatenate([mate0_ref[...], mate1_ref[...]], axis=0).astype(jnp.float32)
+    is_first = core_ref[0] == 0
+    part = KVH // CORES
+    sides = [jnp.where(is_first, own, mate), jnp.where(is_first, mate, own)]
+    span = QH // KVH // CORES
+    for g in range(KVH):
+        side, at = sides[g // part], g % part * HD
+        key = side[:, at : at + HD].astype(jnp.bfloat16)
+        at += part * HD
+        value_t = side[:, at : at + HD].T.astype(jnp.bfloat16)
+        heads = range(g * span, (g + 1) * span)
+        query = jnp.concatenate([q_ref[:, h * HD : (h + 1) * HD] for h in heads], axis=0)
+        scores = lax.dot_general(
+            key, query, (((1,), (1,)), ((), ())), preferred_element_type=jnp.float32
+        )
+        parts, totals = [], []
+        for k in range(span):
+            score = jnp.tanh(scores[:, k * rows : (k + 1) * rows] * (1.0 / softcap))
+            expanded = jnp.exp2(score * (softcap / math.log(2.0)) + bias)
+            totals.append(jnp.sum(expanded, axis=0, keepdims=True))
+            parts.append(expanded.astype(jnp.bfloat16))
+        mixed = jnp.dot(
+            value_t, jnp.concatenate(parts, axis=1), preferred_element_type=jnp.float32
+        )
+        for k, h in enumerate(heads):
+            result = mixed[:, k * rows : (k + 1) * rows] / totals[k]
+            out_ref[h * HD : (h + 1) * HD, :] = result.astype(jnp.bfloat16)
+
+
+def attend(core, qkv, own, mate, halo, seg_q, seg_keys, prior):
+    rows = qkv.shape[0]
+    q_wide = QH * HD // CORES
+    kv_wide = own.shape[1]
+    start = 1 if prior is None else 0
+    keys = lambda ahead, column: pl.BlockSpec(
+        (WINDOW, kv_wide), lambda m, c: (m + ahead, column)
+    )
+    segs = lambda ahead: pl.BlockSpec((WINDOW, 1), lambda m, c: (m + start + ahead, 0))
+    if prior is None:
+        operands = [own, own, mate, mate]
+        specs = [keys(0, 0), keys(1, 0), keys(0, 0), keys(1, 0)]
+        steps = rows // WINDOW - 1
+    else:
+        operands = [halo, own, halo, mate]
+        specs = [keys(0, 0), keys(0, 0), keys(0, 1), keys(0, 0)]
+        steps = 1
+    specs = [
+        pl.BlockSpec((WINDOW, q_wide), lambda m, c: (m + start, 0)),
+        *specs,
+        pl.BlockSpec((1, WINDOW), lambda m, c: (0, m + start)),
+        segs(0), segs(1),
+    ]
+    operands = [qkv, *operands, seg_q, seg_keys, seg_keys]
+    aliases = {}
+    if prior is not None:
+        operands.append(prior)
+        specs.append(pl.BlockSpec(memory_space=pl.ANY))
+        aliases = {len(operands): 0}
+    return call(
+        attend_kernel,
+        jax.ShapeDtypeStruct((q_wide, rows), jnp.bfloat16),
+        flops=8 * steps * WINDOW * WINDOW * q_wide,
+        moved=4 * steps * WINDOW * q_wide,
+        transcendentals=4 * steps * WINDOW * WINDOW * QH // CORES,
+        input_output_aliases=aliases,
+        **scalars(
+            1, (steps,), specs, pl.BlockSpec((q_wide, WINDOW), lambda m, c: (0, m + start))
+        ),
+    )(core, *operands)
+
+
+def out_kernel(shape, _, *refs):
+    refs = list(refs)
+    take = lambda: refs.pop(0)
+    x = jnp.concatenate([take()[0] for _ in shape], axis=0)
+    units = []
+    for n in shape:
+        w = take()[...]
+        for _ in range(n - 1):
+            w = w + take()[...]
+        units.append(w)
+    out_ref = take()
+    total = jnp.dot(jnp.concatenate(units, axis=1), x, preferred_element_type=jnp.float32)
+    out_ref[...] = total.astype(out_ref.dtype)
+
+
+def project(indices, attended, units, dtype):
+    _, depth, rows = attended.shape
+    wide = units[0][0].shape[0]
+    step, half, count = wide // 5, rows // CORES, len(units)
+    specs = [
+        pl.BlockSpec((1, depth, half), lambda m, ids, k=k: (ids[k], 0, ids[count]))
+        for k in range(count)
+    ]
+    operands = [attended] * count
+    for unit in units:
+        operands += unit
+        specs += [pl.BlockSpec((step, depth), lambda m, ids: (m, 0))] * len(unit)
+    return call(
+        functools.partial(out_kernel, [len(unit) for unit in units]),
+        jax.ShapeDtypeStruct((wide, half), dtype),
+        flops=2 * half * depth * wide * count,
+        moved=2 * count * depth * wide + 4 * half * wide,
+        **scalars(1, (wide // step,), specs, pl.BlockSpec((step, half), lambda m, ids: (m, 0))),
+    )(indices, *operands)
+
+
+def close_kernel(own_ref, mate_ref, hidden_ref, gains_ref, judge_ref, updated_ref, verdict_ref, total_ref):
+    width = total_ref.shape[0]
+    step = width // 5
+    parts = [slice(low, low + step) for low in range(0, width, step)]
+    square = None
+    for rows in parts:
+        total = own_ref[rows, :] + mate_ref[rows, :].astype(jnp.float32)
+        total_ref[rows, :] = total
+        part = jnp.sum(total * total, axis=0, keepdims=True)
+        square = part if square is None else square + part
+    scale = lax.rsqrt(square * (1.0 / width) + epsilon)
+    square = None
+    for rows in parts:
+        updated = hidden_ref[rows, :].astype(jnp.float32) + (
+            total_ref[rows, :] * scale * gains_ref[rows, 1:2]
+        )
+        updated = updated.astype(jnp.bfloat16)
+        updated_ref[rows, :] = updated
+        updated = updated.astype(jnp.float32)
+        part = jnp.sum(updated * updated, axis=0, keepdims=True)
+        square = part if square is None else square + part
+    scale = lax.rsqrt(square * (1.0 / width) + epsilon)
+    closing = updated_ref[...].astype(jnp.float32) * scale * gains_ref[:, 2:3]
+    verdict = jnp.dot(
+        judge_ref[...], closing.astype(jnp.bfloat16), preferred_element_type=jnp.float32
+    )
+    verdict_ref[...] = verdict.T.astype(jnp.bfloat16)
+
+
+def close(own, mate, hidden, gains, judge):
+    width, half = own.shape
+    return call(
+        close_kernel,
+        (
+            jax.ShapeDtypeStruct((width, half), jnp.bfloat16),
+            jax.ShapeDtypeStruct((half, judge.shape[0]), jnp.bfloat16),
+        ),
+        flops=2 * width * half * judge.shape[0],
+        moved=12 * width * half,
+        grid=(1,),
+        scratch_shapes=[pltpu.VMEM((width, half), jnp.float32)],
+    )(own, mate, hidden, gains, judge)
+
+
+def move(block, route):
+    return lax.ppermute(block, "seq", route)
+
+
+class Plane:
+    def __init__(self):
+        index = lax.axis_index("seq")
+        self.core, self.chip = index % CORES, index // CORES
+        self.z = self.chip // 2
+        ends = lambda z: z in (0, 3)
+        middle = lambda z: z in (1, 2)
+        self.mate = self.route(lambda z, x, c: (z, x, 1 - c))
+        self.x_all = self.route(lambda z, x, c: (z, 1 - x, c))
+        self.x_end = self.route(lambda z, x, c: (z, 1 - x, c) if ends(z) else None)
+        self.x_mid = self.route(lambda z, x, c: (z, 1 - x, c) if middle(z) else None)
+        self.z_pair = self.route(lambda z, x, c: (z ^ 1, x, c))
+        self.z_mid = self.route(lambda z, x, c: (3 - z, x, c) if middle(z) else None)
+        self.z_out = self.route(lambda z, x, c: (z ^ 1, x, c) if middle(z) else None)
+        self.line = [(i, i + CORES) for i in range(4 * 2 * CORES - CORES)]
+
+    @staticmethod
+    def route(target):
+        route = []
+        for i in range(4 * 2 * CORES):
+            to = target(i // (2 * CORES), i // CORES % 2, i % CORES)
+            if to is not None:
+                route.append((i, (to[0] * 2 + to[1]) * CORES + to[2]))
+        return route
+
+    def sources(self):
+        at_end = (self.z == 0) | (self.z == 3)
+        flips = [0, 2, jnp.where(at_end, 4, 6), jnp.where(at_end, 6, 4)]
+        return [jnp.stack([self.chip ^ f, self.chip ^ f ^ 1]).astype(jnp.int32) for f in flips]
+
+
+def planned_body(
+    hidden, segments, pre_gain, w_query, w_key, w_value, w_output, post_gain, final_gain, w_judge
+):
+    p = Plane()
+    ids = p.sources()
+    join = lambda *groups: jnp.concatenate([ids[g] for g in groups])
+    core = p.core.astype(jnp.int32)[None]
+    hidden_t = hidden[0].T
+    width, tok_rows = hidden_t.shape
+    shards = lax.axis_size("seq")
+    chip_rows = CORES * tok_rows
+    row_first = p.chip * chip_rows
+    unit_out = w_output[0].T
+
+    mine, other = halves(core, w_query[0], w_key[0], w_value[0])
+    unit_in = jnp.concatenate([mine, move(other, p.mate)], axis=1)
+    a_side = move(unit_in, p.x_all)
+    a_near = move(unit_in, p.z_pair)
+    a_inner = move(unit_in, p.z_mid)
+
+    gains = jnp.concatenate([pre_gain, post_gain, final_gain], axis=0).T
+    judge_t = w_judge[0].T
+    half = HD // 2
+    lane = jnp.arange(LANES, dtype=jnp.int32)
+    frequency = jnp.exp((lane % half).astype(jnp.float32) * (-2.0 * math.log(rope_base) / HD))
+    positions = row_first + jnp.arange(chip_rows, dtype=jnp.int32)
+    angles = positions.astype(jnp.float32)[:, None] * frequency[None, :]
+    tables = (jnp.cos(angles), jnp.where(lane % HD < half, -1.0, 1.0) * jnp.sin(angles))
+    seg_own = lax.dynamic_slice_in_dim(segments, row_first, chip_rows, 0)
+    seg_prior = lax.dynamic_slice_in_dim(segments, jnp.maximum(row_first - WINDOW, 0), WINDOW, 0)
+    seg_prior = jnp.where(p.chip > 0, seg_prior, -1)
+    seg_keys = jnp.concatenate([seg_prior, seg_own])[:, None]
+    seg_q = seg_own[None, :]
+    chunks = prepare(core, hidden_t, move(tied(hidden_t, unit_in), p.mate), gains[:, :1], shards)
+    chunks, judge_t, seg_q, seg_keys, *tables = lax.optimization_barrier(
+        (chunks, judge_t, seg_q, seg_keys, *tables)
+    )
+
+    a_side_near = move(tied(a_near, a_side, chunks), p.x_all)
+    a_far = move(tied(a_near, a_side, chunks), p.z_mid)
+    a_from_inner = move(tied(a_inner, a_side, chunks), p.z_out)
+
+    o_near = move(tied(unit_out, a_from_inner), p.z_pair)
+    o_inner = move(tied(unit_out, a_far), p.z_mid)
+    a_x_third = move(a_from_inner, p.x_end)
+    a_x_far = move(a_far, p.x_mid)
+    a_side_inner = move(tied(a_side, a_far), p.z_mid)
+    a_from_far = move(tied(a_far, a_from_inner), p.z_out)
+    o_side = move(tied(unit_out, a_side_near), p.x_all)
+    units = [[unit_in], [a_side], [a_near], [a_side_near]]
+    acc = qkv_group(CORES * join(0, 1) + p.core, chunks, units, None, None)
+
+    a_x_fourth = move(tied(a_from_far, acc, o_near, o_inner, o_side, a_x_third, a_x_far, a_side_inner), p.x_end)
+    o_far = move(tied(o_near, acc), p.z_mid)
+    o_from_inner = move(tied(o_inner, acc), p.z_out)
+    units = [[a_inner, a_from_inner], [a_side_inner, a_x_third]]
+    acc = qkv_group(CORES * join(2) + p.core, chunks, units, acc, None)
+
+    o_x_third = move(tied(o_from_inner, a_x_fourth, acc), p.x_end)
+    o_x_near = move(tied(o_near, a_x_far, acc), p.x_mid)
+    o_from_far = move(tied(o_far, a_x_fourth, acc), p.z_out)
+    o_side_inner = move(tied(o_side, o_far, acc), p.z_mid)
+    units = [[a_far, a_from_far], [a_x_far, a_x_fourth]]
+    qkv = qkv_group(CORES * join(3) + p.core, chunks, units, acc, tables)
+
+    o_x_far = move(tied(o_far, o_x_near, qkv), p.x_mid)
+    o_x_fourth = move(tied(o_from_far, o_x_third, qkv), p.x_end)
+    o_z_side = move(tied(o_side, o_from_far, qkv), p.z_out)
+    own_kv = qkv[:, QH * HD // CORES :]
+    mate_kv = move(tied(own_kv, o_x_third, o_x_near, o_from_far, o_side_inner), p.mate)
+    halo = jnp.concatenate([own_kv, mate_kv], axis=1)[chip_rows - WINDOW :]
+    halo = move(halo, p.line)
+    attended = attend(core, qkv, own_kv, mate_kv, None, seg_q, seg_keys, None)
+    attended = attend(core, qkv, own_kv, mate_kv, halo, seg_q, seg_keys, attended)
+    attended = attended.reshape(shards // CORES, -1, chip_rows)
+
+    units = [[unit_out], [o_side], [o_near], [o_x_near, o_z_side]]
+    units += [[o_inner, o_from_inner], [o_side_inner, o_x_third]]
+    units += [[o_far, o_from_far], [o_x_far, o_x_fourth]]
+    order = join(0, 1, 2, 3)
+    mate = project(jnp.concatenate([order, 1 - core]), attended, units, jnp.bfloat16)
+    own = project(jnp.concatenate([order, core]), attended, units, jnp.float32)
+    updated, verdict = close(own, move(mate, p.mate), hidden_t, gains, judge_t)
+
+    members = lax.axis_size("member")
+    summed = verdict.astype(jnp.float32)
+    for step in range(1, members):
+        ring = [(i, (i + step) % members) for i in range(members)]
+        summed = summed + lax.ppermute(verdict, "member", ring).astype(jnp.float32)
+    return updated.T[None], summed / members
+
+
 def solution(mesh):
+    across = mesh.shape["member"]
+    planned = across == 2 and mesh.shape["seq"] == 4 * across * CORES
     return jax.shard_map(
-        body,
+        planned_body if planned else gathered_body,
         mesh=mesh,
         in_specs=(
             P("member", "seq", None),

time: 374 us -> 211 us (0.56)
  waiting for transfers between devices: 213 us -> 74.3 us
  Pallas kernels: 0 us -> 73.2 us
  local copies, waits for them, and re-layouts: 72.8 us -> 13.7 us
  matrix products: 53 us -> 0 us
  starting transfers between devices: 3.43 us -> 41.9 us
  between operations: 14 us -> 1.09 us
  other arithmetic: 10.8 us -> 3.23 us
  loops' own time: 5.3 us -> 0 us
    all_gather x4 -> x0, waiting for transfers between devices: 191 us -> none  [the longest x1 117 us: body(): lax.all_gather(w_query[0], 'seq', axis=0, tiled=True)]
    ppermute x1 -> x29, waiting for transfers between devices: 0.01 us -> 74.3 us  [the longest x28 70.7 us: move(): return lax.ppermute(block, 'seq', route)]
    pallas_call x0 -> x10, Pallas kernels: none -> 73.2 us  [the longest x3 28.3 us: qkv_group(): call(functools.partial(qkv_kernel, [len(unit) for unit in units], first,...]
    dot_general x13 -> x0, matrix products: 53 us -> none  [the longest x4 12 us: one_head(): jnp.einsum('qgd,kd->gqk', query_head, key_head, preferred_element_type=jn...]
    dot_general x1 -> x0, local copies, waits for them, and re-layouts: 50.9 us -> none  [body(): jnp.dot(normed, lax.all_gather(w_query[0], 'seq', axis=0, tiled=True), pr...]
    ppermute x1 -> x29, starting transfers between devices: 3.23 us -> 41.9 us  [the longest x28 40.4 us: move(): return lax.ppermute(block, 'seq', route)]
    psum x1 -> x0, waiting for transfers between devices: 21.3 us -> none  [body(): lax.psum(verdict.astype(jnp.bfloat16), 'member').astype(jnp.float32)]
    dynamic_slice x9 -> x1, local copies, waits for them, and re-layouts: 7.29 us -> 0.78 us  [planned_body(): seg_own = lax.dynamic_slice_in_dim(segments, row_first, chip_rows, 0)]
  transfers between devices with their start and end apart: 6 -> 29, of which waited for: 4 -> 9; matrix products, arithmetic and copies ran while one was open for 31% -> 3% of each run, Pallas kernels for 0% -> 28%
where the time goes in v2:
time: 211 us; the launch traced here: 207 us
  waiting for transfers between devices  74.3 us (35%)
  Pallas kernels  73.2 us (35%)
  starting transfers between devices  41.9 us (20%)
  local copies, waits for them, and re-layouts  13.7 us (6%)
  other arithmetic  3.23 us (2%)
    ppermute x28, waiting for transfers between devices, move(): return lax.ppermute(block, 'seq', route)  70.7 us
    ppermute x28, starting transfers between devices, move(): return lax.ppermute(block, 'seq', route)  40.4 us
    pallas_call x3, Pallas kernels, qkv_group(): call(functools.partial(qkv_kernel, [len(unit) for unit in units], first,...  28.3 us
    pallas_call x2, Pallas kernels, project(): call(functools.partial(out_kernel, [len(unit) for unit in units]), jax.Sh...  19 us
    pallas_call x2, Pallas kernels, attend(): call(attend_kernel, jax.ShapeDtypeStruct((q_wide, rows), jnp.bfloat16), f...  11.4 us
    unnamed x38, local copies, waits for them, and re-layouts  11 us
    pallas_call x1, Pallas kernels, prepare(): call(prepare_kernel, jax.ShapeDtypeStruct((count, CORES * rows, depth), j...  7.5 us
    pallas_call x1, Pallas kernels, close(): call(close_kernel, (jax.ShapeDtypeStruct((width, half), jnp.bfloat16), ja...  6.92 us
  transfers between devices with their start and end apart: 29, of which 9 were waited for; matrix products, arithmetic and copies ran while one was open for 3% of the time, Pallas kernels for 28%

profile of v2, /device:TPU:0, one launch (start us, length us, event | category | flops | bytes accessed | tf_op | source)
XLA Modules:
  0.0 207.4 jit_solution(1952384552255163653)
XLA Ops:
  0.7 1.1 copy-done.11
  4.3 1.4 collective-permute-done
  6.2 2.7 %collective-permute-start.2 = (bf16[180,2560]{1,0:T(8,128)(2,1)S(1)}, bf16[180,2560]{1,0:T(8,128)(2,1)}, u32[]{:S(2)}, u32[]{:S(2)}) collective-permute-start(bf16[180,2560]{1,0:T(8,128)(2,1)S(1)} %constant_dynamic-update-slice_fusion.refs_8_.refs_9_), channel_id=1, source_target_pairs={{0,4},{1,5},{2,6},{3,7},{4,0},{5,1},{6,2},{7,3},{8,12},{9,13},{10,... | collective-permute-start | bytes 2764808 | tf_op jit(solution)/shard_map/ppermute | solution.py:496
  8.9 1.5 collective-permute-start.3
  10.4 1.6 collective-permute-start.5
  14.2 1.2 copy.26
  15.4 1.5 fusion
  16.9 7.5 %shard_map.114.refs_0_.refs_1_.refs_2_.refs_3_.refs_4_.refs_5_.refs_6_.refs_7_ = bf16[16,768,180]{2,1,0:T(8,128)(2,1)} custom-call(s32[1]{0:T(128)} %bitcast.8.core_ref, bf16[2880,384]{1,0:T(8,128)(2,1)} %bitcast.10.own_ref.hidden_ref, bf16[2880,384]{1,0:T(8,128)(2,1)} %collective-permute-done.1.mate_ref, f32[2880,1]{1,0:T(8,128)S(1)} %bitcast.43), custom_call_target="tpu_custom_call" | custom-call | flops 1000 | bytes 1000 | tf_op jit(solution)/shard_map/pallas_call | solution.py:232
  24.4 7.5 %collective-permute-done.3.refs_10_.refs_11_ = bf16[180,2560]{1,0:T(8,128)(2,1)} collective-permute-done((bf16[180,2560]{1,0:T(8,128)(2,1)S(1)}, bf16[180,2560]{1,0:T(8,128)(2,1)}, u32[]{:S(2)}, u32[]{:S(2)}) %collective-permute-start.3) | collective-permute-done | bytes 921632 | tf_op jit(solution)/shard_map/ppermute | solution.py:496
  31.9 1.3 collective-permute-start.6
  33.2 1.6 collective-permute-start.4
  34.8 1.5 collective-permute-start.9
  36.3 22.0 %collective-permute-done.6.refs_6_.refs_7_ = bf16[180,2560]{1,0:T(8,128)(2,1)} collective-permute-done((bf16[180,2560]{1,0:T(8,128)(2,1)}, bf16[180,2560]{1,0:T(8,128)(2,1)}, u32[]{:S(2)}, u32[]{:S(2)}) %collective-permute-start.6) | collective-permute-done | bytes 921632 | tf_op jit(solution)/shard_map/ppermute | solution.py:496
  58.3 1.5 collective-permute-start.11
  59.8 1.6 collective-permute-start.14
  61.4 1.3 collective-permute-start.7
  63.6 2.4 %collective-permute-start.13 = (bf16[180,2560]{1,0:T(8,128)(2,1)}, bf16[180,2560]{1,0:T(8,128)(2,1)}, u32[]{:S(2)}, u32[]{:S(2)}) collective-permute-start(bf16[180,2560]{1,0:T(8,128)(2,1)} %collective-permute-done.6.refs_6_.refs_7_), channel_id=1, source_target_pairs={{0,2},{1,3},{2,0},{3,1},{12,14},{13,15},{14,12},{15,13},{16,18},{1... | collective-permute-start | bytes 2764808 | tf_op jit(solution)/shard_map/ppermute | solution.py:496
  66.1 11.9 %collective-permute-done.10.refs_10_ = bf16[2880,128]{1,0:T(8,128)(2,1)} collective-permute-done((bf16[2880,128]{1,0:T(8,128)(2,1)}, bf16[2880,128]{1,0:T(8,128)(2,1)}, u32[]{:S(2)}, u32[]{:S(2)}) %collective-permute-start.10) | collective-permute-done | bytes 737312 | tf_op jit(solution)/shard_map/ppermute | solution.py:496
  78.0 1.6 collective-permute-start.8
  80.2 1.2 copy-done.6
  81.4 9.2 %shard_map.115.refs_12_ = f32[768,1280]{1,0:T(8,128)} custom-call(s32[4]{0:T(128)S(1)} %fusion.5._, bf16[16,768,180]{2,1,0:T(8,128)(2,1)} %shard_map.114.refs_0_.refs_1_.refs_2_.refs_3_.refs_4_.refs_5_.refs_6_.refs_7_, bf16[16,768,180]{2,1,0:T(8,128)(2,1)} %shard_map.114.refs_0_.refs_1_.refs_2_.refs_3_.refs_4_.refs_5_.refs_6_.refs_7_, ...), custom_call_target="tpu_custom_call" | custom-call | flops 1000 | bytes 1000 | tf_op jit(solution)/shard_map/pallas_call | solution.py:322
  90.6 12.4 %collective-permute-done.12.refs_9_ = bf16[2880,128]{1,0:T(8,128)(2,1)} collective-permute-done((bf16[2880,128]{1,0:T(8,128)(2,1)}, bf16[2880,128]{1,0:T(8,128)(2,1)}, u32[]{:S(2)}, u32[]{:S(2)}) %collective-permute-start.12) | collective-permute-done | bytes 737312 | tf_op jit(solution)/shard_map/ppermute | solution.py:496
  103.0 2.4 %collective-permute-start.15 = (bf16[180,2560]{1,0:T(8,128)(2,1)}, bf16[180,2560]{1,0:T(8,128)(2,1)}, u32[]{:S(2)}, u32[]{:S(2)}) collective-permute-start(bf16[180,2560]{1,0:T(8,128)(2,1)} %collective-permute-done.7.refs_6_.refs_7_), channel_id=1, source_target_pairs={{0,2},{1,3},{2,0},{3,1},{12,14},{13,15},{14,12},{15,13},{16,18},{1... | collective-permute-start | bytes 2764808 | tf_op jit(solution)/shard_map/ppermute | solution.py:496
  105.5 1.5 collective-permute-start.19
  107.0 1.3 collective-permute-start.16
  108.4 9.4 %shard_map.116.refs_12_ = f32[768,1280]{1,0:T(8,128)} custom-call(s32[2]{0:T(128)S(1)} %fusion.6._, bf16[16,768,180]{2,1,0:T(8,128)(2,1)} %shard_map.114.refs_0_.refs_1_.refs_2_.refs_3_.refs_4_.refs_5_.refs_6_.refs_7_, bf16[16,768,180]{2,1,0:T(8,128)(2,1)} %shard_map.114.refs_0_.refs_1_.refs_2_.refs_3_.refs_4_.refs_5_.refs_6_.refs_7_, ...), custom_call_target="tpu_custom_call" | custom-call | flops 1000 | bytes 1000 | tf_op jit(solution)/shard_map/pallas_call | solution.py:322
  118.6 7.1 %collective-permute-done.15.refs_10_.refs_11_ = bf16[180,2560]{1,0:T(8,128)(2,1)} collective-permute-done((bf16[180,2560]{1,0:T(8,128)(2,1)}, bf16[180,2560]{1,0:T(8,128)(2,1)}, u32[]{:S(2)}, u32[]{:S(2)}) %collective-permute-start.15) | collective-permute-done | bytes 921632 | tf_op jit(solution)/shard_map/ppermute | solution.py:496
  125.7 1.3 collective-permute-start.20
  127.0 6.5 %collective-permute-done.16.refs_14_ = bf16[2880,128]{1,0:T(8,128)(2,1)} collective-permute-done((bf16[2880,128]{1,0:T(8,128)(2,1)}, bf16[2880,128]{1,0:T(8,128)(2,1)}, u32[]{:S(2)}, u32[]{:S(2)}) %collective-permute-start.16) | collective-permute-done | bytes 737312 | tf_op jit(solution)/shard_map/ppermute | solution.py:496
  133.5 1.9 collective-permute-start.17
  135.4 1.6 collective-permute-start.21
  137.1 9.7 %shard_map.117.q_ref = bf16[768,1280]{1,0:T(8,128)(2,1)} custom-call(s32[2]{0:T(128)S(1)} %fusion.4._, bf16[16,768,180]{2,1,0:T(8,128)(2,1)} %shard_map.114.refs_0_.refs_1_.refs_2_.refs_3_.refs_4_.refs_5_.refs_6_.refs_7_, bf16[16,768,180]{2,1,0:T(8,128)(2,1)} %shard_map.114.refs_0_.refs_1_.refs_2_.refs_3_.refs_4_.refs_5_.refs_6_.refs_7_, ...), custom_call_target="tpu_custom_call" | custom-call | flops 1000 | bytes 1000 | tf_op jit(solution)/shard_map/pallas_call | solution.py:322
  146.8 1.5 collective-permute-start.25
  148.3 3.9 %collective-permute-start.26 = (bf16[2880,128]{1,0:T(8,128)(2,1)}, bf16[2880,128]{1,0:T(8,128)(2,1)}, u32[]{:S(2)}, u32[]{:S(2)}) collective-permute-start(bf16[2880,128]{1,0:T(8,128)(2,1)} %collective-permute-done.20.refs_18_), channel_id=1, source_target_pairs={{0,2},{1,3},{2,0},{3,1},{12,14},{13,15},{14,12},{15,13},{16,18},{1... | collective-permute-start | bytes 2211848 | tf_op jit(solution)/shard_map/ppermute | solution.py:496
  152.2 1.3 collective-permute-start.24
  153.5 1.0 slice.13.own0_ref.own1_ref
  154.7 1.7 collective-permute-done.22.mate0_ref.mate1_ref
  157.9 2.5 %collective-permute-start.23 = (bf16[128,512]{1,0:T(8,128)(2,1)S(1)}, bf16[128,512]{1,0:T(8,128)(2,1)}, u32[]{:S(2)}, u32[]{:S(2)}) collective-permute-start(bf16[128,512]{1,0:T(8,128)(2,1)S(1)} %pad_maximum_fusion), channel_id=1, source_target_pairs={{0,2},{1,3},{2,4},{3,5},{4,6},{5,7},{6,8},{7,9},{8,10},{9,11},{10,... | collective-permute-start | bytes 393224 | tf_op jit(solution)/shard_map/ppermute | solution.py:496
  160.7 1.0 copy-done.2
  161.7 1.0 copy-done.4
  162.7 8.8 %shard_map.118.out_refs_0_ = bf16[1024,768]{1,0:T(8,128)(2,1)S(1)} custom-call(s32[1]{0:T(128)} %bitcast.8.core_ref, bf16[768,1280]{1,0:T(8,128)(2,1)} %shard_map.117.q_ref, bf16[768,256]{1,0:T(8,128)(2,1)S(1)} %copy-done.2, bf16[768,256]{1,0:T(8,128)(2,1)S(1)} %copy-done.2, bf16[768,256]{1,0:T(8,128)(2,1)S(1)} %copy-done.4, bf16[768,256]{1,0:T(8,128)(2,1)S(1)} %copy-done.4, ...), custom_call_target="tpu_custom_call" | custom-call | flops 1000 | bytes 1000 | tf_op jit(solution)/shard_map/pallas_call | solution.py:402
  171.6 2.6 %shard_map.119 = bf16[1024,768]{1,0:T(8,128)(2,1)S(1)} custom-call(s32[1]{0:T(128)} %bitcast.8.core_ref, bf16[768,1280]{1,0:T(8,128)(2,1)} %shard_map.117.q_ref, bf16[128,512]{1,0:T(8,128)(2,1)} %collective-permute-done.23.own0_ref.mate0_ref, bf16[768,256]{1,0:T(8,128)(2,1)S(1)} %copy-done.2, ...), custom_call_target="tpu_custom_call", output_to_operand_aliasing={{}: (9, {})} | custom-call | flops 1000 | bytes 1000 | tf_op jit(solution)/shard_map/pallas_call | solution.py:402
  174.1 1.2 copy-done
  175.4 9.0 %shard_map.121 = bf16[2880,384]{1,0:T(8,128)(2,1)} custom-call(s32[9]{0:T(128)S(1)} %concatenate.32._, bf16[8,128,768]{2,1,0:T(8,128)(2,1)} %bitcast.27, bf16[8,128,768]{2,1,0:T(8,128)(2,1)} %bitcast.28, bf16[8,128,768]{2,1,0:T(8,128)(2,1)} %bitcast.29, bf16[8,128,768]{2,1,0:T(8,128)(2,1)} %bitcast.30, bf16[8,128,768]{2,1,0:T(8,128)(2,1)} %bitcast.31, ...), custom_call_target="tpu_custom_call" | custom-call | flops 1000 | bytes 1000 | tf_op jit(solution)/shard_map/pallas_call | solution.py:442
  184.6 10.0 %shard_map.120.own_ref = f32[2880,384]{1,0:T(8,128)} custom-call(s32[9]{0:T(128)S(1)} %concatenate.26._, bf16[8,128,768]{2,1,0:T(8,128)(2,1)} %bitcast.35, bf16[8,128,768]{2,1,0:T(8,128)(2,1)} %bitcast.36, bf16[8,128,768]{2,1,0:T(8,128)(2,1)} %bitcast.37, bf16[8,128,768]{2,1,0:T(8,128)(2,1)} %bitcast.38, bf16[8,128,768]{2,1,0:T(8,128)(2,1)} %bitcast.39, ...), custom_call_target="tpu_custom_call" | custom-call | flops 1000 | bytes 1000 | tf_op jit(solution)/shard_map/pallas_call | solution.py:442
  194.6 6.9 %shard_map.122 = (bf16[2880,384]{1,0:T(8,128)(2,1)}, bf16[384,128]{1,0:T(8,128)(2,1)S(1)}) custom-call(f32[2880,384]{1,0:T(8,128)} %shard_map.120.own_ref, bf16[2880,384]{1,0:T(8,128)(2,1)} %collective-permute-done.27.mate_ref, bf16[2880,384]{1,0:T(8,128)(2,1)} %bitcast.10.own_ref.hidden_ref, f32[2880,3]{1,0:T(8,128)S(1)} %bitcast.44, ...), custom_call_target="tpu_custom_call" | custom-call | flops 1000 | bytes 1000 | tf_op jit(solution)/shard_map/pallas_call | solution.py:482
  201.5 1.5 collective-permute-start.28
  203.0 3.7 %collective-permute-done.28 = bf16[384,128]{1,0:T(8,128)(2,1)S(1)} collective-permute-done((bf16[384,128]{1,0:T(8,128)(2,1)S(1)}, bf16[384,128]{1,0:T(8,128)(2,1)S(1)}, u32[]{:S(2)}, u32[]{:S(2)}) %collective-permute-start.28) | collective-permute-done | bytes 98336 | tf_op jit(solution)/shard_map/ppermute | solution.py:618
  (78 shorter events, 10.3 us)
Async XLA Ops:
  0.6 11.4 %copy-start.16 = (f32[1,2880]{1,0:T(1,128)S(1)}, f32[1,2880]{1,0:T(1,128)}, u32[]{:S(2)}) copy-start(f32[1,2880]{1,0:T(1,128)} %param.17) | copy-start | bytes 34564
  0.6 11.4 %copy-start.15 = (f32[1,2880]{1,0:T(1,128)S(1)}, f32[1,2880]{1,0:T(1,128)}, u32[]{:S(2)}) copy-start(f32[1,2880]{1,0:T(1,128)} %param.18) | copy-start | bytes 34564
  0.7 1.1 copy-start.11
  1.8 0.9 copy-start.12
  2.7 0.9 copy-start.13
  3.6 8.5 %copy-start.17 = (f32[1,2880]{1,0:T(1,128)S(1)}, f32[1,2880]{1,0:T(1,128)}, u32[]{:S(2)}) copy-start(f32[1,2880]{1,0:T(1,128)} %param.12) | copy-start | bytes 34564
  3.6 10.6 %copy-start.14 = (bf16[1,2880,128]{2,1,0:T(8,128)(2,1)S(1)}, bf16[1,2880,128]{2,1,0:T(8,128)(2,1)}, u32[]{:S(2)}) copy-start(bf16[1,2880,128]{2,1,0:T(8,128)(2,1)} %param.19) | copy-start | bytes 2211844
  3.8 2.0 collective-permute-start
  5.8 11.1 %collective-permute-start.1 = (bf16[2880,384]{1,0:T(8,128)(2,1)}, bf16[2880,384]{1,0:T(8,128)(2,1)}, u32[]{:S(2)}, u32[]{:S(2)}) collective-permute-start(bf16[2880,384]{1,0:T(8,128)(2,1)} %bitcast.10.own_ref.hidden_ref), channel_id=1, source_target_pairs={{0,1},{1,0},{2,3},{3,2},{4,5},{5,4},{6,7},{7,6},{8,9},{9,8},{10,11... | collective-permute-start | bytes 6635528 | tf_op jit(solution)/shard_map/ppermute | solution.py:496
  6.2 27.0 %collective-permute-start.2 = (bf16[180,2560]{1,0:T(8,128)(2,1)S(1)}, bf16[180,2560]{1,0:T(8,128)(2,1)}, u32[]{:S(2)}, u32[]{:S(2)}) collective-permute-start(bf16[180,2560]{1,0:T(8,128)(2,1)S(1)} %constant_dynamic-update-slice_fusion.refs_8_.refs_9_), channel_id=1, source_target_pairs={{0,4},{1,5},{2,6},{3,7},{4,0},{5,1},{6,2},{7,3},{8,12},{9,13},{10,... | collective-permute-start | bytes 2764808 | tf_op jit(solution)/shard_map/ppermute | solution.py:496
  8.9 23.0 %collective-permute-start.3 = (bf16[180,2560]{1,0:T(8,128)(2,1)S(1)}, bf16[180,2560]{1,0:T(8,128)(2,1)}, u32[]{:S(2)}, u32[]{:S(2)}) collective-permute-start(bf16[180,2560]{1,0:T(8,128)(2,1)S(1)} %constant_dynamic-update-slice_fusion.refs_8_.refs_9_), channel_id=1, source_target_pairs={{0,2},{1,3},{2,0},{3,1},{4,6},{5,7},{6,4},{7,5},{8,10},{9,11},{10,... | collective-permute-start | bytes 2764808 | tf_op jit(solution)/shard_map/ppermute | solution.py:496
  10.4 21.5 %collective-permute-start.5 = (bf16[180,2560]{1,0:T(8,128)(2,1)S(1)}, bf16[180,2560]{1,0:T(8,128)(2,1)}, u32[]{:S(2)}, u32[]{:S(2)}) collective-permute-start(bf16[180,2560]{1,0:T(8,128)(2,1)S(1)} %constant_dynamic-update-slice_fusion.refs_8_.refs_9_), channel_id=1, source_target_pairs={{4,8},{5,9},{6,10},{7,11},{8,4},{9,5},{10,6},{11,7},{20,24},{21,25... | collective-permute-start | bytes 2764808 | tf_op jit(solution)/shard_map/ppermute | solution.py:496
  31.9 26.4 %collective-permute-start.6 = (bf16[180,2560]{1,0:T(8,128)(2,1)}, bf16[180,2560]{1,0:T(8,128)(2,1)}, u32[]{:S(2)}, u32[]{:S(2)}) collective-permute-start(bf16[180,2560]{1,0:T(8,128)(2,1)} %collective-permute-done.5.refs_4_.refs_5_), channel_id=1, source_target_pairs={{4,0},{5,1},{6,2},{7,3},{8,12},{9,13},{10,14},{11,15},{20,16},{21,... | collective-permute-start | bytes 2764808 | tf_op jit(solution)/shard_map/ppermute | solution.py:496
  33.2 25.1 %collective-permute-start.4 = (bf16[180,2560]{1,0:T(8,128)(2,1)}, bf16[180,2560]{1,0:T(8,128)(2,1)}, u32[]{:S(2)}, u32[]{:S(2)}) collective-permute-start(bf16[180,2560]{1,0:T(8,128)(2,1)} %collective-permute-done.2.refs_12_.refs_13_), channel_id=1, source_target_pairs={{4,8},{5,9},{6,10},{7,11},{8,4},{9,5},{10,6},{11,7},{20,24},{21,25... | collective-permute-start | bytes 2764808 | tf_op jit(solution)/shard_map/ppermute | solution.py:496
  34.8 27.9 %collective-permute-start.9 = (bf16[180,2560]{1,0:T(8,128)(2,1)}, bf16[180,2560]{1,0:T(8,128)(2,1)S(1)}, u32[]{:S(2)}, u32[]{:S(2)}) collective-permute-start(bf16[180,2560]{1,0:T(8,128)(2,1)} %collective-permute-done.2.refs_12_.refs_13_), channel_id=1, source_target_pairs={{0,2},{1,3},{2,0},{3,1},{4,6},{5,7},{6,4},{7,5},{8,10},{9,11},{10,... | collective-permute-start | bytes 2764808 | tf_op jit(solution)/shard_map/ppermute | solution.py:496
  58.3 19.7 %collective-permute-start.10 = (bf16[2880,128]{1,0:T(8,128)(2,1)}, bf16[2880,128]{1,0:T(8,128)(2,1)}, u32[]{:S(2)}, u32[]{:S(2)}) collective-permute-start(bf16[2880,128]{1,0:T(8,128)(2,1)} %bitcast.19.refs_8_), channel_id=1, source_target_pairs={{0,4},{1,5},{2,6},{3,7},{4,0},{5,1},{6,2},{7,3},{8,12},{9,13},{10,... | collective-permute-start | bytes 2211848 | tf_op jit(solution)/shard_map/ppermute | solution.py:496
  58.3 21.4 %collective-permute-start.11 = (bf16[2880,128]{1,0:T(8,128)(2,1)}, bf16[2880,128]{1,0:T(8,128)(2,1)}, u32[]{:S(2)}, u32[]{:S(2)}) collective-permute-start(bf16[2880,128]{1,0:T(8,128)(2,1)} %bitcast.19.refs_8_), channel_id=1, source_target_pairs={{4,8},{5,9},{6,10},{7,11},{8,4},{9,5},{10,6},{11,7},{20,24},{21,25... | collective-permute-start | bytes 2211848 | tf_op jit(solution)/shard_map/ppermute | solution.py:496
  59.8 43.2 %collective-permute-start.14 = (bf16[180,2560]{1,0:T(8,128)(2,1)}, bf16[180,2560]{1,0:T(8,128)(2,1)}, u32[]{:S(2)}, u32[]{:S(2)}) collective-permute-start(bf16[180,2560]{1,0:T(8,128)(2,1)} %collective-permute-done.3.refs_10_.refs_11_), channel_id=1, source_target_pairs={{4,8},{5,9},{6,10},{7,11},{8,4},{9,5},{10,6},{11,7},{20,24},{21,25... | collective-permute-start | bytes 2764808 | tf_op jit(solution)/shard_map/ppermute | solution.py:496
  61.4 41.6 %collective-permute-start.7 = (bf16[180,2560]{1,0:T(8,128)(2,1)}, bf16[180,2560]{1,0:T(8,128)(2,1)}, u32[]{:S(2)}, u32[]{:S(2)}) collective-permute-start(bf16[180,2560]{1,0:T(8,128)(2,1)} %collective-permute-done.4.refs_4_.refs_5_), channel_id=1, source_target_pairs={{4,0},{5,1},{6,2},{7,3},{8,12},{9,13},{10,14},{11,15},{20,16},{21,... | collective-permute-start | bytes 2764808 | tf_op jit(solution)/shard_map/ppermute | solution.py:496
  62.7 0.9 copy-start.5
  63.6 39.4 %collective-permute-start.13 = (bf16[180,2560]{1,0:T(8,128)(2,1)}, bf16[180,2560]{1,0:T(8,128)(2,1)}, u32[]{:S(2)}, u32[]{:S(2)}) collective-permute-start(bf16[180,2560]{1,0:T(8,128)(2,1)} %collective-permute-done.6.refs_6_.refs_7_), channel_id=1, source_target_pairs={{0,2},{1,3},{2,0},{3,1},{12,14},{13,15},{14,12},{15,13},{16,18},{1... | collective-permute-start | bytes 2764808 | tf_op jit(solution)/shard_map/ppermute | solution.py:496
  78.0 25.0 %collective-permute-start.8 = (bf16[180,2560]{1,0:T(8,128)(2,1)}, bf16[180,2560]{1,0:T(8,128)(2,1)}, u32[]{:S(2)}, u32[]{:S(2)}) collective-permute-start(bf16[180,2560]{1,0:T(8,128)(2,1)} %collective-permute-done.4.refs_4_.refs_5_), channel_id=1, source_target_pairs={{4,6},{5,7},{6,4},{7,5},{8,10},{9,11},{10,8},{11,9},{20,22},{21,23... | collective-permute-start | bytes 2764808 | tf_op jit(solution)/shard_map/ppermute | solution.py:496
  79.6 23.4 %collective-permute-start.12 = (bf16[2880,128]{1,0:T(8,128)(2,1)}, bf16[2880,128]{1,0:T(8,128)(2,1)}, u32[]{:S(2)}, u32[]{:S(2)}) collective-permute-start(bf16[2880,128]{1,0:T(8,128)(2,1)} %bitcast.19.refs_8_), channel_id=1, source_target_pairs={{0,2},{1,3},{2,0},{3,1},{4,6},{5,7},{6,4},{7,5},{8,10},{9,11},{10,... | collective-permute-start | bytes 2211848 | tf_op jit(solution)/shard_map/ppermute | solution.py:496
  80.2 1.2 copy-start.6
  103.0 22.7 %collective-permute-start.15 = (bf16[180,2560]{1,0:T(8,128)(2,1)}, bf16[180,2560]{1,0:T(8,128)(2,1)}, u32[]{:S(2)}, u32[]{:S(2)}) collective-permute-start(bf16[180,2560]{1,0:T(8,128)(2,1)} %collective-permute-done.7.refs_6_.refs_7_), channel_id=1, source_target_pairs={{0,2},{1,3},{2,0},{3,1},{12,14},{13,15},{14,12},{15,13},{16,18},{1... | collective-permute-start | bytes 2764808 | tf_op jit(solution)/shard_map/ppermute | solution.py:496
  105.5 13.1 %collective-permute-start.19 = (bf16[2880,128]{1,0:T(8,128)(2,1)}, bf16[2880,128]{1,0:T(8,128)(2,1)}, u32[]{:S(2)}, u32[]{:S(2)}) collective-permute-start(bf16[2880,128]{1,0:T(8,128)(2,1)} %collective-permute-done.10.refs_10_), channel_id=1, source_target_pairs={{4,8},{5,9},{6,10},{7,11},{8,4},{9,5},{10,6},{11,7},{20,24},{21,25... | collective-permute-start | bytes 2211848 | tf_op jit(solution)/shard_map/ppermute | solution.py:496
  107.0 26.5 %collective-permute-start.16 = (bf16[2880,128]{1,0:T(8,128)(2,1)}, bf16[2880,128]{1,0:T(8,128)(2,1)}, u32[]{:S(2)}, u32[]{:S(2)}) collective-permute-start(bf16[2880,128]{1,0:T(8,128)(2,1)} %collective-permute-done.11.refs_13_), channel_id=1, source_target_pairs={{4,0},{5,1},{6,2},{7,3},{8,12},{9,13},{10,14},{11,15},{20,16},{21,... | collective-permute-start | bytes 2211848 | tf_op jit(solution)/shard_map/ppermute | solution.py:496
  117.9 28.9 %collective-permute-start.18 = (bf16[2880,128]{1,0:T(8,128)(2,1)}, bf16[2880,128]{1,0:T(8,128)(2,1)S(1)}, u32[]{:S(2)}, u32[]{:S(2)}) collective-permute-start(bf16[2880,128]{1,0:T(8,128)(2,1)} %collective-permute-done.10.refs_10_), channel_id=1, source_target_pairs={{4,6},{5,7},{6,4},{7,5},{8,10},{9,11},{10,8},{11,9},{20,22},{21,23... | collective-permute-start | bytes 2211848 | tf_op jit(solution)/shard_map/ppermute | solution.py:496
  125.7 22.6 %collective-permute-start.20 = (bf16[2880,128]{1,0:T(8,128)(2,1)}, bf16[2880,128]{1,0:T(8,128)(2,1)}, u32[]{:S(2)}, u32[]{:S(2)}) collective-permute-start(bf16[2880,128]{1,0:T(8,128)(2,1)} %collective-permute-done.19.refs_17_), channel_id=1, source_target_pairs={{4,0},{5,1},{6,2},{7,3},{8,12},{9,13},{10,14},{11,15},{20,16},{21,... | collective-permute-start | bytes 2211848 | tf_op jit(solution)/shard_map/ppermute | solution.py:496
  133.5 14.8 %collective-permute-start.17 = (bf16[2880,128]{1,0:T(8,128)(2,1)}, bf16[2880,128]{1,0:T(8,128)(2,1)}, u32[]{:S(2)}, u32[]{:S(2)}) collective-permute-start(bf16[2880,128]{1,0:T(8,128)(2,1)} %collective-permute-done.16.refs_14_), channel_id=1, source_target_pairs={{0,2},{1,3},{2,0},{3,1},{12,14},{13,15},{14,12},{15,13},{16,18},{1... | collective-permute-start | bytes 2211848 | tf_op jit(solution)/shard_map/ppermute | solution.py:496
  135.4 19.1 %collective-permute-start.21 = (bf16[2880,128]{1,0:T(8,128)(2,1)}, bf16[2880,128]{1,0:T(8,128)(2,1)}, u32[]{:S(2)}, u32[]{:S(2)}) collective-permute-start(bf16[2880,128]{1,0:T(8,128)(2,1)} %collective-permute-done.12.refs_9_), channel_id=1, source_target_pairs={{4,8},{5,9},{6,10},{7,11},{8,4},{9,5},{10,6},{11,7},{20,24},{21,25... | collective-permute-start | bytes 2211848 | tf_op jit(solution)/shard_map/ppermute | solution.py:496
  146.8 13.8 %copy-start.8 = (bf16[2880,128]{1,0:T(8,128)(2,1)}, bf16[2880,128]{1,0:T(8,128)(2,1)S(1)}, u32[]{:S(2)}) copy-start(bf16[2880,128]{1,0:T(8,128)(2,1)S(1)} %collective-permute-done.18.refs_11_) | copy-start | bytes 2211844
  146.8 28.6 %collective-permute-start.25 = (bf16[2880,128]{1,0:T(8,128)(2,1)}, bf16[2880,128]{1,0:T(8,128)(2,1)}, u32[]{:S(2)}, u32[]{:S(2)}) collective-permute-start(bf16[2880,128]{1,0:T(8,128)(2,1)} %collective-permute-done.19.refs_17_), channel_id=1, source_target_pairs={{4,6},{5,7},{6,4},{7,5},{8,10},{9,11},{10,8},{11,9},{20,22},{21,23... | collective-permute-start | bytes 2211848 | tf_op jit(solution)/shard_map/ppermute | solution.py:496
  148.3 27.1 %collective-permute-start.26 = (bf16[2880,128]{1,0:T(8,128)(2,1)}, bf16[2880,128]{1,0:T(8,128)(2,1)}, u32[]{:S(2)}, u32[]{:S(2)}) collective-permute-start(bf16[2880,128]{1,0:T(8,128)(2,1)} %collective-permute-done.20.refs_18_), channel_id=1, source_target_pairs={{0,2},{1,3},{2,0},{3,1},{12,14},{13,15},{14,12},{15,13},{16,18},{1... | collective-permute-start | bytes 2211848 | tf_op jit(solution)/shard_map/ppermute | solution.py:496
  152.2 23.1 %collective-permute-start.24 = (bf16[2880,128]{1,0:T(8,128)(2,1)}, bf16[2880,128]{1,0:T(8,128)(2,1)}, u32[]{:S(2)}, u32[]{:S(2)}) collective-permute-start(bf16[2880,128]{1,0:T(8,128)(2,1)} %collective-permute-done.12.refs_9_), channel_id=1, source_target_pairs={{4,0},{5,1},{6,2},{7,3},{8,12},{9,13},{10,14},{11,15},{20,16},{21,... | collective-permute-start | bytes 2211848 | tf_op jit(solution)/shard_map/ppermute | solution.py:496
  154.6 1.8 collective-permute-start.22
  156.4 0.8 copy-start.3
  157.1 0.7 copy-start.1
  157.9 13.7 %collective-permute-start.23 = (bf16[128,512]{1,0:T(8,128)(2,1)S(1)}, bf16[128,512]{1,0:T(8,128)(2,1)}, u32[]{:S(2)}, u32[]{:S(2)}) collective-permute-start(bf16[128,512]{1,0:T(8,128)(2,1)S(1)} %pad_maximum_fusion), channel_id=1, source_target_pairs={{0,2},{1,3},{2,4},{3,5},{4,6},{5,7},{6,8},{7,9},{8,10},{9,11},{10,... | collective-permute-start | bytes 393224 | tf_op jit(solution)/shard_map/ppermute | solution.py:496
  160.7 1.0 copy-start.2
  161.7 1.0 copy-start.4
  171.5 3.9 %copy-start.9 = (bf16[2880,128]{1,0:T(8,128)(2,1)S(1)}, bf16[2880,128]{1,0:T(8,128)(2,1)}, u32[]{:S(2)}) copy-start(bf16[2880,128]{1,0:T(8,128)(2,1)} %copy-done.8) | copy-start | bytes 2211844
  174.1 1.3 copy-start
  175.4 9.2 %copy-start.10 = (bf16[2880,128]{1,0:T(8,128)(2,1)S(1)}, bf16[2880,128]{1,0:T(8,128)(2,1)}, u32[]{:S(2)}) copy-start(bf16[2880,128]{1,0:T(8,128)(2,1)} %copy-done.8) | copy-start | bytes 2211844
  184.4 10.2 %collective-permute-start.27 = (bf16[2880,384]{1,0:T(8,128)(2,1)}, bf16[2880,384]{1,0:T(8,128)(2,1)}, u32[]{:S(2)}, u32[]{:S(2)}) collective-permute-start(bf16[2880,384]{1,0:T(8,128)(2,1)} %shard_map.121), channel_id=1, source_target_pairs={{0,1},{1,0},{2,3},{3,2},{4,5},{5,4},{6,7},{7,6},{8,9},{9,8},{10,11... | collective-permute-start | bytes 6635528 | tf_op jit(solution)/shard_map/ppermute | solution.py:496
  184.6 10.0 %copy-start.7 = (bf16[1,2880,128]{1,2,0:T(8,128)(2,1)S(1)}, bf16[1,2880,128]{1,2,0:T(8,128)(2,1)}, u32[]{:S(2)}) copy-start(bf16[1,2880,128]{1,2,0:T(8,128)(2,1)} %copy.26) | copy-start | bytes 2211844
  201.5 5.2 %collective-permute-start.28 = (bf16[384,128]{1,0:T(8,128)(2,1)S(1)}, bf16[384,128]{1,0:T(8,128)(2,1)S(1)}, u32[]{:S(2)}, u32[]{:S(2)}) collective-permute-start(bf16[384,128]{1,0:T(8,128)(2,1)S(1)} %get-tuple-element.59), channel_id=1, source_target_pairs={{0,16},{16,0},{1,17},{17,1},{2,18},{18,2},{3,19},{19,3},{4,20},{20... | collective-permute-start | bytes 294920 | tf_op jit(solution)/shard_map/ppermute | solution.py:618

commit v3 on v2

--- a/solution.py
+++ b/solution.py
@@ -18,7 +18,7 @@
 epsilon = 1e-06
 softcap = 50.0
 rope_base = 10000.0
-VMEM_LIMIT = 50 * 1024 * 1024
+MIB = 1024 * 1024
 
 
 def from_behind(block, axis, distance):
@@ -153,16 +153,20 @@
     return lax.optimization_barrier((value, *others))[0]
 
 
-def call(kernel, out_shape, *, flops=0, moved=0, transcendentals=0, **spec):
+def call(kernel, out_shape, vmem, **spec):
     return pl.pallas_call(
         kernel,
         out_shape=out_shape,
-        compiler_params=pltpu.CompilerParams(vmem_limit_bytes=VMEM_LIMIT),
-        cost_estimate=pl.CostEstimate(
-            flops=1000, bytes_accessed=1000, transcendentals=0
-        ),
+        compiler_params=pltpu.CompilerParams(vmem_limit_bytes=vmem * MIB),
+        cost_estimate=pl.CostEstimate(flops=1000, bytes_accessed=1000, transcendentals=0),
         **spec,
     )
+
+
+def resident(count):
+    return [pl.BlockSpec(memory_space=pltpu.SMEM)] + [
+        pl.BlockSpec(memory_space=pltpu.VMEM)
+    ] * count
 
 
 def scalars(count, grid, in_specs, out_specs, scratch=()):
@@ -203,42 +207,50 @@
     half = jax.ShapeDtypeStruct((rows, wide), w_query.dtype)
     ins = (w_query, w_key, w_value)
     return call(
-        halves_kernel, (half, half), moved=8 * rows * wide,
+        halves_kernel, (half, half), 12,
         **scalars(1, (1,), [whole(a) for a in ins], (whole(half), whole(half))),
     )(core, *ins)
 
 
-def prepare_kernel(core_ref, own_ref, mate_ref, gain_ref, chunks_ref):
-    count, _, depth = chunks_ref.shape
-    own = pl.program_id(0) == core_ref[0]
-
-    def write(hidden_ref):
+def prepare_kernel(slots_ref, own_ref, mate_ref, gain_ref, *chunk_refs):
+    count = slots_ref.shape[0] - 1
+    width, rows = own_ref.shape
+    depth = width // count
+
+    def write(hidden_ref, half):
         values = hidden_ref[...].astype(jnp.float32)
-        mean = jnp.sum(values * values, axis=0, keepdims=True) * (1.0 / values.shape[0])
+        mean = jnp.sum(values * values, axis=0, keepdims=True) * (1.0 / width)
         scale = lax.rsqrt(mean + epsilon)
         for j in range(count):
             part = slice(j * depth, (j + 1) * depth)
             normed = hidden_ref[part, :].astype(jnp.float32) * scale * gain_ref[part, :]
-            chunks_ref[j] = normed.T.astype(jnp.bfloat16)
-
-    pl.when(own)(lambda: write(own_ref))
-    pl.when(jnp.logical_not(own))(lambda: write(mate_ref))
-
-
-def prepare(core, own, mate, gain, count):
+            normed = normed.T.astype(jnp.bfloat16)
+            slot = slots_ref[j]
+            low = 0
+            for ref in chunk_refs:
+                size = ref.shape[0]
+
+                @pl.when((slot >= low) & (slot < low + size))
+                def _(ref=ref, low=low):
+                    ref[slot - low, pl.ds(pl.multiple_of(half * rows, LANES), rows), :] = normed
+
+                low += size
+
+    core = slots_ref[count]
+    write(own_ref, core)
+    write(mate_ref, 1 - core)
+
+
+def prepare(slots, own, mate, gain, sizes):
     width, rows = own.shape
-    depth = width // count
-    whole = lambda array: pl.BlockSpec(array.shape, lambda m, c: (0, 0))
+    depth = width // (slots.shape[0] - 1)
     return call(
         prepare_kernel,
-        jax.ShapeDtypeStruct((count, CORES * rows, depth), jnp.bfloat16),
-        flops=10 * rows * width,
-        moved=10 * rows * width,
-        **scalars(
-            1, (CORES,), [whole(own), whole(mate), whole(gain)],
-            pl.BlockSpec((count, rows, depth), lambda m, c: (0, m, 0)),
-        ),
-    )(core, own, mate, gain)
+        [jax.ShapeDtypeStruct((n, CORES * rows, depth), jnp.bfloat16) for n in sizes],
+        14,
+        in_specs=resident(3),
+        out_specs=[pl.BlockSpec(memory_space=pltpu.VMEM)] * len(sizes),
+    )(slots, own, mate, gain)
 
 
 def rotated(block, cosine, sine):
@@ -250,82 +262,69 @@
     return block * cosine + other * sine
 
 
-def qkv_kernel(shape, first, last, _, *refs):
+def qkv_kernel(shape, first, last, chunks_ref, *refs):
     refs = list(refs)
     take = lambda: refs.pop(0)
-    x_refs = [[take() for _ in range(CORES)] for _ in shape]
-    total = None
-    w_refs = [[[take() for _ in range(CORES)] for _ in range(n)] for n in shape]
-    if not first:
-        total = take()[...]
-    for x_pair, parts in zip(x_refs, w_refs):
-        for side in range(CORES):
-            w = parts[0][side][...]
-            for extra in parts[1:]:
-                w = w + extra[side][...]
-            part = jnp.dot(x_pair[side][0], w, preferred_element_type=jnp.float32)
-            total = part if total is None else total + part
-    if not last:
-        take()[...] = total
-        return
-    cosine, sine = take()[...], take()[...]
+    units = [[take() for _ in range(n)] for n in shape]
+    acc_ref = None if first else take()
+    tables = (take(), take()) if last else None
     out_ref = take()
-    width = out_ref.shape[1]
-    lanes = lambda low: slice(low, low + LANES)
+    wide = out_ref.shape[1]
     keys = KVH * HD // CORES
-    is_query = pl.program_id(0) < pl.num_programs(0) - 1
-
-    @pl.when(is_query)
-    def _():
-        for low in range(0, width, LANES):
-            block = rotated(total[:, lanes(low)], cosine, sine) * (1.0 / math.sqrt(HD))
-            out_ref[:, lanes(low)] = block.astype(jnp.bfloat16)
-
-    @pl.when(jnp.logical_not(is_query))
-    def _():
-        for low in range(0, width, LANES):
-            block = total[:, lanes(low)]
-            if low < keys:
-                block = rotated(block, cosine, sine)
-            out_ref[:, lanes(low)] = block.astype(jnp.bfloat16)
-
-
-def qkv_group(indices, chunks, units, acc, tables):
-    _, rows, depth = chunks.shape
+    step = 2 * keys
+
+    def total_of(at):
+        total = None if first else acc_ref[:, pl.ds(at, step)]
+        for k, parts in enumerate(units):
+            for side in range(CORES):
+                cols = pl.ds(at + side * wide, step)
+                w = parts[0][:, cols]
+                for extra in parts[1:]:
+                    w = w + extra[:, cols]
+                x = chunks_ref[CORES * k + side]
+                part = jnp.dot(x, w, preferred_element_type=jnp.float32)
+                total = part if total is None else total + part
+        return total
+
+    def finish(at, total, rotate_to, scale):
+        for low in range(0, step, LANES):
+            block = total[:, low : low + LANES]
+            if low < rotate_to:
+                block = rotated(block, tables[0][...], tables[1][...])
+            if scale is not None:
+                block = block * scale
+            out_ref[:, pl.ds(at + low, LANES)] = block.astype(jnp.bfloat16)
+
+    whole = wide - step if last else wide
+
+    @pl.loop(0, whole // step)
+    def _(n):
+        at = pl.multiple_of(n * step, step)
+        if last:
+            finish(at, total_of(at), step, 1.0 / math.sqrt(HD))
+        else:
+            out_ref[:, pl.ds(at, step)] = total_of(at)
+
+    if last:
+        finish(whole, total_of(whole), keys, None)
+
+
+def qkv_group(chunks, units, acc, tables):
+    rows = chunks.shape[1]
     wide = units[0][0].shape[1] // CORES
-    step = 2 * KVH * HD // CORES
-    steps = wide // step
     first, last = acc is None, tables is not None
-    specs, operands = [], []
-    for k in range(len(units)):
-        for side in range(CORES):
-            specs.append(
-                pl.BlockSpec(
-                    (1, rows, depth), lambda n, ids, k=k, side=side: (ids[k] ^ side, 0, 0)
-                )
-            )
-            operands.append(chunks)
-    for unit in units:
-        for part in unit:
-            for side in range(CORES):
-                specs.append(
-                    pl.BlockSpec((depth, step), lambda n, ids, side=side: (0, n + side * steps))
-                )
-                operands.append(part)
-    block = pl.BlockSpec((rows, step), lambda n, ids: (0, n))
+    operands = [chunks] + [part for unit in units for part in unit]
     if not first:
         operands.append(acc)
-        specs.append(block)
     if last:
         operands += list(tables)
-        specs += [pl.BlockSpec((rows, LANES), lambda n, ids: (0, 0))] * 2
     return call(
         functools.partial(qkv_kernel, [len(unit) for unit in units], first, last),
         jax.ShapeDtypeStruct((rows, wide), jnp.bfloat16 if last else jnp.float32),
-        flops=2 * rows * depth * wide * len(units) * CORES,
-        moved=4 * len(units) * depth * wide + 8 * rows * wide,
-        **scalars(1, (steps,), specs, block),
-    )(indices, *operands)
+        12,
+        in_specs=resident(len(operands))[1:],
+        out_specs=pl.BlockSpec(memory_space=pltpu.VMEM),
+    )(*operands)
 
 
 def attend_kernel(core_ref, q_ref, own0_ref, own1_ref, mate0_ref, mate1_ref, seg_q_ref, seg0_ref, seg1_ref, *out_refs):
@@ -337,7 +336,8 @@
         + rows
         - lax.broadcasted_iota(jnp.int32, (count, rows), 0)
     )
-    seg_keys = jnp.concatenate([seg0_ref[...], seg1_ref[...]], axis=0)
+    seg_keys = jnp.concatenate([seg0_ref[...], seg1_ref[...]], axis=1)
+    seg_keys = jnp.broadcast_to(seg_keys, (rows, count)).T
     allowed = (distance >= 0) & (distance < WINDOW) & (seg_q_ref[...] == seg_keys)
     bias = jnp.where(allowed, 0.0, -1e9)
     own = jnp.concatenate([own0_ref[...], own1_ref[...]], axis=0).astype(jnp.float32)
@@ -378,7 +378,7 @@
     keys = lambda ahead, column: pl.BlockSpec(
         (WINDOW, kv_wide), lambda m, c: (m + ahead, column)
     )
-    segs = lambda ahead: pl.BlockSpec((WINDOW, 1), lambda m, c: (m + start + ahead, 0))
+    segs = lambda ahead: pl.BlockSpec((1, WINDOW), lambda m, c: (0, m + start + ahead))
     if prior is None:
         operands = [own, own, mate, mate]
         specs = [keys(0, 0), keys(1, 0), keys(0, 0), keys(1, 0)]
@@ -402,9 +402,7 @@
     return call(
         attend_kernel,
         jax.ShapeDtypeStruct((q_wide, rows), jnp.bfloat16),
-        flops=8 * steps * WINDOW * WINDOW * q_wide,
-        moved=4 * steps * WINDOW * q_wide,
-        transcendentals=4 * steps * WINDOW * WINDOW * QH // CORES,
+        12,
         input_output_aliases=aliases,
         **scalars(
             1, (steps,), specs, pl.BlockSpec((q_wide, WINDOW), lambda m, c: (0, m + start))
@@ -412,57 +410,70 @@
     )(core, *operands)
 
 
-def out_kernel(shape, _, *refs):
+def out_kernel(shape, first, last, ids_ref, attended_ref, *refs):
     refs = list(refs)
-    take = lambda: refs.pop(0)
-    x = jnp.concatenate([take()[0] for _ in shape], axis=0)
-    units = []
-    for n in shape:
-        w = take()[...]
-        for _ in range(n - 1):
-            w = w + take()[...]
-        units.append(w)
-    out_ref = take()
-    total = jnp.dot(jnp.concatenate(units, axis=1), x, preferred_element_type=jnp.float32)
-    out_ref[...] = total.astype(out_ref.dtype)
-
-
-def project(indices, attended, units, dtype):
-    _, depth, rows = attended.shape
+    units = [[refs.pop(0) for _ in range(n)] for n in shape]
+    acc_ref = None if first else refs.pop(0)
     wide = units[0][0].shape[0]
-    step, half, count = wide // 5, rows // CORES, len(units)
-    specs = [
-        pl.BlockSpec((1, depth, half), lambda m, ids, k=k: (ids[k], 0, ids[count]))
-        for k in range(count)
-    ]
-    operands = [attended] * count
-    for unit in units:
-        operands += unit
-        specs += [pl.BlockSpec((step, depth), lambda m, ids: (m, 0))] * len(unit)
+    half = attended_ref.shape[2] // CORES
+    step = wide // 5
+    core = ids_ref[len(shape)]
+    x = jnp.concatenate([attended_ref[ids_ref[k]] for k in range(len(shape))], axis=0)
+    for low in range(0, wide, step):
+        rows = slice(low, low + step)
+        parts = []
+        for unit in units:
+            w = unit[0][rows, :]
+            for extra in unit[1:]:
+                w = w + extra[rows, :]
+            parts.append(w)
+        total = jnp.dot(jnp.concatenate(parts, axis=1), x, preferred_element_type=jnp.float32)
+        if not first:
+            total = total + acc_ref[rows, :]
+        if last:
+            left, right = total[:, :half], total[:, half:]
+            refs[0][rows, :] = jnp.where(core == 0, left, right)
+            refs[1][rows, :] = jnp.where(core == 0, right, left).astype(jnp.bfloat16)
+        else:
+            refs[0][rows, :] = total
+
+
+def project(indices, attended, units, acc, last):
+    operands = [attended] + [part for unit in units for part in unit]
+    if acc is not None:
+        operands.append(acc)
+    wide, rows = units[0][0].shape[0], attended.shape[2]
+    shape = (wide, rows // CORES)
+    out_shape = jax.ShapeDtypeStruct((wide, rows), jnp.float32)
+    if last:
+        out_shape = (
+            jax.ShapeDtypeStruct(shape, jnp.float32), jax.ShapeDtypeStruct(shape, jnp.bfloat16)
+        )
+    vmem = pl.BlockSpec(memory_space=pltpu.VMEM)
     return call(
-        functools.partial(out_kernel, [len(unit) for unit in units]),
-        jax.ShapeDtypeStruct((wide, half), dtype),
-        flops=2 * half * depth * wide * count,
-        moved=2 * count * depth * wide + 4 * half * wide,
-        **scalars(1, (wide // step,), specs, pl.BlockSpec((step, half), lambda m, ids: (m, 0))),
+        functools.partial(out_kernel, [len(unit) for unit in units], acc is None, last),
+        out_shape,
+        14,
+        in_specs=resident(len(operands)),
+        out_specs=(vmem, vmem) if last else vmem,
     )(indices, *operands)
 
 
-def close_kernel(own_ref, mate_ref, hidden_ref, gains_ref, judge_ref, updated_ref, verdict_ref, total_ref):
-    width = total_ref.shape[0]
+def close_kernel(own_ref, mate_ref, hidden_ref, gains_ref, judge_ref, updated_ref, verdict_ref):
+    width = own_ref.shape[0]
     step = width // 5
     parts = [slice(low, low + step) for low in range(0, width, step)]
+    total_of = lambda rows: own_ref[rows, :] + mate_ref[rows, :].astype(jnp.float32)
     square = None
     for rows in parts:
-        total = own_ref[rows, :] + mate_ref[rows, :].astype(jnp.float32)
-        total_ref[rows, :] = total
+        total = total_of(rows)
         part = jnp.sum(total * total, axis=0, keepdims=True)
         square = part if square is None else square + part
     scale = lax.rsqrt(square * (1.0 / width) + epsilon)
     square = None
     for rows in parts:
         updated = hidden_ref[rows, :].astype(jnp.float32) + (
-            total_ref[rows, :] * scale * gains_ref[rows, 1:2]
+            total_of(rows) * scale * gains_ref[rows, 1:2]
         )
         updated = updated.astype(jnp.bfloat16)
         updated_ref[rows, :] = updated
@@ -485,10 +496,9 @@
             jax.ShapeDtypeStruct((width, half), jnp.bfloat16),
             jax.ShapeDtypeStruct((half, judge.shape[0]), jnp.bfloat16),
         ),
-        flops=2 * width * half * judge.shape[0],
-        moved=12 * width * half,
-        grid=(1,),
-        scratch_shapes=[pltpu.VMEM((width, half), jnp.float32)],
+        16,
+        in_specs=resident(5)[1:],
+        out_specs=(pl.BlockSpec(memory_space=pltpu.VMEM),) * 2,
     )(own, mate, hidden, gains, judge)
 
 
@@ -523,8 +533,9 @@
 
     def sources(self):
         at_end = (self.z == 0) | (self.z == 3)
-        flips = [0, 2, jnp.where(at_end, 4, 6), jnp.where(at_end, 6, 4)]
-        return [jnp.stack([self.chip ^ f, self.chip ^ f ^ 1]).astype(jnp.int32) for f in flips]
+        pick = lambda end, mid: jnp.where(at_end, end, mid)
+        flips = [0, 1, 2, 3, pick(4, 6), pick(5, 5), pick(6, 4), pick(7, 7)]
+        return jnp.stack([self.chip ^ f for f in flips]).astype(jnp.int32)
 
 
 def planned_body(
@@ -532,7 +543,6 @@
 ):
     p = Plane()
     ids = p.sources()
-    join = lambda *groups: jnp.concatenate([ids[g] for g in groups])
     core = p.core.astype(jnp.int32)[None]
     hidden_t = hidden[0].T
     width, tok_rows = hidden_t.shape
@@ -548,21 +558,15 @@
     a_inner = move(unit_in, p.z_mid)
 
     gains = jnp.concatenate([pre_gain, post_gain, final_gain], axis=0).T
-    judge_t = w_judge[0].T
-    half = HD // 2
-    lane = jnp.arange(LANES, dtype=jnp.int32)
-    frequency = jnp.exp((lane % half).astype(jnp.float32) * (-2.0 * math.log(rope_base) / HD))
-    positions = row_first + jnp.arange(chip_rows, dtype=jnp.int32)
-    angles = positions.astype(jnp.float32)[:, None] * frequency[None, :]
-    tables = (jnp.cos(angles), jnp.where(lane % HD < half, -1.0, 1.0) * jnp.sin(angles))
-    seg_own = lax.dynamic_slice_in_dim(segments, row_first, chip_rows, 0)
-    seg_prior = lax.dynamic_slice_in_dim(segments, jnp.maximum(row_first - WINDOW, 0), WINDOW, 0)
-    seg_prior = jnp.where(p.chip > 0, seg_prior, -1)
-    seg_keys = jnp.concatenate([seg_prior, seg_own])[:, None]
-    seg_q = seg_own[None, :]
-    chunks = prepare(core, hidden_t, move(tied(hidden_t, unit_in), p.mate), gains[:, :1], shards)
-    chunks, judge_t, seg_q, seg_keys, *tables = lax.optimization_barrier(
-        (chunks, judge_t, seg_q, seg_keys, *tables)
+    order = jnp.repeat(CORES * ids + p.core, CORES)
+    order = order ^ (jnp.arange(shards, dtype=jnp.int32) % CORES)
+    slots = jnp.argmax(
+        order[None, :] == jnp.arange(shards, dtype=jnp.int32)[:, None], axis=1
+    ).astype(jnp.int32)
+    mate_t = move(tied(hidden_t, unit_in), p.mate)
+    chunks, next_chunks, last_chunks = prepare(
+        jnp.concatenate([slots, core]), hidden_t, mate_t, gains[:, :1],
+        (shards // 2, shards // 4, shards // 4),
     )
 
     a_side_near = move(tied(a_near, a_side, chunks), p.x_all)
@@ -571,44 +575,60 @@
 
     o_near = move(tied(unit_out, a_from_inner), p.z_pair)
     o_inner = move(tied(unit_out, a_far), p.z_mid)
-    a_x_third = move(a_from_inner, p.x_end)
-    a_x_far = move(a_far, p.x_mid)
+    a_round = move(a_from_inner + a_far, p.x_all)
     a_side_inner = move(tied(a_side, a_far), p.z_mid)
     a_from_far = move(tied(a_far, a_from_inner), p.z_out)
     o_side = move(tied(unit_out, a_side_near), p.x_all)
     units = [[unit_in], [a_side], [a_near], [a_side_near]]
-    acc = qkv_group(CORES * join(0, 1) + p.core, chunks, units, None, None)
-
-    a_x_fourth = move(tied(a_from_far, acc, o_near, o_inner, o_side, a_x_third, a_x_far, a_side_inner), p.x_end)
-    o_far = move(tied(o_near, acc), p.z_mid)
-    o_from_inner = move(tied(o_inner, acc), p.z_out)
-    units = [[a_inner, a_from_inner], [a_side_inner, a_x_third]]
-    acc = qkv_group(CORES * join(2) + p.core, chunks, units, acc, None)
-
-    o_x_third = move(tied(o_from_inner, a_x_fourth, acc), p.x_end)
-    o_x_near = move(tied(o_near, a_x_far, acc), p.x_mid)
-    o_from_far = move(tied(o_far, a_x_fourth, acc), p.z_out)
-    o_side_inner = move(tied(o_side, o_far, acc), p.z_mid)
-    units = [[a_far, a_from_far], [a_x_far, a_x_fourth]]
-    qkv = qkv_group(CORES * join(3) + p.core, chunks, units, acc, tables)
-
-    o_x_far = move(tied(o_far, o_x_near, qkv), p.x_mid)
-    o_x_fourth = move(tied(o_from_far, o_x_third, qkv), p.x_end)
-    o_z_side = move(tied(o_side, o_from_far, qkv), p.z_out)
+    acc = qkv_group(chunks, units, None, None)
+
+    half = HD // 2
+    lane = jnp.arange(LANES, dtype=jnp.int32)
+    frequency = jnp.exp((lane % half).astype(jnp.float32) * (-2.0 * math.log(rope_base) / HD))
+    positions = tied(row_first, a_near) + jnp.arange(chip_rows, dtype=jnp.int32)
+    angles = positions.astype(jnp.float32)[:, None] * frequency[None, :]
+    tables = (jnp.cos(angles), jnp.where(lane % HD < half, -1.0, 1.0) * jnp.sin(angles))
+    seg_all = tied(segments, a_near)
+    seg_own = lax.dynamic_slice_in_dim(seg_all, row_first, chip_rows, 0)
+    seg_prior = lax.dynamic_slice_in_dim(seg_all, jnp.maximum(row_first - WINDOW, 0), WINDOW, 0)
+    seg_prior = jnp.where(p.chip > 0, seg_prior, -1)
+    seg_keys = jnp.concatenate([seg_prior, seg_own])[None, :]
+    seg_q = seg_own[None, :]
+    judge_t = tied(w_judge, a_near)[0].T
+    next_chunks, judge_t, seg_q, seg_keys, *tables = lax.optimization_barrier(
+        (next_chunks, judge_t, seg_q, seg_keys, *tables)
+    )
+
+    done = (acc, o_near, o_inner, o_side, a_round, a_side_inner)
+    a_x_fourth = move(tied(a_from_far, *done), p.x_end)
+    o_far = move(tied(o_near, a_from_far, *done), p.z_mid)
+    o_from_inner = move(tied(o_inner, a_from_far, *done), p.z_out)
+    o_x_near = move(tied(o_near, a_from_far, *done), p.x_mid)
+    acc = qkv_group(next_chunks, [[a_inner, a_from_inner], [a_round]], acc, None)
+
+    done = (a_x_fourth, o_x_near, acc)
+    o_round = move(tied(o_from_inner + o_far, *done), p.x_all)
+    o_from_far = move(tied(o_far, *done), p.z_out)
+    o_side_inner = move(tied(o_side, *done), p.z_mid)
+    units = [[a_far, a_from_far], [a_side_inner, a_x_fourth]]
+    qkv = qkv_group(last_chunks, units, acc, tables)
     own_kv = qkv[:, QH * HD // CORES :]
-    mate_kv = move(tied(own_kv, o_x_third, o_x_near, o_from_far, o_side_inner), p.mate)
+    mate_kv = move(own_kv, p.mate)
     halo = jnp.concatenate([own_kv, mate_kv], axis=1)[chip_rows - WINDOW :]
     halo = move(halo, p.line)
+
     attended = attend(core, qkv, own_kv, mate_kv, None, seg_q, seg_keys, None)
+
+    done = (o_round, halo)
+    o_x_fourth = move(tied(o_from_far, *done), p.x_end)
+    o_z_side = move(tied(o_side, o_from_far, *done), p.z_out)
     attended = attend(core, qkv, own_kv, mate_kv, halo, seg_q, seg_keys, attended)
     attended = attended.reshape(shards // CORES, -1, chip_rows)
 
-    units = [[unit_out], [o_side], [o_near], [o_x_near, o_z_side]]
-    units += [[o_inner, o_from_inner], [o_side_inner, o_x_third]]
-    units += [[o_far, o_from_far], [o_x_far, o_x_fourth]]
-    order = join(0, 1, 2, 3)
-    mate = project(jnp.concatenate([order, 1 - core]), attended, units, jnp.bfloat16)
-    own = project(jnp.concatenate([order, core]), attended, units, jnp.float32)
+    units = [[unit_out], [o_side], [o_near], [o_inner, o_from_inner], [o_round], [o_far, o_from_far]]
+    acc = project(jnp.concatenate([ids[:3], ids[4:7], core]), attended, units, None, False)
+    units = [[o_x_near, o_z_side], [o_side_inner, o_x_fourth]]
+    own, mate = project(jnp.concatenate([ids[3:4], ids[7:], core]), attended, units, acc, True)
     updated, verdict = close(own, move(mate, p.mate), hidden_t, gains, judge_t)
 
     members = lax.axis_size("member")

time: 211 us -> 189 us (0.90); the launches traced: 207 us -> 188 us
  Pallas kernels: 73.2 us -> 50.7 us
  local copies, waits for them, and re-layouts: 13.7 us -> 22 us
  starting transfers between devices: 41.9 us -> 37.7 us
  waiting for transfers between devices: 74.3 us -> 70.5 us
  other arithmetic: 3.23 us -> 5.75 us
    pallas_call x3, Pallas kernels: 28.3 us -> 16.2 us  [qkv_group(): call(functools.partial(qkv_kernel, [len(unit) for unit in units], first,...]
    pallas_call x6, Pallas kernels: 38 us -> 29.2 us  [the longest x1 10.5 us: prepare(): call(prepare_kernel, [jax.ShapeDtypeStruct((n, CORES * rows, depth), jnp....]
    unnamed x38 -> x67, local copies, waits for them, and re-layouts: 11 us -> 18 us
    ppermute x28 -> x26, starting transfers between devices: 40.4 us -> 36.2 us  [move(): return lax.ppermute(block, 'seq', route)]
    ppermute x28 -> x26, waiting for transfers between devices: 70.7 us -> 67.2 us  [move(): return lax.ppermute(block, 'seq', route)]
  transfers between devices with their start and end apart: 29 -> 27, of which waited for: 9 -> 13; matrix products, arithmetic and copies ran while one was open for 3% -> 5% of each run, Pallas kernels for 28% -> 22%
where the time goes in v3:
time: 189 us; the launch traced here: 188 us
  waiting for transfers between devices  70.5 us (37%)
  Pallas kernels  50.7 us (27%)
  starting transfers between devices  37.7 us (20%)
  local copies, waits for them, and re-layouts  22 us (12%)
  other arithmetic  5.75 us (3%)
    ppermute x26, waiting for transfers between devices, move(): return lax.ppermute(block, 'seq', route)  67.2 us
    ppermute x26, starting transfers between devices, move(): return lax.ppermute(block, 'seq', route)  36.2 us
    unnamed x67, local copies, waits for them, and re-layouts  18 us
    pallas_call x3, Pallas kernels, qkv_group(): call(functools.partial(qkv_kernel, [len(unit) for unit in units], first,...  16.2 us
    pallas_call x1, Pallas kernels, prepare(): call(prepare_kernel, [jax.ShapeDtypeStruct((n, CORES * rows, depth), jnp....  10.5 us
    pallas_call x2, Pallas kernels, attend(): call(attend_kernel, jax.ShapeDtypeStruct((q_wide, rows), jnp.bfloat16), 1...  9.4 us
    pallas_call x2, Pallas kernels, project(): call(functools.partial(out_kernel, [len(unit) for unit in units], acc is...  9.16 us
    pallas_call x1, Pallas kernels, close(): call(close_kernel, (jax.ShapeDtypeStruct((width, half), jnp.bfloat16), ja...  5.31 us
  transfers between devices with their start and end apart: 27, of which 13 were waited for; matrix products, arithmetic and copies ran while one was open for 5% of the time, Pallas kernels for 22%

profile of v3, /device:TPU:0, one launch (start us, length us, event | category | flops | bytes accessed | tf_op | source)
XLA Modules:
  0.0 187.7 jit_solution(11192458096773156274)
XLA Ops:
  0.7 1.1 copy-done.19
  4.3 1.4 collective-permute-done
  6.3 2.6 %collective-permute-start.3 = (bf16[180,2560]{1,0:T(8,128)(2,1)S(1)}, bf16[180,2560]{1,0:T(8,128)(2,1)}, u32[]{:S(2)}, u32[]{:S(2)}) collective-permute-start(bf16[180,2560]{1,0:T(8,128)(2,1)S(1)} %constant_dynamic-update-slice_fusion.refs_0_), channel_id=1, source_target_pairs={{0,2},{1,3},{2,0},{3,1},{4,6},{5,7},{6,4},{7,5},{8,10},{9,11},{10,... | collective-permute-start | bytes 2764808 | tf_op jit(solution)/shard_map/ppermute | solution.py:506
  8.9 1.6 collective-permute-start.2
  10.7 1.7 collective-permute-start.5
  13.8 10.5 %shard_map.114 = (bf16[8,768,180]{2,1,0:T(8,128)(2,1)S(1)}, bf16[4,768,180]{2,1,0:T(8,128)(2,1)S(1)}, bf16[4,768,180]{2,1,0:T(8,128)(2,1)S(1)}) custom-call(s32[17]{0:T(128)S(1)} %pad_add_fusion.2.slots_ref, bf16[2880,384]{1,0:T(8,128)(2,1)} %bitcast.10.own_ref.hidden_ref, bf16[2880,384]{1,0:T(8,128)(2,1)} %collective-permute-done.1.mate_ref, ...), custom_call_target="tpu_custom_call" | custom-call | flops 1000 | bytes 1000 | tf_op jit(solution)/shard_map/pallas_call | solution.py:247
  24.3 1.2 copy-done.13
  25.4 5.0 %collective-permute-done.3.refs_1_ = bf16[180,2560]{1,0:T(8,128)(2,1)} collective-permute-done((bf16[180,2560]{1,0:T(8,128)(2,1)S(1)}, bf16[180,2560]{1,0:T(8,128)(2,1)}, u32[]{:S(2)}, u32[]{:S(2)}) %collective-permute-start.3) | collective-permute-done | bytes 921632 | tf_op jit(solution)/shard_map/ppermute | solution.py:506
  30.4 1.5 collective-permute-done.2.refs_2_
  33.0 1.3 collective-permute-start.6
  34.3 19.8 %collective-permute-done.9.refs_3_ = bf16[180,2560]{1,0:T(8,128)(2,1)S(1)} collective-permute-done((bf16[180,2560]{1,0:T(8,128)(2,1)}, bf16[180,2560]{1,0:T(8,128)(2,1)S(1)}, u32[]{:S(2)}, u32[]{:S(2)}) %collective-permute-start.9) | collective-permute-done | bytes 921632 | tf_op jit(solution)/shard_map/ppermute | solution.py:506
  55.5 3.2 %collective-permute-done.6.refs_1_ = bf16[180,2560]{1,0:T(8,128)(2,1)S(1)} collective-permute-done((bf16[180,2560]{1,0:T(8,128)(2,1)}, bf16[180,2560]{1,0:T(8,128)(2,1)S(1)}, u32[]{:S(2)}, u32[]{:S(2)}) %collective-permute-start.6) | collective-permute-done | bytes 921632 | tf_op jit(solution)/shard_map/ppermute | solution.py:506
  59.0 1.5 collective-permute-start.13
  60.5 1.3 collective-permute-start.7
  61.8 1.5 collective-permute-start.11
  63.4 10.3 %collective-permute-done.12.refs_1_ = bf16[2880,128]{1,0:T(8,128)(2,1)} collective-permute-done((bf16[2880,128]{1,0:T(8,128)(2,1)S(1)}, bf16[2880,128]{1,0:T(8,128)(2,1)}, u32[]{:S(2)}, u32[]{:S(2)}) %collective-permute-start.12) | collective-permute-done | bytes 737312 | tf_op jit(solution)/shard_map/ppermute | solution.py:506
  73.7 1.6 collective-permute-start.10
  75.2 6.3 %shard_map.115.refs_3_ = f32[768,1280]{1,0:T(8,128)S(1)} custom-call(bf16[8,768,180]{2,1,0:T(8,128)(2,1)S(1)} %get-tuple-element.42.chunks_ref, bf16[180,2560]{1,0:T(8,128)(2,1)S(1)} %constant_dynamic-update-slice_fusion.refs_0_, bf16[180,2560]{1,0:T(8,128)(2,1)} %collective-permute-done.3.refs_1_, bf16[180,2560]{1,0:T(8,128)(2,1)} %collective-permute-done.2.refs_2_, ...), custom_call_target="tpu_custom_call" | custom-call | flops 1000 | bytes 1000 | tf_op jit(solution)/shard_map/pallas_call | solution.py:321
  81.6 1.9 %copy-done = f32[768,1280]{1,0:T(8,128)} copy-done((f32[768,1280]{1,0:T(8,128)}, f32[768,1280]{1,0:T(8,128)S(1)}, u32[]{:S(2)}) %copy-start) | copy-done | bytes 3932184
  83.5 15.4 %collective-permute-done.10.refs_2_ = bf16[2880,128]{1,0:T(8,128)(2,1)} collective-permute-done((bf16[2880,128]{1,0:T(8,128)(2,1)S(1)}, bf16[2880,128]{1,0:T(8,128)(2,1)}, u32[]{:S(2)}, u32[]{:S(2)}) %collective-permute-start.10) | collective-permute-done | bytes 737312 | tf_op jit(solution)/shard_map/ppermute | solution.py:506
  100.7 2.6 %collective-permute-start.14 = (bf16[180,2560]{1,0:T(8,128)(2,1)}, bf16[180,2560]{1,0:T(8,128)(2,1)}, u32[]{:S(2)}, u32[]{:S(2)}) collective-permute-start(bf16[180,2560]{1,0:T(8,128)(2,1)} %collective-permute-done.7.refs_1_), channel_id=1, source_target_pairs={{0,2},{1,3},{2,0},{3,1},{12,14},{13,15},{14,12},{15,13},{16,18},{1... | collective-permute-start | bytes 2764808 | tf_op jit(solution)/shard_map/ppermute | solution.py:506
  103.3 1.5 collective-permute-start.18
  104.9 1.3 collective-permute-start.20
  108.6 2.3 %copy.24 = bf16[1,2880,128]{1,2,0:T(8,128)(2,1)} copy(bf16[1,2880,128]{2,1,0:T(8,128)(2,1)} %param.19) | data formatting | bytes 1474560 | tf_op jit(solution)/shard_map/optimization_barrier | solution.py:153
  111.0 1.4 fusion
  112.4 2.1 %copy-done.1 = f32[768,1280]{1,0:T(8,128)S(1)} copy-done((f32[768,1280]{1,0:T(8,128)S(1)}, f32[768,1280]{1,0:T(8,128)}, u32[]{:S(2)}) %copy-start.1) | copy-done | bytes 3932184
  114.5 1.4 copy-done.14
  115.9 1.2 copy-done.18
  117.1 4.2 %shard_map.116.refs_4_ = f32[768,1280]{1,0:T(8,128)S(1)} custom-call(bf16[4,768,180]{2,1,0:T(8,128)(2,1)S(1)} %copy-done.14, bf16[180,2560]{1,0:T(8,128)(2,1)} %collective-permute-done.5.refs_0_, bf16[180,2560]{1,0:T(8,128)(2,1)S(1)} %collective-permute-done.6.refs_1_, bf16[180,2560]{1,0:T(8,128)(2,1)S(1)} %copy-done.18, f32[768,1280]{1,0:T(8,128)S(1)} %copy-done.1), custom_call_target="tpu_custom_call" | custom-call | flops 1000 | bytes 1000 | tf_op jit(solution)/shard_map/pallas_call | solution.py:321
  122.0 1.6 add.74
  124.5 1.3 collective-permute-start.19
  125.8 1.4 collective-permute-start.21
  127.2 5.7 %shard_map.117.q_ref = bf16[768,1280]{1,0:T(8,128)(2,1)S(1)} custom-call(bf16[4,768,180]{2,1,0:T(8,128)(2,1)S(1)} %copy-done.12, bf16[180,2560]{1,0:T(8,128)(2,1)S(1)} %collective-permute-done.4.refs_0_, bf16[180,2560]{1,0:T(8,128)(2,1)} %collective-permute-done.7.refs_1_, bf16[180,2560]{1,0:T(8,128)(2,1)S(1)} %copy-done.16, ...), custom_call_target="tpu_custom_call" | custom-call | flops 1000 | bytes 1000 | tf_op jit(solution)/shard_map/pallas_call | solution.py:321
  133.0 1.7 collective-permute-done.15.mate0_ref.mate1_ref
  134.7 2.6 %collective-permute-start.16 = (bf16[128,512]{1,0:T(8,128)(2,1)S(1)}, bf16[128,512]{1,0:T(8,128)(2,1)S(1)}, u32[]{:S(2)}, u32[]{:S(2)}) collective-permute-start(bf16[128,512]{1,0:T(8,128)(2,1)S(1)} %pad_maximum_fusion), channel_id=1, source_target_pairs={{0,2},{1,3},{2,4},{3,5},{4,6},{5,7},{6,8},{7,9},{8,10},{9,11},{10,... | collective-permute-start | bytes 393224 | tf_op jit(solution)/shard_map/ppermute | solution.py:506
  137.3 1.5 collective-permute-start.23
  138.9 3.1 %collective-permute-done.16.own0_ref.mate0_ref = bf16[128,512]{1,0:T(8,128)(2,1)S(1)} collective-permute-done((bf16[128,512]{1,0:T(8,128)(2,1)S(1)}, bf16[128,512]{1,0:T(8,128)(2,1)S(1)}, u32[]{:S(2)}, u32[]{:S(2)}) %collective-permute-start.16) | collective-permute-done | bytes 131104 | tf_op jit(solution)/shard_map/ppermute | solution.py:506
  144.3 1.3 collective-permute-start.22
  145.6 5.1 %collective-permute-start.24 = (bf16[2880,128]{1,0:T(8,128)(2,1)}, bf16[2880,128]{1,0:T(8,128)(2,1)}, u32[]{:S(2)}, u32[]{:S(2)}) collective-permute-start(bf16[2880,128]{1,0:T(8,128)(2,1)} %collective-permute-done.19.refs_7_), channel_id=1, source_target_pairs={{0,2},{1,3},{2,0},{3,1},{12,14},{13,15},{14,12},{15,13},{16,18},{1... | collective-permute-start | bytes 2211848 | tf_op jit(solution)/shard_map/ppermute | solution.py:506
  150.8 7.9 %shard_map.118.out_refs_0_ = bf16[1024,768]{1,0:T(8,128)(2,1)S(1)} custom-call(s32[1]{0:T(128)} %bitcast.2.core_ref, bf16[768,1280]{1,0:T(8,128)(2,1)S(1)} %shard_map.117.q_ref, bf16[768,256]{1,0:T(8,128)(2,1)S(1)} %slice.17.own0_ref.own1_ref, bf16[768,256]{1,0:T(8,128)(2,1)S(1)} %slice.17.own0_ref.own1_ref, ...), custom_call_target="tpu_custom_call" | custom-call | flops 1000 | bytes 1000 | tf_op jit(solution)/shard_map/pallas_call | solution.py:402
  158.8 1.0 copy-done.5
  161.7 1.5 shard_map.119
  163.2 5.7 %shard_map.120.refs_4_ = f32[2880,768]{1,0:T(8,128)S(1)} custom-call(s32[7]{0:T(128)S(1)} %concatenate.30.ids_ref, bf16[8,128,768]{2,1,0:T(8,128)(2,1)S(1)} %bitcast.27, bf16[2880,128]{1,0:T(8,128)(2,1)S(1)} %bitcast.36, bf16[2880,128]{1,0:T(8,128)(2,1)} %collective-permute-done.12.refs_1_, bf16[2880,128]{1,0:T(8,128)(2,1)} %collective-permute-done.10.refs_2_, ...), custom_call_target="tpu_custom_call" | custom-call | flops 1000 | bytes 1000 | tf_op jit(solution)/shard_map/pallas_call | solution.py:453
  169.1 3.4 %shard_map.121 = (f32[2880,384]{1,0:T(8,128)S(1)}, bf16[2880,384]{1,0:T(8,128)(2,1)S(1)}) custom-call(s32[3]{0:T(128)S(1)} %pad_add_fusion.1.ids_ref, bf16[8,128,768]{2,1,0:T(8,128)(2,1)S(1)} %bitcast.28, bf16[2880,128]{1,0:T(8,128)(2,1)S(1)} %copy-done.25, bf16[2880,128]{1,0:T(8,128)(2,1)} %collective-permute-done.22.refs_1_, ...), custom_call_target="tpu_custom_call" | custom-call | flops 1000 | bytes 1000 | tf_op jit(solution)/shard_map/pallas_call | solution.py:453
  172.6 4.3 %collective-permute-done.25.mate_ref = bf16[2880,384]{1,0:T(8,128)(2,1)S(1)} collective-permute-done((bf16[2880,384]{1,0:T(8,128)(2,1)S(1)}, bf16[2880,384]{1,0:T(8,128)(2,1)S(1)}, u32[]{:S(2)}, u32[]{:S(2)}) %collective-permute-start.25) | collective-permute-done | bytes 2211872 | tf_op jit(solution)/shard_map/ppermute | solution.py:506
  176.9 5.3 %shard_map.122 = (bf16[2880,384]{1,0:T(8,128)(2,1)}, bf16[384,128]{1,0:T(8,128)(2,1)S(1)}) custom-call(f32[2880,384]{1,0:T(8,128)S(1)} %get-tuple-element.67.own_ref, bf16[2880,384]{1,0:T(8,128)(2,1)S(1)} %collective-permute-done.25.mate_ref, bf16[2880,384]{1,0:T(8,128)(2,1)} %bitcast.10.own_ref.hidden_ref, f32[2880,3]{1,0:T(8,128)S(1)} %bitcast.30, ...), custom_call_target="tpu_custom_call" | custom-call | flops 1000 | bytes 1000 | tf_op jit(solution)/shard_map/pallas_call | solution.py:493
  182.2 1.5 collective-permute-start.26
  183.7 3.3 %collective-permute-done.26 = bf16[384,128]{1,0:T(8,128)(2,1)S(1)} collective-permute-done((bf16[384,128]{1,0:T(8,128)(2,1)S(1)}, bf16[384,128]{1,0:T(8,128)(2,1)S(1)}, u32[]{:S(2)}, u32[]{:S(2)}) %collective-permute-start.26) | collective-permute-done | bytes 98336 | tf_op jit(solution)/shard_map/ppermute | solution.py:638
  (109 shorter events, 18.7 us)
Async XLA Ops:
  0.6 10.0 %copy-start.30 = (f32[1,2880]{1,0:T(1,128)S(1)}, f32[1,2880]{1,0:T(1,128)}, u32[]{:S(2)}) copy-start(f32[1,2880]{1,0:T(1,128)} %param.18) | copy-start | bytes 34564
  0.6 10.0 %copy-start.31 = (f32[1,2880]{1,0:T(1,128)S(1)}, f32[1,2880]{1,0:T(1,128)}, u32[]{:S(2)}) copy-start(f32[1,2880]{1,0:T(1,128)} %param.17) | copy-start | bytes 34564
  3.6 7.1 %copy-start.32 = (f32[1,2880]{1,0:T(1,128)S(1)}, f32[1,2880]{1,0:T(1,128)}, u32[]{:S(2)}) copy-start(f32[1,2880]{1,0:T(1,128)} %param.12) | copy-start | bytes 34564
  3.7 2.0 %collective-permute-start = (bf16[180,1280]{1,0:T(8,128)(2,1)S(1)}, bf16[180,1280]{1,0:T(8,128)(2,1)S(1)}, u32[]{:S(2)}, u32[]{:S(2)}) collective-permute-start(bf16[180,1280]{1,0:T(8,128)(2,1)S(1)} %get-tuple-element.39), channel_id=1, source_target_pairs={{0,1},{1,0},{2,3},{3,2},{4,5},{5,4},{6,7},{7,6},{8,9},{9,8},{10,11... | collective-permute-start | bytes 1382408 | tf_op jit(solution)/shard_map/ppermute | solution.py:506
  5.8 8.0 %collective-permute-start.1 = (bf16[2880,384]{1,0:T(8,128)(2,1)}, bf16[2880,384]{1,0:T(8,128)(2,1)}, u32[]{:S(2)}, u32[]{:S(2)}) collective-permute-start(bf16[2880,384]{1,0:T(8,128)(2,1)} %bitcast.10.own_ref.hidden_ref), channel_id=1, source_target_pairs={{0,1},{1,0},{2,3},{3,2},{4,5},{5,4},{6,7},{7,6},{8,9},{9,8},{10,11... | collective-permute-start | bytes 6635528 | tf_op jit(solution)/shard_map/ppermute | solution.py:506
  6.3 24.2 %collective-permute-start.3 = (bf16[180,2560]{1,0:T(8,128)(2,1)S(1)}, bf16[180,2560]{1,0:T(8,128)(2,1)}, u32[]{:S(2)}, u32[]{:S(2)}) collective-permute-start(bf16[180,2560]{1,0:T(8,128)(2,1)S(1)} %constant_dynamic-update-slice_fusion.refs_0_), channel_id=1, source_target_pairs={{0,2},{1,3},{2,0},{3,1},{4,6},{5,7},{6,4},{7,5},{8,10},{9,11},{10,... | collective-permute-start | bytes 2764808 | tf_op jit(solution)/shard_map/ppermute | solution.py:506
  8.9 23.0 %collective-permute-start.2 = (bf16[180,2560]{1,0:T(8,128)(2,1)S(1)}, bf16[180,2560]{1,0:T(8,128)(2,1)}, u32[]{:S(2)}, u32[]{:S(2)}) collective-permute-start(bf16[180,2560]{1,0:T(8,128)(2,1)S(1)} %constant_dynamic-update-slice_fusion.refs_0_), channel_id=1, source_target_pairs={{0,4},{1,5},{2,6},{3,7},{4,0},{5,1},{6,2},{7,3},{8,12},{9,13},{10,... | collective-permute-start | bytes 2764808 | tf_op jit(solution)/shard_map/ppermute | solution.py:506
  10.7 22.3 %collective-permute-start.5 = (bf16[180,2560]{1,0:T(8,128)(2,1)S(1)}, bf16[180,2560]{1,0:T(8,128)(2,1)}, u32[]{:S(2)}, u32[]{:S(2)}) collective-permute-start(bf16[180,2560]{1,0:T(8,128)(2,1)S(1)} %constant_dynamic-update-slice_fusion.refs_0_), channel_id=1, source_target_pairs={{4,8},{5,9},{6,10},{7,11},{8,4},{9,5},{10,6},{11,7},{20,24},{21,25... | collective-permute-start | bytes 2764808 | tf_op jit(solution)/shard_map/ppermute | solution.py:506
  12.9 11.3 %copy-start.2 = (f32[3,2880]{0,1:T(8,128)}, f32[3,2880]{0,1:T(8,128)S(1)}, u32[]{:S(2)}) copy-start(f32[3,2880]{0,1:T(8,128)S(1)} %copy.23) | copy-start | bytes 103684
  13.8 40.4 %copy-start.20 = (bf16[1,128,2880]{1,2,0:T(8,128)(2,1)S(1)}, bf16[1,128,2880]{1,2,0:T(8,128)(2,1)}, u32[]{:S(2)}) copy-start(bf16[1,128,2880]{1,2,0:T(8,128)(2,1)} %param.16) | copy-start | bytes 2211844
  25.4 56.1 %copy-start.11 = (bf16[4,768,180]{2,1,0:T(8,128)(2,1)}, bf16[4,768,180]{2,1,0:T(8,128)(2,1)S(1)}, u32[]{:S(2)}) copy-start(bf16[4,768,180]{2,1,0:T(8,128)(2,1)S(1)} %get-tuple-element.41.chunks_ref) | copy-start | bytes 3317764
  31.9 22.2 %collective-permute-start.9 = (bf16[180,2560]{1,0:T(8,128)(2,1)}, bf16[180,2560]{1,0:T(8,128)(2,1)S(1)}, u32[]{:S(2)}, u32[]{:S(2)}) collective-permute-start(bf16[180,2560]{1,0:T(8,128)(2,1)} %collective-permute-done.2.refs_2_), channel_id=1, source_target_pairs={{0,2},{1,3},{2,0},{3,1},{4,6},{5,7},{6,4},{7,5},{8,10},{9,11},{10,... | collective-permute-start | bytes 2764808 | tf_op jit(solution)/shard_map/ppermute | solution.py:506
  32.3 22.6 %collective-permute-start.4 = (bf16[180,2560]{1,0:T(8,128)(2,1)}, bf16[180,2560]{1,0:T(8,128)(2,1)S(1)}, u32[]{:S(2)}, u32[]{:S(2)}) collective-permute-start(bf16[180,2560]{1,0:T(8,128)(2,1)} %collective-permute-done.2.refs_2_), channel_id=1, source_target_pairs={{4,8},{5,9},{6,10},{7,11},{8,4},{9,5},{10,6},{11,7},{20,24},{21,25... | collective-permute-start | bytes 2764808 | tf_op jit(solution)/shard_map/ppermute | solution.py:506
  33.0 25.8 %collective-permute-start.6 = (bf16[180,2560]{1,0:T(8,128)(2,1)}, bf16[180,2560]{1,0:T(8,128)(2,1)S(1)}, u32[]{:S(2)}, u32[]{:S(2)}) collective-permute-start(bf16[180,2560]{1,0:T(8,128)(2,1)} %collective-permute-done.5.refs_0_), channel_id=1, source_target_pairs={{4,0},{5,1},{6,2},{7,3},{8,12},{9,13},{10,14},{11,15},{20,16},{21,... | collective-permute-start | bytes 2764808 | tf_op jit(solution)/shard_map/ppermute | solution.py:506
  54.1 19.5 %collective-permute-start.12 = (bf16[2880,128]{1,0:T(8,128)(2,1)S(1)}, bf16[2880,128]{1,0:T(8,128)(2,1)}, u32[]{:S(2)}, u32[]{:S(2)}) collective-permute-start(bf16[2880,128]{1,0:T(8,128)(2,1)S(1)} %bitcast.33), channel_id=1, source_target_pairs={{0,2},{1,3},{2,0},{3,1},{4,6},{5,7},{6,4},{7,5},{8,10},{9,11},{10,... | collective-permute-start | bytes 2211848 | tf_op jit(solution)/shard_map/ppermute | solution.py:506
  54.8 44.0 %collective-permute-start.8 = (bf16[180,2560]{1,0:T(8,128)(2,1)}, bf16[180,2560]{1,0:T(8,128)(2,1)S(1)}, u32[]{:S(2)}, u32[]{:S(2)}) collective-permute-start(bf16[180,2560]{1,0:T(8,128)(2,1)} %collective-permute-done.3.refs_1_), channel_id=1, source_target_pairs={{4,8},{5,9},{6,10},{7,11},{8,4},{9,5},{10,6},{11,7},{20,24},{21,25... | collective-permute-start | bytes 2764808 | tf_op jit(solution)/shard_map/ppermute | solution.py:506
  59.0 40.7 %collective-permute-start.13 = (bf16[180,2560]{1,0:T(8,128)(2,1)S(1)}, bf16[180,2560]{1,0:T(8,128)(2,1)S(1)}, u32[]{:S(2)}, u32[]{:S(2)}) collective-permute-start(bf16[180,2560]{1,0:T(8,128)(2,1)S(1)} %add.68), channel_id=1, source_target_pairs={{0,2},{1,3},{2,0},{3,1},{4,6},{5,7},{6,4},{7,5},{8,10},{9,11},{10,... | collective-permute-start | bytes 2764808 | tf_op jit(solution)/shard_map/ppermute | solution.py:506
  60.5 40.2 %collective-permute-start.7 = (bf16[180,2560]{1,0:T(8,128)(2,1)S(1)}, bf16[180,2560]{1,0:T(8,128)(2,1)}, u32[]{:S(2)}, u32[]{:S(2)}) collective-permute-start(bf16[180,2560]{1,0:T(8,128)(2,1)S(1)} %collective-permute-done.4.refs_0_), channel_id=1, source_target_pairs={{4,0},{5,1},{6,2},{7,3},{8,12},{9,13},{10,14},{11,15},{20,16},{21,... | collective-permute-start | bytes 2764808 | tf_op jit(solution)/shard_map/ppermute | solution.py:506
  61.8 21.6 %collective-permute-start.11 = (bf16[2880,128]{1,0:T(8,128)(2,1)S(1)}, bf16[2880,128]{1,0:T(8,128)(2,1)}, u32[]{:S(2)}, u32[]{:S(2)}) collective-permute-start(bf16[2880,128]{1,0:T(8,128)(2,1)S(1)} %bitcast.34), channel_id=1, source_target_pairs={{4,8},{5,9},{6,10},{7,11},{8,4},{9,5},{10,6},{11,7},{20,24},{21,25... | collective-permute-start | bytes 2211848 | tf_op jit(solution)/shard_map/ppermute | solution.py:506
  73.7 25.2 %collective-permute-start.10 = (bf16[2880,128]{1,0:T(8,128)(2,1)S(1)}, bf16[2880,128]{1,0:T(8,128)(2,1)}, u32[]{:S(2)}, u32[]{:S(2)}) collective-permute-start(bf16[2880,128]{1,0:T(8,128)(2,1)S(1)} %bitcast.35), channel_id=1, source_target_pairs={{0,4},{1,5},{2,6},{3,7},{4,0},{5,1},{6,2},{7,3},{8,12},{9,13},{10,... | collective-permute-start | bytes 2211848 | tf_op jit(solution)/shard_map/ppermute | solution.py:506
  81.6 1.9 %copy-start = (f32[768,1280]{1,0:T(8,128)}, f32[768,1280]{1,0:T(8,128)S(1)}, u32[]{:S(2)}) copy-start(f32[768,1280]{1,0:T(8,128)S(1)} %shard_map.115.refs_3_) | copy-start | bytes 11796484
  100.7 23.8 %collective-permute-start.14 = (bf16[180,2560]{1,0:T(8,128)(2,1)}, bf16[180,2560]{1,0:T(8,128)(2,1)}, u32[]{:S(2)}, u32[]{:S(2)}) collective-permute-start(bf16[180,2560]{1,0:T(8,128)(2,1)} %collective-permute-done.7.refs_1_), channel_id=1, source_target_pairs={{0,2},{1,3},{2,0},{3,1},{12,14},{13,15},{14,12},{15,13},{16,18},{1... | collective-permute-start | bytes 2764808 | tf_op jit(solution)/shard_map/ppermute | solution.py:506
  103.3 18.0 %collective-permute-start.18 = (bf16[2880,128]{1,0:T(8,128)(2,1)}, bf16[2880,128]{1,0:T(8,128)(2,1)}, u32[]{:S(2)}, u32[]{:S(2)}) collective-permute-start(bf16[2880,128]{1,0:T(8,128)(2,1)} %collective-permute-done.10.refs_2_), channel_id=1, source_target_pairs={{4,8},{5,9},{6,10},{7,11},{8,4},{9,5},{10,6},{11,7},{20,24},{21,25... | collective-permute-start | bytes 2211848 | tf_op jit(solution)/shard_map/ppermute | solution.py:506
  104.9 17.1 %collective-permute-start.20 = (bf16[2880,128]{1,0:T(8,128)(2,1)}, bf16[2880,128]{1,0:T(8,128)(2,1)S(1)}, u32[]{:S(2)}, u32[]{:S(2)}) collective-permute-start(bf16[2880,128]{1,0:T(8,128)(2,1)} %collective-permute-done.11.refs_3_), channel_id=1, source_target_pairs={{4,0},{5,1},{6,2},{7,3},{8,12},{9,13},{10,14},{11,15},{20,16},{21,... | collective-permute-start | bytes 2211848 | tf_op jit(solution)/shard_map/ppermute | solution.py:506
  106.1 17.4 %collective-permute-start.17 = (bf16[2880,128]{1,0:T(8,128)(2,1)}, bf16[2880,128]{1,0:T(8,128)(2,1)S(1)}, u32[]{:S(2)}, u32[]{:S(2)}) collective-permute-start(bf16[2880,128]{1,0:T(8,128)(2,1)} %collective-permute-done.10.refs_2_), channel_id=1, source_target_pairs={{4,6},{5,7},{6,4},{7,5},{8,10},{9,11},{10,8},{11,9},{20,22},{21,23... | collective-permute-start | bytes 2211848 | tf_op jit(solution)/shard_map/ppermute | solution.py:506
  112.4 2.1 %copy-start.1 = (f32[768,1280]{1,0:T(8,128)S(1)}, f32[768,1280]{1,0:T(8,128)}, u32[]{:S(2)}) copy-start(f32[768,1280]{1,0:T(8,128)} %copy-done) | copy-start | bytes 11796484
  114.5 1.4 copy-start.14
  115.9 1.2 copy-start.18
  117.1 10.1 %copy-start.16 = (bf16[180,2560]{1,0:T(8,128)(2,1)S(1)}, bf16[180,2560]{1,0:T(8,128)(2,1)}, u32[]{:S(2)}) copy-start(bf16[180,2560]{1,0:T(8,128)(2,1)} %copy-done.15) | copy-start | bytes 2764804
  121.3 5.9 %copy-start.12 = (bf16[4,768,180]{2,1,0:T(8,128)(2,1)S(1)}, bf16[4,768,180]{2,1,0:T(8,128)(2,1)}, u32[]{:S(2)}) copy-start(bf16[4,768,180]{2,1,0:T(8,128)(2,1)} %copy-done.11) | copy-start | bytes 3317764
  122.0 5.2 %copy-start.9 = (bf16[2880,128]{1,0:T(8,128)(2,1)}, bf16[2880,128]{1,0:T(8,128)(2,1)S(1)}, u32[]{:S(2)}) copy-start(bf16[2880,128]{1,0:T(8,128)(2,1)S(1)} %collective-permute-done.20.refs_4_) | copy-start | bytes 2211844
  124.5 18.9 %collective-permute-start.19 = (bf16[2880,128]{1,0:T(8,128)(2,1)}, bf16[2880,128]{1,0:T(8,128)(2,1)}, u32[]{:S(2)}, u32[]{:S(2)}) collective-permute-start(bf16[2880,128]{1,0:T(8,128)(2,1)} %collective-permute-done.18.refs_6_), channel_id=1, source_target_pairs={{4,0},{5,1},{6,2},{7,3},{8,12},{9,13},{10,14},{11,15},{20,16},{21,... | collective-permute-start | bytes 2211848 | tf_op jit(solution)/shard_map/ppermute | solution.py:506
  125.8 17.6 %collective-permute-start.21 = (bf16[2880,128]{1,0:T(8,128)(2,1)S(1)}, bf16[2880,128]{1,0:T(8,128)(2,1)S(1)}, u32[]{:S(2)}, u32[]{:S(2)}) collective-permute-start(bf16[2880,128]{1,0:T(8,128)(2,1)S(1)} %add.74), channel_id=1, source_target_pairs={{0,2},{1,3},{2,0},{3,1},{4,6},{5,7},{6,4},{7,5},{8,10},{9,11},{10,... | collective-permute-start | bytes 2211848 | tf_op jit(solution)/shard_map/ppermute | solution.py:506
  132.9 17.9 %copy-start.4 = (bf16[768,256]{1,0:T(8,128)(2,1)}, bf16[768,256]{1,0:T(8,128)(2,1)S(1)}, u32[]{:S(2)}) copy-start(bf16[768,256]{1,0:T(8,128)(2,1)S(1)} %slice.17.own0_ref.own1_ref) | copy-start | bytes 1179652
  132.9 1.8 collective-permute-start.15
  134.7 16.1 %copy-start.6 = (bf16[768,256]{1,0:T(8,128)(2,1)}, bf16[768,256]{1,0:T(8,128)(2,1)S(1)}, u32[]{:S(2)}) copy-start(bf16[768,256]{1,0:T(8,128)(2,1)S(1)} %collective-permute-done.15.mate0_ref.mate1_ref) | copy-start | bytes 1179652
  134.7 7.2 %collective-permute-start.16 = (bf16[128,512]{1,0:T(8,128)(2,1)S(1)}, bf16[128,512]{1,0:T(8,128)(2,1)S(1)}, u32[]{:S(2)}, u32[]{:S(2)}) collective-permute-start(bf16[128,512]{1,0:T(8,128)(2,1)S(1)} %pad_maximum_fusion), channel_id=1, source_target_pairs={{0,2},{1,3},{2,4},{3,5},{4,6},{5,7},{6,8},{7,9},{8,10},{9,11},{10,... | collective-permute-start | bytes 393224 | tf_op jit(solution)/shard_map/ppermute | solution.py:506
  137.3 31.7 %collective-permute-start.23 = (bf16[2880,128]{1,0:T(8,128)(2,1)}, bf16[2880,128]{1,0:T(8,128)(2,1)}, u32[]{:S(2)}, u32[]{:S(2)}) collective-permute-start(bf16[2880,128]{1,0:T(8,128)(2,1)} %collective-permute-done.12.refs_1_), channel_id=1, source_target_pairs={{4,8},{5,9},{6,10},{7,11},{8,4},{9,5},{10,6},{11,7},{20,24},{21,25... | collective-permute-start | bytes 2211848 | tf_op jit(solution)/shard_map/ppermute | solution.py:506
  144.3 24.7 %collective-permute-start.22 = (bf16[2880,128]{1,0:T(8,128)(2,1)}, bf16[2880,128]{1,0:T(8,128)(2,1)}, u32[]{:S(2)}, u32[]{:S(2)}) collective-permute-start(bf16[2880,128]{1,0:T(8,128)(2,1)} %collective-permute-done.12.refs_1_), channel_id=1, source_target_pairs={{4,0},{5,1},{6,2},{7,3},{8,12},{9,13},{10,14},{11,15},{20,16},{21,... | collective-permute-start | bytes 2211848 | tf_op jit(solution)/shard_map/ppermute | solution.py:506
  145.6 23.5 %collective-permute-start.24 = (bf16[2880,128]{1,0:T(8,128)(2,1)}, bf16[2880,128]{1,0:T(8,128)(2,1)}, u32[]{:S(2)}, u32[]{:S(2)}) collective-permute-start(bf16[2880,128]{1,0:T(8,128)(2,1)} %collective-permute-done.19.refs_7_), channel_id=1, source_target_pairs={{0,2},{1,3},{2,0},{3,1},{12,14},{13,15},{14,12},{15,13},{16,18},{1... | collective-permute-start | bytes 2211848 | tf_op jit(solution)/shard_map/ppermute | solution.py:506
  161.7 1.5 copy-start.10
  161.7 1.5 copy-start.21
  161.7 1.6 copy-start.23
  163.2 5.8 %copy-start.25 = (bf16[2880,128]{1,0:T(8,128)(2,1)S(1)}, bf16[2880,128]{1,0:T(8,128)(2,1)}, u32[]{:S(2)}) copy-start(bf16[2880,128]{1,0:T(8,128)(2,1)} %copy-done.24) | copy-start | bytes 2211844
  169.0 7.9 %copy-start.3 = (f32[3,2880]{0,1:T(8,128)S(1)}, f32[3,2880]{0,1:T(8,128)}, u32[]{:S(2)}) copy-start(f32[3,2880]{0,1:T(8,128)} %copy-done.2) | copy-start | bytes 103684
  169.0 7.9 %copy-start.8 = (bf16[1,2880,128]{1,2,0:T(8,128)(2,1)S(1)}, bf16[1,2880,128]{1,2,0:T(8,128)(2,1)}, u32[]{:S(2)}) copy-start(bf16[1,2880,128]{1,2,0:T(8,128)(2,1)} %copy.24) | copy-start | bytes 2211844
  172.5 4.4 %collective-permute-start.25 = (bf16[2880,384]{1,0:T(8,128)(2,1)S(1)}, bf16[2880,384]{1,0:T(8,128)(2,1)S(1)}, u32[]{:S(2)}, u32[]{:S(2)}) collective-permute-start(bf16[2880,384]{1,0:T(8,128)(2,1)S(1)} %get-tuple-element.68), channel_id=1, source_target_pairs={{0,1},{1,0},{2,3},{3,2},{4,5},{5,4},{6,7},{7,6},{8,9},{9,8},{10,11... | collective-permute-start | bytes 6635528 | tf_op jit(solution)/shard_map/ppermute | solution.py:506
  182.2 4.8 %collective-permute-start.26 = (bf16[384,128]{1,0:T(8,128)(2,1)S(1)}, bf16[384,128]{1,0:T(8,128)(2,1)S(1)}, u32[]{:S(2)}, u32[]{:S(2)}) collective-permute-start(bf16[384,128]{1,0:T(8,128)(2,1)S(1)} %get-tuple-element.71), channel_id=1, source_target_pairs={{0,16},{16,0},{1,17},{17,1},{2,18},{18,2},{3,19},{19,3},{4,20},{20... | collective-permute-start | bytes 294920 | tf_op jit(solution)/shard_map/ppermute | solution.py:638
  (12 other events, 11.3 us)

commit v4 on v3

--- a/solution.py
+++ b/solution.py
@@ -551,11 +551,15 @@
     row_first = p.chip * chip_rows
     unit_out = w_output[0].T
 
-    mine, other = halves(core, w_query[0], w_key[0], w_value[0])
+    o_side = move(unit_out, p.x_all)
+    o_near = move(unit_out, p.z_pair)
+    o_inner = move(unit_out, p.z_mid)
+    mate_t = move(hidden_t, p.mate)
+    mine, other = halves(core, tied(w_query, mate_t)[0], w_key[0], w_value[0])
     unit_in = jnp.concatenate([mine, move(other, p.mate)], axis=1)
-    a_side = move(unit_in, p.x_all)
-    a_near = move(unit_in, p.z_pair)
-    a_inner = move(unit_in, p.z_mid)
+    a_inner = move(tied(unit_in, o_inner), p.z_mid)
+    a_near = move(tied(unit_in, o_near), p.z_pair)
+    a_side = move(tied(unit_in, o_side), p.x_all)
 
     gains = jnp.concatenate([pre_gain, post_gain, final_gain], axis=0).T
     order = jnp.repeat(CORES * ids + p.core, CORES)
@@ -563,7 +567,6 @@
     slots = jnp.argmax(
         order[None, :] == jnp.arange(shards, dtype=jnp.int32)[:, None], axis=1
     ).astype(jnp.int32)
-    mate_t = move(tied(hidden_t, unit_in), p.mate)
     chunks, next_chunks, last_chunks = prepare(
         jnp.concatenate([slots, core]), hidden_t, mate_t, gains[:, :1],
         (shards // 2, shards // 4, shards // 4),
@@ -573,12 +576,9 @@
     a_far = move(tied(a_near, a_side, chunks), p.z_mid)
     a_from_inner = move(tied(a_inner, a_side, chunks), p.z_out)
 
-    o_near = move(tied(unit_out, a_from_inner), p.z_pair)
-    o_inner = move(tied(unit_out, a_far), p.z_mid)
     a_round = move(a_from_inner + a_far, p.x_all)
     a_side_inner = move(tied(a_side, a_far), p.z_mid)
     a_from_far = move(tied(a_far, a_from_inner), p.z_out)
-    o_side = move(tied(unit_out, a_side_near), p.x_all)
     units = [[unit_in], [a_side], [a_near], [a_side_near]]
     acc = qkv_group(chunks, units, None, None)
 
@@ -599,7 +599,7 @@
         (next_chunks, judge_t, seg_q, seg_keys, *tables)
     )
 
-    done = (acc, o_near, o_inner, o_side, a_round, a_side_inner)
+    done = (acc, a_round, a_side_inner)
     a_x_fourth = move(tied(a_from_far, *done), p.x_end)
     o_far = move(tied(o_near, a_from_far, *done), p.z_mid)
     o_from_inner = move(tied(o_inner, a_from_far, *done), p.z_out)

time: 189 us -> 184 us (0.974)
  waiting for transfers between devices: 70.5 us -> 57.8 us
  local copies, waits for them, and re-layouts: 22 us -> 28.6 us
  starting transfers between devices: 37.7 us -> 40.6 us
  Pallas kernels: 50.7 us -> 48.8 us
    ppermute x26, waiting for transfers between devices: 67.2 us -> 54.4 us  [move(): return lax.ppermute(block, 'seq', route)]
    unnamed x67 -> x75, local copies, waits for them, and re-layouts: 18 us -> 23.6 us
    ppermute x26, starting transfers between devices: 36.2 us -> 39.1 us  [move(): return lax.ppermute(block, 'seq', route)]
  transfers between devices with their start and end apart: 27 -> 27, of which waited for: 13 -> 13; matrix products, arithmetic and copies ran while one was open for 5% -> 6% of each run, Pallas kernels for 22% -> 22%
where the time goes in v4:
time: 184 us; the launch traced here: 183 us
  waiting for transfers between devices  57.8 us (31%)
  Pallas kernels  48.8 us (27%)
  starting transfers between devices  40.6 us (22%)
  local copies, waits for them, and re-layouts  28.6 us (16%)
  other arithmetic  5.8 us (3%)
    ppermute x26, waiting for transfers between devices, move(): return lax.ppermute(block, 'seq', route)  54.4 us
    ppermute x26, starting transfers between devices, move(): return lax.ppermute(block, 'seq', route)  39.1 us
    unnamed x75, local copies, waits for them, and re-layouts  23.6 us
    pallas_call x3, Pallas kernels, qkv_group(): call(functools.partial(qkv_kernel, [len(unit) for unit in units], first,...  16.2 us
    pallas_call x2, Pallas kernels, attend(): call(attend_kernel, jax.ShapeDtypeStruct((q_wide, rows), jnp.bfloat16), 1...  9.42 us
    pallas_call x2, Pallas kernels, project(): call(functools.partial(out_kernel, [len(unit) for unit in units], acc is...  9.17 us
    pallas_call x1, Pallas kernels, prepare(): call(prepare_kernel, [jax.ShapeDtypeStruct((n, CORES * rows, depth), jnp....  8.7 us
    pallas_call x1, Pallas kernels, close(): call(close_kernel, (jax.ShapeDtypeStruct((width, half), jnp.bfloat16), ja...  4.43 us
  transfers between devices with their start and end apart: 27, of which 13 were waited for; matrix products, arithmetic and copies ran while one was open for 6% of the time, Pallas kernels for 22%

profile of v4, /device:TPU:0, one launch (start us, length us, event | category | flops | bytes accessed | tf_op | source)
XLA Modules:
  0.0 182.7 jit_solution(9674477301354629959)
XLA Ops:
  1.2 1.5 collective-permute-start.7
  2.7 2.5 %collective-permute-start.4 = (bf16[2880,128]{1,0:T(8,128)(2,1)}, bf16[2880,128]{1,0:T(8,128)(2,1)}, u32[]{:S(2)}, u32[]{:S(2)}) collective-permute-start(bf16[2880,128]{1,0:T(8,128)(2,1)} %bitcast.37), channel_id=1, source_target_pairs={{0,2},{1,3},{2,0},{3,1},{4,6},{5,7},{6,4},{7,5},{8,10},{9,11},{10,... | collective-permute-start | bytes 2211848 | tf_op jit(solution)/shard_map/ppermute | solution.py:506
  5.2 3.6 %collective-permute-start.2 = (bf16[2880,128]{1,0:T(8,128)(2,1)}, bf16[2880,128]{1,0:T(8,128)(2,1)}, u32[]{:S(2)}, u32[]{:S(2)}) collective-permute-start(bf16[2880,128]{1,0:T(8,128)(2,1)} %bitcast.38), channel_id=1, source_target_pairs={{0,4},{1,5},{2,6},{3,7},{4,0},{5,1},{6,2},{7,3},{8,12},{9,13},{10,... | collective-permute-start | bytes 2211848 | tf_op jit(solution)/shard_map/ppermute | solution.py:506
  8.8 1.6 copy-done.23
  14.1 1.1 constant_dynamic-update-slice_fusion.1
  17.3 5.4 %collective-permute-done.4.refs_1_ = bf16[2880,128]{1,0:T(8,128)(2,1)} collective-permute-done((bf16[2880,128]{1,0:T(8,128)(2,1)}, bf16[2880,128]{1,0:T(8,128)(2,1)}, u32[]{:S(2)}, u32[]{:S(2)}) %collective-permute-start.4) | collective-permute-done | bytes 737312 | tf_op jit(solution)/shard_map/ppermute | solution.py:506
  22.7 3.1 %collective-permute-done.2.refs_2_ = bf16[2880,128]{1,0:T(8,128)(2,1)} collective-permute-done((bf16[2880,128]{1,0:T(8,128)(2,1)}, bf16[2880,128]{1,0:T(8,128)(2,1)}, u32[]{:S(2)}, u32[]{:S(2)}) %collective-permute-start.2) | collective-permute-done | bytes 737312 | tf_op jit(solution)/shard_map/ppermute | solution.py:506
  25.7 1.7 collective-permute-start.3
  28.0 1.7 collective-permute-start.8
  31.2 1.6 copy-done.6
  32.9 1.6 copy-done.14
  34.5 8.7 %shard_map.113 = (bf16[8,768,180]{2,1,0:T(8,128)(2,1)S(1)}, bf16[4,768,180]{2,1,0:T(8,128)(2,1)S(1)}, bf16[4,768,180]{2,1,0:T(8,128)(2,1)S(1)}) custom-call(s32[17]{0:T(128)S(1)} %pad_add_fusion.2.slots_ref, bf16[2880,384]{1,0:T(8,128)(2,1)S(1)} %bitcast.32, bf16[2880,384]{1,0:T(8,128)(2,1)S(1)} %copy-done.14, f32[2880,1]{1,0:T(8,128)S(1)} %bitcast.29), custom_call_target="tpu_custom_call" | custom-call | flops 1000 | bytes 1000 | tf_op jit(solution)/shard_map/pallas_call | solution.py:247
  43.2 1.2 copy-done.17
  44.4 3.6 %collective-permute-done.3.refs_2_ = bf16[180,2560]{1,0:T(8,128)(2,1)} collective-permute-done((bf16[180,2560]{1,0:T(8,128)(2,1)S(1)}, bf16[180,2560]{1,0:T(8,128)(2,1)}, u32[]{:S(2)}, u32[]{:S(2)}) %collective-permute-start.3) | collective-permute-done | bytes 921632 | tf_op jit(solution)/shard_map/ppermute | solution.py:506
  48.0 1.1 collective-permute-done.5.refs_1_
  49.8 1.3 collective-permute-start.9
  52.5 20.6 %collective-permute-done.9.refs_1_ = bf16[180,2560]{1,0:T(8,128)(2,1)S(1)} collective-permute-done((bf16[180,2560]{1,0:T(8,128)(2,1)}, bf16[180,2560]{1,0:T(8,128)(2,1)S(1)}, u32[]{:S(2)}, u32[]{:S(2)}) %collective-permute-start.9) | collective-permute-done | bytes 921632 | tf_op jit(solution)/shard_map/ppermute | solution.py:506
  74.2 1.3 collective-permute-start.10
  75.5 6.3 %shard_map.115.refs_3_ = f32[768,1280]{1,0:T(8,128)S(1)} custom-call(bf16[8,768,180]{2,1,0:T(8,128)(2,1)S(1)} %get-tuple-element.44.chunks_ref, bf16[180,2560]{1,0:T(8,128)(2,1)S(1)} %constant_dynamic-update-slice_fusion.refs_0_, bf16[180,2560]{1,0:T(8,128)(2,1)} %collective-permute-done.5.refs_1_, bf16[180,2560]{1,0:T(8,128)(2,1)} %collective-permute-done.3.refs_2_, ...), custom_call_target="tpu_custom_call" | custom-call | flops 1000 | bytes 1000 | tf_op jit(solution)/shard_map/pallas_call | solution.py:321
  81.9 1.9 %copy-done = f32[768,1280]{1,0:T(8,128)} copy-done((f32[768,1280]{1,0:T(8,128)}, f32[768,1280]{1,0:T(8,128)S(1)}, u32[]{:S(2)}) %copy-start) | copy-done | bytes 3932184
  84.7 8.9 %collective-permute-done.13.refs_2_ = bf16[180,2560]{1,0:T(8,128)(2,1)S(1)} collective-permute-done((bf16[180,2560]{1,0:T(8,128)(2,1)S(1)}, bf16[180,2560]{1,0:T(8,128)(2,1)S(1)}, u32[]{:S(2)}, u32[]{:S(2)}) %collective-permute-start.13) | collective-permute-done | bytes 921632 | tf_op jit(solution)/shard_map/ppermute | solution.py:506
  94.5 1.5 collective-permute-done.10.refs_1_
  96.0 3.2 %collective-permute-start.14 = (bf16[180,2560]{1,0:T(8,128)(2,1)}, bf16[180,2560]{1,0:T(8,128)(2,1)}, u32[]{:S(2)}, u32[]{:S(2)}) collective-permute-start(bf16[180,2560]{1,0:T(8,128)(2,1)} %collective-permute-done.10.refs_1_), channel_id=1, source_target_pairs={{0,2},{1,3},{2,0},{3,1},{12,14},{13,15},{14,12},{15,13},{16,18},{1... | collective-permute-start | bytes 2764808 | tf_op jit(solution)/shard_map/ppermute | solution.py:506
  99.2 1.5 collective-permute-start.18
  100.7 1.3 collective-permute-start.20
  104.5 2.3 %copy.24 = bf16[1,2880,128]{1,2,0:T(8,128)(2,1)} copy(bf16[1,2880,128]{2,1,0:T(8,128)(2,1)} %param.19) | data formatting | bytes 1474560 | tf_op jit(solution)/shard_map/optimization_barrier | solution.py:153
  106.8 1.4 fusion
  108.3 2.1 %copy-done.1 = f32[768,1280]{1,0:T(8,128)S(1)} copy-done((f32[768,1280]{1,0:T(8,128)S(1)}, f32[768,1280]{1,0:T(8,128)}, u32[]{:S(2)}) %copy-start.1) | copy-done | bytes 3932184
  110.4 1.4 copy-done.18
  111.8 1.2 copy-done.22
  113.0 4.2 %shard_map.116.refs_4_ = f32[768,1280]{1,0:T(8,128)S(1)} custom-call(bf16[4,768,180]{2,1,0:T(8,128)(2,1)S(1)} %copy-done.18, bf16[180,2560]{1,0:T(8,128)(2,1)} %collective-permute-done.8.refs_0_, bf16[180,2560]{1,0:T(8,128)(2,1)S(1)} %collective-permute-done.9.refs_1_, bf16[180,2560]{1,0:T(8,128)(2,1)S(1)} %copy-done.22, f32[768,1280]{1,0:T(8,128)S(1)} %copy-done.1), custom_call_target="tpu_custom_call" | custom-call | flops 1000 | bytes 1000 | tf_op jit(solution)/shard_map/pallas_call | solution.py:321
  117.2 1.6 add.74
  119.8 1.3 collective-permute-start.19
  121.9 5.7 %shard_map.117.q_ref = bf16[768,1280]{1,0:T(8,128)(2,1)S(1)} custom-call(bf16[4,768,180]{2,1,0:T(8,128)(2,1)S(1)} %copy-done.16, bf16[180,2560]{1,0:T(8,128)(2,1)S(1)} %collective-permute-done.6.refs_0_, bf16[180,2560]{1,0:T(8,128)(2,1)} %collective-permute-done.10.refs_1_, bf16[180,2560]{1,0:T(8,128)(2,1)S(1)} %copy-done.20, ...), custom_call_target="tpu_custom_call" | custom-call | flops 1000 | bytes 1000 | tf_op jit(solution)/shard_map/pallas_call | solution.py:321
  127.7 1.7 collective-permute-done.15.mate0_ref.mate1_ref
  129.4 3.2 %collective-permute-start.16 = (bf16[128,512]{1,0:T(8,128)(2,1)S(1)}, bf16[128,512]{1,0:T(8,128)(2,1)S(1)}, u32[]{:S(2)}, u32[]{:S(2)}) collective-permute-start(bf16[128,512]{1,0:T(8,128)(2,1)S(1)} %pad_maximum_fusion), channel_id=1, source_target_pairs={{0,2},{1,3},{2,4},{3,5},{4,6},{5,7},{6,8},{7,9},{8,10},{9,11},{10,... | collective-permute-start | bytes 393224 | tf_op jit(solution)/shard_map/ppermute | solution.py:506
  132.6 1.5 collective-permute-start.23
  134.2 2.3 %collective-permute-done.16.own0_ref.mate0_ref = bf16[128,512]{1,0:T(8,128)(2,1)S(1)} collective-permute-done((bf16[128,512]{1,0:T(8,128)(2,1)S(1)}, bf16[128,512]{1,0:T(8,128)(2,1)S(1)}, u32[]{:S(2)}, u32[]{:S(2)}) %collective-permute-start.16) | collective-permute-done | bytes 131104 | tf_op jit(solution)/shard_map/ppermute | solution.py:506
  138.8 1.3 collective-permute-start.22
  140.1 6.4 %collective-permute-start.24 = (bf16[2880,128]{1,0:T(8,128)(2,1)}, bf16[2880,128]{1,0:T(8,128)(2,1)}, u32[]{:S(2)}, u32[]{:S(2)}) collective-permute-start(bf16[2880,128]{1,0:T(8,128)(2,1)} %collective-permute-done.19.refs_7_), channel_id=1, source_target_pairs={{0,2},{1,3},{2,0},{3,1},{12,14},{13,15},{14,12},{15,13},{16,18},{1... | collective-permute-start | bytes 2211848 | tf_op jit(solution)/shard_map/ppermute | solution.py:506
  146.6 7.9 %shard_map.118.out_refs_0_ = bf16[1024,768]{1,0:T(8,128)(2,1)S(1)} custom-call(s32[1]{0:T(128)} %bitcast.2.core_ref, bf16[768,1280]{1,0:T(8,128)(2,1)S(1)} %shard_map.117.q_ref, bf16[768,256]{1,0:T(8,128)(2,1)S(1)} %slice.17.own0_ref.own1_ref, bf16[768,256]{1,0:T(8,128)(2,1)S(1)} %slice.17.own0_ref.own1_ref, ...), custom_call_target="tpu_custom_call" | custom-call | flops 1000 | bytes 1000 | tf_op jit(solution)/shard_map/pallas_call | solution.py:402
  157.6 1.5 shard_map.119
  159.1 5.7 %shard_map.120.refs_4_ = f32[2880,768]{1,0:T(8,128)S(1)} custom-call(s32[7]{0:T(128)S(1)} %concatenate.30.ids_ref, bf16[8,128,768]{2,1,0:T(8,128)(2,1)S(1)} %bitcast.27, bf16[2880,128]{1,0:T(8,128)(2,1)S(1)} %bitcast.39, bf16[2880,128]{1,0:T(8,128)(2,1)} %collective-permute-done.4.refs_1_, bf16[2880,128]{1,0:T(8,128)(2,1)} %collective-permute-done.2.refs_2_, ...), custom_call_target="tpu_custom_call" | custom-call | flops 1000 | bytes 1000 | tf_op jit(solution)/shard_map/pallas_call | solution.py:453
  164.9 3.4 %shard_map.121 = (f32[2880,384]{1,0:T(8,128)S(1)}, bf16[2880,384]{1,0:T(8,128)(2,1)S(1)}) custom-call(s32[3]{0:T(128)S(1)} %pad_add_fusion.1.ids_ref, bf16[8,128,768]{2,1,0:T(8,128)(2,1)S(1)} %bitcast.28, bf16[2880,128]{1,0:T(8,128)(2,1)S(1)} %copy-done.28, bf16[2880,128]{1,0:T(8,128)(2,1)} %collective-permute-done.22.refs_1_, ...), custom_call_target="tpu_custom_call" | custom-call | flops 1000 | bytes 1000 | tf_op jit(solution)/shard_map/pallas_call | solution.py:453
  168.4 4.3 %collective-permute-done.25.mate_ref = bf16[2880,384]{1,0:T(8,128)(2,1)S(1)} collective-permute-done((bf16[2880,384]{1,0:T(8,128)(2,1)S(1)}, bf16[2880,384]{1,0:T(8,128)(2,1)S(1)}, u32[]{:S(2)}, u32[]{:S(2)}) %collective-permute-start.25) | collective-permute-done | bytes 2211872 | tf_op jit(solution)/shard_map/ppermute | solution.py:506
  172.8 4.4 %shard_map.122 = (bf16[2880,384]{1,0:T(8,128)(2,1)}, bf16[384,128]{1,0:T(8,128)(2,1)S(1)}) custom-call(f32[2880,384]{1,0:T(8,128)S(1)} %get-tuple-element.67.own_ref, bf16[2880,384]{1,0:T(8,128)(2,1)S(1)} %collective-permute-done.25.mate_ref, bf16[2880,384]{1,0:T(8,128)(2,1)S(1)} %bitcast.33, f32[2880,3]{1,0:T(8,128)S(1)} %bitcast.30, ...), custom_call_target="tpu_custom_call" | custom-call | flops 1000 | bytes 1000 | tf_op jit(solution)/shard_map/pallas_call | solution.py:493
  177.2 1.5 collective-permute-start.26
  178.7 3.3 %collective-permute-done.26 = bf16[384,128]{1,0:T(8,128)(2,1)S(1)} collective-permute-done((bf16[384,128]{1,0:T(8,128)(2,1)S(1)}, bf16[384,128]{1,0:T(8,128)(2,1)S(1)}, u32[]{:S(2)}, u32[]{:S(2)}) %collective-permute-start.26) | collective-permute-done | bytes 98336 | tf_op jit(solution)/shard_map/ppermute | solution.py:638
  (117 shorter events, 24.0 us)
Async XLA Ops:
  0.6 29.2 %copy-start.34 = (f32[1,2880]{1,0:T(1,128)S(1)}, f32[1,2880]{1,0:T(1,128)}, u32[]{:S(2)}) copy-start(f32[1,2880]{1,0:T(1,128)} %param.18) | copy-start | bytes 34564
  0.6 29.2 %copy-start.35 = (f32[1,2880]{1,0:T(1,128)S(1)}, f32[1,2880]{1,0:T(1,128)}, u32[]{:S(2)}) copy-start(f32[1,2880]{1,0:T(1,128)} %param.17) | copy-start | bytes 34564
  0.7 29.2 %copy-start.36 = (f32[1,2880]{1,0:T(1,128)S(1)}, f32[1,2880]{1,0:T(1,128)}, u32[]{:S(2)}) copy-start(f32[1,2880]{1,0:T(1,128)} %param.12) | copy-start | bytes 34564
  0.7 8.2 %collective-permute-start = (bf16[2880,384]{1,0:T(8,128)(2,1)}, bf16[2880,384]{1,0:T(8,128)(2,1)S(1)}, u32[]{:S(2)}, u32[]{:S(2)}) collective-permute-start(bf16[2880,384]{1,0:T(8,128)(2,1)} %bitcast.31), channel_id=1, source_target_pairs={{0,1},{1,0},{2,3},{3,2},{4,5},{5,4},{6,7},{7,6},{8,9},{9,8},{10,11... | collective-permute-start | bytes 6635528 | tf_op jit(solution)/shard_map/ppermute | solution.py:506
  1.2 16.1 %collective-permute-start.7 = (bf16[2880,128]{1,0:T(8,128)(2,1)}, bf16[2880,128]{1,0:T(8,128)(2,1)}, u32[]{:S(2)}, u32[]{:S(2)}) collective-permute-start(bf16[2880,128]{1,0:T(8,128)(2,1)} %bitcast.36), channel_id=1, source_target_pairs={{4,8},{5,9},{6,10},{7,11},{8,4},{9,5},{10,6},{11,7},{20,24},{21,25... | collective-permute-start | bytes 2211848 | tf_op jit(solution)/shard_map/ppermute | solution.py:506
  2.7 20.0 %collective-permute-start.4 = (bf16[2880,128]{1,0:T(8,128)(2,1)}, bf16[2880,128]{1,0:T(8,128)(2,1)}, u32[]{:S(2)}, u32[]{:S(2)}) collective-permute-start(bf16[2880,128]{1,0:T(8,128)(2,1)} %bitcast.37), channel_id=1, source_target_pairs={{0,2},{1,3},{2,0},{3,1},{4,6},{5,7},{6,4},{7,5},{8,10},{9,11},{10,... | collective-permute-start | bytes 2211848 | tf_op jit(solution)/shard_map/ppermute | solution.py:506
  5.2 20.5 %collective-permute-start.2 = (bf16[2880,128]{1,0:T(8,128)(2,1)}, bf16[2880,128]{1,0:T(8,128)(2,1)}, u32[]{:S(2)}, u32[]{:S(2)}) collective-permute-start(bf16[2880,128]{1,0:T(8,128)(2,1)} %bitcast.38), channel_id=1, source_target_pairs={{0,4},{1,5},{2,6},{3,7},{4,0},{5,1},{6,2},{7,3},{8,12},{9,13},{10,... | collective-permute-start | bytes 2211848 | tf_op jit(solution)/shard_map/ppermute | solution.py:506
  8.8 21.0 %copy-start.13 = (bf16[2880,384]{1,0:T(8,128)(2,1)}, bf16[2880,384]{1,0:T(8,128)(2,1)S(1)}, u32[]{:S(2)}) copy-start(bf16[2880,384]{1,0:T(8,128)(2,1)S(1)} %collective-permute-done.mate_ref) | copy-start | bytes 6635524
  8.8 1.6 copy-start.23
  14.0 2.2 %collective-permute-start.1 = (bf16[180,1280]{1,0:T(8,128)(2,1)}, bf16[180,1280]{1,0:T(8,128)(2,1)}, u32[]{:S(2)}, u32[]{:S(2)}) collective-permute-start(bf16[180,1280]{1,0:T(8,128)(2,1)} %get-tuple-element.41), channel_id=1, source_target_pairs={{0,1},{1,0},{2,3},{3,2},{4,5},{5,4},{6,7},{7,6},{8,9},{9,8},{10,11... | collective-permute-start | bytes 1382408 | tf_op jit(solution)/shard_map/ppermute | solution.py:506
  25.7 22.3 %collective-permute-start.3 = (bf16[180,2560]{1,0:T(8,128)(2,1)S(1)}, bf16[180,2560]{1,0:T(8,128)(2,1)}, u32[]{:S(2)}, u32[]{:S(2)}) collective-permute-start(bf16[180,2560]{1,0:T(8,128)(2,1)S(1)} %constant_dynamic-update-slice_fusion.refs_0_), channel_id=1, source_target_pairs={{0,4},{1,5},{2,6},{3,7},{4,0},{5,1},{6,2},{7,3},{8,12},{9,13},{10,... | collective-permute-start | bytes 2764808 | tf_op jit(solution)/shard_map/ppermute | solution.py:506
  27.5 21.7 %collective-permute-start.5 = (bf16[180,2560]{1,0:T(8,128)(2,1)S(1)}, bf16[180,2560]{1,0:T(8,128)(2,1)}, u32[]{:S(2)}, u32[]{:S(2)}) collective-permute-start(bf16[180,2560]{1,0:T(8,128)(2,1)S(1)} %constant_dynamic-update-slice_fusion.refs_0_), channel_id=1, source_target_pairs={{0,2},{1,3},{2,0},{3,1},{4,6},{5,7},{6,4},{7,5},{8,10},{9,11},{10,... | collective-permute-start | bytes 2764808 | tf_op jit(solution)/shard_map/ppermute | solution.py:506
  28.0 21.9 %collective-permute-start.8 = (bf16[180,2560]{1,0:T(8,128)(2,1)S(1)}, bf16[180,2560]{1,0:T(8,128)(2,1)}, u32[]{:S(2)}, u32[]{:S(2)}) collective-permute-start(bf16[180,2560]{1,0:T(8,128)(2,1)S(1)} %constant_dynamic-update-slice_fusion.refs_0_), channel_id=1, source_target_pairs={{4,8},{5,9},{6,10},{7,11},{8,4},{9,5},{10,6},{11,7},{20,24},{21,25... | collective-permute-start | bytes 2764808 | tf_op jit(solution)/shard_map/ppermute | solution.py:506
  30.4 12.8 %copy-start.2 = (f32[3,2880]{0,1:T(8,128)}, f32[3,2880]{0,1:T(8,128)S(1)}, u32[]{:S(2)}) copy-start(f32[3,2880]{0,1:T(8,128)S(1)} %copy.23) | copy-start | bytes 103684
  31.2 1.6 copy-start.6
  32.9 1.6 copy-start.14
  44.4 37.5 %copy-start.15 = (bf16[4,768,180]{2,1,0:T(8,128)(2,1)}, bf16[4,768,180]{2,1,0:T(8,128)(2,1)S(1)}, u32[]{:S(2)}) copy-start(bf16[4,768,180]{2,1,0:T(8,128)(2,1)S(1)} %get-tuple-element.38.chunks_ref) | copy-start | bytes 3317764
  49.1 2.7 %collective-permute-start.6 = (bf16[180,2560]{1,0:T(8,128)(2,1)}, bf16[180,2560]{1,0:T(8,128)(2,1)S(1)}, u32[]{:S(2)}, u32[]{:S(2)}) collective-permute-start(bf16[180,2560]{1,0:T(8,128)(2,1)} %collective-permute-done.3.refs_2_), channel_id=1, source_target_pairs={{4,8},{5,9},{6,10},{7,11},{8,4},{9,5},{10,6},{11,7},{20,24},{21,25... | collective-permute-start | bytes 2764808 | tf_op jit(solution)/shard_map/ppermute | solution.py:506
  49.8 23.3 %collective-permute-start.9 = (bf16[180,2560]{1,0:T(8,128)(2,1)}, bf16[180,2560]{1,0:T(8,128)(2,1)S(1)}, u32[]{:S(2)}, u32[]{:S(2)}) collective-permute-start(bf16[180,2560]{1,0:T(8,128)(2,1)} %collective-permute-done.8.refs_0_), channel_id=1, source_target_pairs={{4,0},{5,1},{6,2},{7,3},{8,12},{9,13},{10,14},{11,15},{20,16},{21,... | collective-permute-start | bytes 2764808 | tf_op jit(solution)/shard_map/ppermute | solution.py:506
  51.1 24.3 %collective-permute-start.12 = (bf16[180,2560]{1,0:T(8,128)(2,1)}, bf16[180,2560]{1,0:T(8,128)(2,1)S(1)}, u32[]{:S(2)}, u32[]{:S(2)}) collective-permute-start(bf16[180,2560]{1,0:T(8,128)(2,1)} %collective-permute-done.3.refs_2_), channel_id=1, source_target_pairs={{0,2},{1,3},{2,0},{3,1},{4,6},{5,7},{6,4},{7,5},{8,10},{9,11},{10,... | collective-permute-start | bytes 2764808 | tf_op jit(solution)/shard_map/ppermute | solution.py:506
  51.8 31.9 %collective-permute-start.11 = (bf16[180,2560]{1,0:T(8,128)(2,1)}, bf16[180,2560]{1,0:T(8,128)(2,1)S(1)}, u32[]{:S(2)}, u32[]{:S(2)}) collective-permute-start(bf16[180,2560]{1,0:T(8,128)(2,1)} %collective-permute-done.5.refs_1_), channel_id=1, source_target_pairs={{4,8},{5,9},{6,10},{7,11},{8,4},{9,5},{10,6},{11,7},{20,24},{21,25... | collective-permute-start | bytes 2764808 | tf_op jit(solution)/shard_map/ppermute | solution.py:506
  73.5 20.1 %collective-permute-start.13 = (bf16[180,2560]{1,0:T(8,128)(2,1)S(1)}, bf16[180,2560]{1,0:T(8,128)(2,1)S(1)}, u32[]{:S(2)}, u32[]{:S(2)}) collective-permute-start(bf16[180,2560]{1,0:T(8,128)(2,1)S(1)} %add.68), channel_id=1, source_target_pairs={{0,2},{1,3},{2,0},{3,1},{4,6},{5,7},{6,4},{7,5},{8,10},{9,11},{10,... | collective-permute-start | bytes 2764808 | tf_op jit(solution)/shard_map/ppermute | solution.py:506
  74.2 21.8 %collective-permute-start.10 = (bf16[180,2560]{1,0:T(8,128)(2,1)S(1)}, bf16[180,2560]{1,0:T(8,128)(2,1)}, u32[]{:S(2)}, u32[]{:S(2)}) collective-permute-start(bf16[180,2560]{1,0:T(8,128)(2,1)S(1)} %collective-permute-done.6.refs_0_), channel_id=1, source_target_pairs={{4,0},{5,1},{6,2},{7,3},{8,12},{9,13},{10,14},{11,15},{20,16},{21,... | collective-permute-start | bytes 2764808 | tf_op jit(solution)/shard_map/ppermute | solution.py:506
  81.8 1.9 %copy-start = (f32[768,1280]{1,0:T(8,128)}, f32[768,1280]{1,0:T(8,128)S(1)}, u32[]{:S(2)}) copy-start(f32[768,1280]{1,0:T(8,128)S(1)} %shard_map.115.refs_3_) | copy-start | bytes 11796484
  96.0 23.8 %collective-permute-start.14 = (bf16[180,2560]{1,0:T(8,128)(2,1)}, bf16[180,2560]{1,0:T(8,128)(2,1)}, u32[]{:S(2)}, u32[]{:S(2)}) collective-permute-start(bf16[180,2560]{1,0:T(8,128)(2,1)} %collective-permute-done.10.refs_1_), channel_id=1, source_target_pairs={{0,2},{1,3},{2,0},{3,1},{12,14},{13,15},{14,12},{15,13},{16,18},{1... | collective-permute-start | bytes 2764808 | tf_op jit(solution)/shard_map/ppermute | solution.py:506
  99.2 18.0 %collective-permute-start.18 = (bf16[2880,128]{1,0:T(8,128)(2,1)}, bf16[2880,128]{1,0:T(8,128)(2,1)}, u32[]{:S(2)}, u32[]{:S(2)}) collective-permute-start(bf16[2880,128]{1,0:T(8,128)(2,1)} %collective-permute-done.2.refs_2_), channel_id=1, source_target_pairs={{4,8},{5,9},{6,10},{7,11},{8,4},{9,5},{10,6},{11,7},{20,24},{21,25... | collective-permute-start | bytes 2211848 | tf_op jit(solution)/shard_map/ppermute | solution.py:506
  100.7 16.5 %collective-permute-start.20 = (bf16[2880,128]{1,0:T(8,128)(2,1)}, bf16[2880,128]{1,0:T(8,128)(2,1)S(1)}, u32[]{:S(2)}, u32[]{:S(2)}) collective-permute-start(bf16[2880,128]{1,0:T(8,128)(2,1)} %collective-permute-done.7.refs_3_), channel_id=1, source_target_pairs={{4,0},{5,1},{6,2},{7,3},{8,12},{9,13},{10,14},{11,15},{20,16},{21,... | collective-permute-start | bytes 2211848 | tf_op jit(solution)/shard_map/ppermute | solution.py:506
  102.0 16.8 %collective-permute-start.17 = (bf16[2880,128]{1,0:T(8,128)(2,1)}, bf16[2880,128]{1,0:T(8,128)(2,1)S(1)}, u32[]{:S(2)}, u32[]{:S(2)}) collective-permute-start(bf16[2880,128]{1,0:T(8,128)(2,1)} %collective-permute-done.2.refs_2_), channel_id=1, source_target_pairs={{4,6},{5,7},{6,4},{7,5},{8,10},{9,11},{10,8},{11,9},{20,22},{21,23... | collective-permute-start | bytes 2211848 | tf_op jit(solution)/shard_map/ppermute | solution.py:506
  108.3 2.1 %copy-start.1 = (f32[768,1280]{1,0:T(8,128)S(1)}, f32[768,1280]{1,0:T(8,128)}, u32[]{:S(2)}) copy-start(f32[768,1280]{1,0:T(8,128)} %copy-done) | copy-start | bytes 11796484
  113.0 8.9 %copy-start.20 = (bf16[180,2560]{1,0:T(8,128)(2,1)S(1)}, bf16[180,2560]{1,0:T(8,128)(2,1)}, u32[]{:S(2)}) copy-start(bf16[180,2560]{1,0:T(8,128)(2,1)} %copy-done.19) | copy-start | bytes 2764804
  117.2 4.7 %copy-start.16 = (bf16[4,768,180]{2,1,0:T(8,128)(2,1)S(1)}, bf16[4,768,180]{2,1,0:T(8,128)(2,1)}, u32[]{:S(2)}) copy-start(bf16[4,768,180]{2,1,0:T(8,128)(2,1)} %copy-done.15) | copy-start | bytes 3317764
  117.2 4.7 %copy-start.11 = (bf16[2880,128]{1,0:T(8,128)(2,1)}, bf16[2880,128]{1,0:T(8,128)(2,1)S(1)}, u32[]{:S(2)}) copy-start(bf16[2880,128]{1,0:T(8,128)(2,1)S(1)} %collective-permute-done.20.refs_4_) | copy-start | bytes 2211844
  119.8 18.1 %collective-permute-start.19 = (bf16[2880,128]{1,0:T(8,128)(2,1)}, bf16[2880,128]{1,0:T(8,128)(2,1)}, u32[]{:S(2)}, u32[]{:S(2)}) collective-permute-start(bf16[2880,128]{1,0:T(8,128)(2,1)} %collective-permute-done.18.refs_6_), channel_id=1, source_target_pairs={{4,0},{5,1},{6,2},{7,3},{8,12},{9,13},{10,14},{11,15},{20,16},{21,... | collective-permute-start | bytes 2211848 | tf_op jit(solution)/shard_map/ppermute | solution.py:506
  121.1 16.9 %collective-permute-start.21 = (bf16[2880,128]{1,0:T(8,128)(2,1)S(1)}, bf16[2880,128]{1,0:T(8,128)(2,1)S(1)}, u32[]{:S(2)}, u32[]{:S(2)}) collective-permute-start(bf16[2880,128]{1,0:T(8,128)(2,1)S(1)} %add.74), channel_id=1, source_target_pairs={{0,2},{1,3},{2,0},{3,1},{4,6},{5,7},{6,4},{7,5},{8,10},{9,11},{10,... | collective-permute-start | bytes 2211848 | tf_op jit(solution)/shard_map/ppermute | solution.py:506
  127.6 19.0 %copy-start.4 = (bf16[768,256]{1,0:T(8,128)(2,1)}, bf16[768,256]{1,0:T(8,128)(2,1)S(1)}, u32[]{:S(2)}) copy-start(bf16[768,256]{1,0:T(8,128)(2,1)S(1)} %slice.17.own0_ref.own1_ref) | copy-start | bytes 1179652
  127.6 1.8 collective-permute-start.15
  129.4 17.2 %copy-start.8 = (bf16[768,256]{1,0:T(8,128)(2,1)}, bf16[768,256]{1,0:T(8,128)(2,1)S(1)}, u32[]{:S(2)}) copy-start(bf16[768,256]{1,0:T(8,128)(2,1)S(1)} %collective-permute-done.15.mate0_ref.mate1_ref) | copy-start | bytes 1179652
  129.4 7.0 %collective-permute-start.16 = (bf16[128,512]{1,0:T(8,128)(2,1)S(1)}, bf16[128,512]{1,0:T(8,128)(2,1)S(1)}, u32[]{:S(2)}, u32[]{:S(2)}) collective-permute-start(bf16[128,512]{1,0:T(8,128)(2,1)S(1)} %pad_maximum_fusion), channel_id=1, source_target_pairs={{0,2},{1,3},{2,4},{3,5},{4,6},{5,7},{6,8},{7,9},{8,10},{9,11},{10,... | collective-permute-start | bytes 393224 | tf_op jit(solution)/shard_map/ppermute | solution.py:506
  132.6 32.3 %collective-permute-start.23 = (bf16[2880,128]{1,0:T(8,128)(2,1)}, bf16[2880,128]{1,0:T(8,128)(2,1)}, u32[]{:S(2)}, u32[]{:S(2)}) collective-permute-start(bf16[2880,128]{1,0:T(8,128)(2,1)} %collective-permute-done.4.refs_1_), channel_id=1, source_target_pairs={{4,8},{5,9},{6,10},{7,11},{8,4},{9,5},{10,6},{11,7},{20,24},{21,25... | collective-permute-start | bytes 2211848 | tf_op jit(solution)/shard_map/ppermute | solution.py:506
  138.8 26.1 %collective-permute-start.22 = (bf16[2880,128]{1,0:T(8,128)(2,1)}, bf16[2880,128]{1,0:T(8,128)(2,1)}, u32[]{:S(2)}, u32[]{:S(2)}) collective-permute-start(bf16[2880,128]{1,0:T(8,128)(2,1)} %collective-permute-done.4.refs_1_), channel_id=1, source_target_pairs={{4,0},{5,1},{6,2},{7,3},{8,12},{9,13},{10,14},{11,15},{20,16},{21,... | collective-permute-start | bytes 2211848 | tf_op jit(solution)/shard_map/ppermute | solution.py:506
  140.1 24.8 %collective-permute-start.24 = (bf16[2880,128]{1,0:T(8,128)(2,1)}, bf16[2880,128]{1,0:T(8,128)(2,1)}, u32[]{:S(2)}, u32[]{:S(2)}) collective-permute-start(bf16[2880,128]{1,0:T(8,128)(2,1)} %collective-permute-done.19.refs_7_), channel_id=1, source_target_pairs={{0,2},{1,3},{2,0},{3,1},{12,14},{13,15},{14,12},{15,13},{16,18},{1... | collective-permute-start | bytes 2211848 | tf_op jit(solution)/shard_map/ppermute | solution.py:506
  157.6 1.6 copy-start.26
  159.1 5.8 %copy-start.28 = (bf16[2880,128]{1,0:T(8,128)(2,1)S(1)}, bf16[2880,128]{1,0:T(8,128)(2,1)}, u32[]{:S(2)}) copy-start(bf16[2880,128]{1,0:T(8,128)(2,1)} %copy-done.27) | copy-start | bytes 2211844
  164.9 7.9 %copy-start.3 = (f32[3,2880]{0,1:T(8,128)S(1)}, f32[3,2880]{0,1:T(8,128)}, u32[]{:S(2)}) copy-start(f32[3,2880]{0,1:T(8,128)} %copy-done.2) | copy-start | bytes 103684
  164.9 7.9 %copy-start.7 = (bf16[1,384,2880]{1,2,0:T(8,128)(2,1)S(1)}, bf16[1,384,2880]{1,2,0:T(8,128)(2,1)}, u32[]{:S(2)}) copy-start(bf16[1,384,2880]{1,2,0:T(8,128)(2,1)} %param.10) | copy-start | bytes 6635524
  164.9 7.9 %copy-start.10 = (bf16[1,2880,128]{1,2,0:T(8,128)(2,1)S(1)}, bf16[1,2880,128]{1,2,0:T(8,128)(2,1)}, u32[]{:S(2)}) copy-start(bf16[1,2880,128]{1,2,0:T(8,128)(2,1)} %copy.24) | copy-start | bytes 2211844
  168.4 4.4 %collective-permute-start.25 = (bf16[2880,384]{1,0:T(8,128)(2,1)S(1)}, bf16[2880,384]{1,0:T(8,128)(2,1)S(1)}, u32[]{:S(2)}, u32[]{:S(2)}) collective-permute-start(bf16[2880,384]{1,0:T(8,128)(2,1)S(1)} %get-tuple-element.68), channel_id=1, source_target_pairs={{0,1},{1,0},{2,3},{3,2},{4,5},{5,4},{6,7},{7,6},{8,9},{9,8},{10,11... | collective-permute-start | bytes 6635528 | tf_op jit(solution)/shard_map/ppermute | solution.py:506
  177.2 4.8 %collective-permute-start.26 = (bf16[384,128]{1,0:T(8,128)(2,1)S(1)}, bf16[384,128]{1,0:T(8,128)(2,1)S(1)}, u32[]{:S(2)}, u32[]{:S(2)}) collective-permute-start(bf16[384,128]{1,0:T(8,128)(2,1)S(1)} %get-tuple-element.71), channel_id=1, source_target_pairs={{0,16},{16,0},{1,17},{17,1},{2,18},{18,2},{3,19},{19,3},{4,20},{20... | collective-permute-start | bytes 294920 | tf_op jit(solution)/shard_map/ppermute | solution.py:638
  (16 other events, 16.7 us)

commit v5 on v4

--- a/solution.py
+++ b/solution.py
@@ -277,11 +277,12 @@
         total = None if first else acc_ref[:, pl.ds(at, step)]
         for k, parts in enumerate(units):
             for side in range(CORES):
-                cols = pl.ds(at + side * wide, step)
-                w = parts[0][:, cols]
+                x = chunks_ref[CORES * k + side]
+                depth = x.shape[1]
+                rows, cols = slice(side * depth, (side + 1) * depth), pl.ds(at, step)
+                w = parts[0][rows, cols]
                 for extra in parts[1:]:
-                    w = w + extra[:, cols]
-                x = chunks_ref[CORES * k + side]
+                    w = w + extra[rows, cols]
                 part = jnp.dot(x, w, preferred_element_type=jnp.float32)
                 total = part if total is None else total + part
         return total
@@ -311,7 +312,7 @@
 
 def qkv_group(chunks, units, acc, tables):
     rows = chunks.shape[1]
-    wide = units[0][0].shape[1] // CORES
+    wide = units[0][0].shape[1]
     first, last = acc is None, tables is not None
     operands = [chunks] + [part for unit in units for part in unit]
     if not first:
@@ -556,7 +557,7 @@
     o_inner = move(unit_out, p.z_mid)
     mate_t = move(hidden_t, p.mate)
     mine, other = halves(core, tied(w_query, mate_t)[0], w_key[0], w_value[0])
-    unit_in = jnp.concatenate([mine, move(other, p.mate)], axis=1)
+    unit_in = jnp.concatenate([mine, move(other, p.mate)], axis=0)
     a_inner = move(tied(unit_in, o_inner), p.z_mid)
     a_near = move(tied(unit_in, o_near), p.z_pair)
     a_side = move(tied(unit_in, o_side), p.x_all)
@@ -609,7 +610,6 @@
     done = (a_x_fourth, o_x_near, acc)
     o_round = move(tied(o_from_inner + o_far, *done), p.x_all)
     o_from_far = move(tied(o_far, *done), p.z_out)
-    o_side_inner = move(tied(o_side, *done), p.z_mid)
     units = [[a_far, a_from_far], [a_side_inner, a_x_fourth]]
     qkv = qkv_group(last_chunks, units, acc, tables)
     own_kv = qkv[:, QH * HD // CORES :]
@@ -620,14 +620,14 @@
     attended = attend(core, qkv, own_kv, mate_kv, None, seg_q, seg_keys, None)
 
     done = (o_round, halo)
-    o_x_fourth = move(tied(o_from_far, *done), p.x_end)
+    o_last = move(tied(o_from_far + o_inner, *done), p.x_all)
     o_z_side = move(tied(o_side, o_from_far, *done), p.z_out)
     attended = attend(core, qkv, own_kv, mate_kv, halo, seg_q, seg_keys, attended)
     attended = attended.reshape(shards // CORES, -1, chip_rows)
 
     units = [[unit_out], [o_side], [o_near], [o_inner, o_from_inner], [o_round], [o_far, o_from_far]]
     acc = project(jnp.concatenate([ids[:3], ids[4:7], core]), attended, units, None, False)
-    units = [[o_x_near, o_z_side], [o_side_inner, o_x_fourth]]
+    units = [[o_x_near, o_z_side], [o_last]]
     own, mate = project(jnp.concatenate([ids[3:4], ids[7:], core]), attended, units, acc, True)
     updated, verdict = close(own, move(mate, p.mate), hidden_t, gains, judge_t)
 

time: 184 us -> 180 us (0.978)
  starting transfers between devices: 40.6 us -> 34 us
  waiting for transfers between devices: 57.8 us -> 61.2 us
  other arithmetic: 5.8 us -> 8.32 us
  local copies, waits for them, and re-layouts: 28.6 us -> 26.7 us
    ppermute x26 -> x25, starting transfers between devices: 39.1 us -> 32.4 us  [move(): return lax.ppermute(block, 'seq', route)]
    ppermute x26 -> x25, waiting for transfers between devices: 54.4 us -> 57.9 us  [move(): return lax.ppermute(block, 'seq', route)]
    add x0 -> x1, other arithmetic: none -> 2.44 us  [planned_body(): o_last = move(tied(o_from_far + o_inner, *done), p.x_all)]
    unnamed x75 -> x76, local copies, waits for them, and re-layouts: 23.6 us -> 22.8 us
  transfers between devices with their start and end apart: 27 -> 26, of which waited for: 13 -> 12; matrix products, arithmetic and copies ran while one was open for 6% -> 6% of each run, Pallas kernels for 22% -> 22%
where the time goes in v5:
time: 180 us; the launch traced here: 179 us
  waiting for transfers between devices  61.2 us (34%)
  Pallas kernels  47.4 us (26%)
  starting transfers between devices  34 us (19%)
  local copies, waits for them, and re-layouts  26.7 us (15%)
  other arithmetic  8.32 us (5%)
    ppermute x25, waiting for transfers between devices, move(): return lax.ppermute(block, 'seq', route)  57.9 us
    ppermute x25, starting transfers between devices, move(): return lax.ppermute(block, 'seq', route)  32.4 us
    unnamed x76, local copies, waits for them, and re-layouts  22.8 us
    pallas_call x3, Pallas kernels, qkv_group(): call(functools.partial(qkv_kernel, [len(unit) for unit in units], first,...  16.2 us
    pallas_call x2, Pallas kernels, attend(): call(attend_kernel, jax.ShapeDtypeStruct((q_wide, rows), jnp.bfloat16), 1...  9.42 us
    pallas_call x1, Pallas kernels, prepare(): call(prepare_kernel, [jax.ShapeDtypeStruct((n, CORES * rows, depth), jnp....  8.7 us
    pallas_call x2, Pallas kernels, project(): call(functools.partial(out_kernel, [len(unit) for unit in units], acc is...  8.6 us
    pallas_call x1, Pallas kernels, close(): call(close_kernel, (jax.ShapeDtypeStruct((width, half), jnp.bfloat16), ja...  4.32 us
  transfers between devices with their start and end apart: 26, of which 12 were waited for; matrix products, arithmetic and copies ran while one was open for 6% of the time, Pallas kernels for 22%

profile of v5, /device:TPU:0, one launch (start us, length us, event | category | flops | bytes accessed | tf_op | source)
XLA Modules:
  0.0 178.8 jit_solution(8763010952569073958)
XLA Ops:
  1.2 1.5 collective-permute-start.7
  2.7 2.5 %collective-permute-start.4 = (bf16[2880,128]{1,0:T(8,128)(2,1)}, bf16[2880,128]{1,0:T(8,128)(2,1)}, u32[]{:S(2)}, u32[]{:S(2)}) collective-permute-start(bf16[2880,128]{1,0:T(8,128)(2,1)} %bitcast.37), channel_id=1, source_target_pairs={{0,2},{1,3},{2,0},{3,1},{4,6},{5,7},{6,4},{7,5},{8,10},{9,11},{10,... | collective-permute-start | bytes 2211848 | tf_op jit(solution)/shard_map/ppermute | solution.py:507
  5.2 3.6 %collective-permute-start.2 = (bf16[2880,128]{1,0:T(8,128)(2,1)}, bf16[2880,128]{1,0:T(8,128)(2,1)}, u32[]{:S(2)}, u32[]{:S(2)}) collective-permute-start(bf16[2880,128]{1,0:T(8,128)(2,1)} %bitcast.38), channel_id=1, source_target_pairs={{0,4},{1,5},{2,6},{3,7},{4,0},{5,1},{6,2},{7,3},{8,12},{9,13},{10,... | collective-permute-start | bytes 2211848 | tf_op jit(solution)/shard_map/ppermute | solution.py:507
  8.8 1.4 copy-done.15
  10.2 1.1 copy-done.25
  13.5 1.7 collective-permute-done.1
  15.3 7.4 %collective-permute-done.4.refs_1_ = bf16[2880,128]{1,0:T(8,128)(2,1)} collective-permute-done((bf16[2880,128]{1,0:T(8,128)(2,1)}, bf16[2880,128]{1,0:T(8,128)(2,1)}, u32[]{:S(2)}, u32[]{:S(2)}) %collective-permute-start.4) | collective-permute-done | bytes 737312 | tf_op jit(solution)/shard_map/ppermute | solution.py:507
  22.7 3.1 %collective-permute-done.2.refs_2_ = bf16[2880,128]{1,0:T(8,128)(2,1)} collective-permute-done((bf16[2880,128]{1,0:T(8,128)(2,1)}, bf16[2880,128]{1,0:T(8,128)(2,1)}, u32[]{:S(2)}, u32[]{:S(2)}) %collective-permute-start.2) | collective-permute-done | bytes 737312 | tf_op jit(solution)/shard_map/ppermute | solution.py:507
  25.7 1.7 collective-permute-start.3
  28.0 1.7 collective-permute-start.8
  31.2 1.6 copy-done.6
  32.8 1.6 copy-done.16
  34.5 8.7 %shard_map.113 = (bf16[8,768,180]{2,1,0:T(8,128)(2,1)S(1)}, bf16[4,768,180]{2,1,0:T(8,128)(2,1)S(1)}, bf16[4,768,180]{2,1,0:T(8,128)(2,1)S(1)}) custom-call(s32[17]{0:T(128)S(1)} %pad_add_fusion.2.slots_ref, bf16[2880,384]{1,0:T(8,128)(2,1)S(1)} %bitcast.32, bf16[2880,384]{1,0:T(8,128)(2,1)S(1)} %copy-done.16, f32[2880,1]{1,0:T(8,128)S(1)} %bitcast.29), custom_call_target="tpu_custom_call" | custom-call | flops 1000 | bytes 1000 | tf_op jit(solution)/shard_map/pallas_call | solution.py:247
  43.2 1.1 copy-done.19
  44.3 3.2 %collective-permute-done.3.refs_2_ = bf16[360,1280]{1,0:T(8,128)(2,1)} collective-permute-done((bf16[360,1280]{1,0:T(8,128)(2,1)S(1)}, bf16[360,1280]{1,0:T(8,128)(2,1)}, u32[]{:S(2)}, u32[]{:S(2)}) %collective-permute-start.3) | collective-permute-done | bytes 921632 | tf_op jit(solution)/shard_map/ppermute | solution.py:507
  49.4 1.3 collective-permute-start.9
  52.1 20.2 %collective-permute-done.9.refs_1_ = bf16[360,1280]{1,0:T(8,128)(2,1)S(1)} collective-permute-done((bf16[360,1280]{1,0:T(8,128)(2,1)}, bf16[360,1280]{1,0:T(8,128)(2,1)S(1)}, u32[]{:S(2)}, u32[]{:S(2)}) %collective-permute-start.9) | collective-permute-done | bytes 921632 | tf_op jit(solution)/shard_map/ppermute | solution.py:507
  73.3 1.3 collective-permute-start.10
  74.6 6.3 %shard_map.115.refs_3_ = f32[768,1280]{1,0:T(8,128)S(1)} custom-call(bf16[8,768,180]{2,1,0:T(8,128)(2,1)S(1)} %get-tuple-element.43.chunks_ref, bf16[360,1280]{1,0:T(8,128)(2,1)S(1)} %pad_maximum_fusion.refs_0_, bf16[360,1280]{1,0:T(8,128)(2,1)} %collective-permute-done.5.refs_1_, bf16[360,1280]{1,0:T(8,128)(2,1)} %collective-permute-done.3.refs_2_, ...), custom_call_target="tpu_custom_call" | custom-call | flops 1000 | bytes 1000 | tf_op jit(solution)/shard_map/pallas_call | solution.py:322
  81.0 1.9 %copy-done = f32[768,1280]{1,0:T(8,128)} copy-done((f32[768,1280]{1,0:T(8,128)}, f32[768,1280]{1,0:T(8,128)S(1)}, u32[]{:S(2)}) %copy-start) | copy-done | bytes 3932184
  83.8 8.4 %collective-permute-done.13.refs_2_ = bf16[360,1280]{1,0:T(8,128)(2,1)S(1)} collective-permute-done((bf16[360,1280]{1,0:T(8,128)(2,1)S(1)}, bf16[360,1280]{1,0:T(8,128)(2,1)S(1)}, u32[]{:S(2)}, u32[]{:S(2)}) %collective-permute-start.13) | collective-permute-done | bytes 921632 | tf_op jit(solution)/shard_map/ppermute | solution.py:507
  93.1 1.5 collective-permute-done.10.refs_1_
  94.7 3.2 %collective-permute-start.14 = (bf16[360,1280]{1,0:T(8,128)(2,1)}, bf16[360,1280]{1,0:T(8,128)(2,1)}, u32[]{:S(2)}, u32[]{:S(2)}) collective-permute-start(bf16[360,1280]{1,0:T(8,128)(2,1)} %collective-permute-done.10.refs_1_), channel_id=1, source_target_pairs={{0,2},{1,3},{2,0},{3,1},{12,14},{13,15},{14,12},{15,13},{16,18},{1... | collective-permute-start | bytes 2764808 | tf_op jit(solution)/shard_map/ppermute | solution.py:507
  97.8 1.5 collective-permute-start.18
  99.4 1.3 collective-permute-start.20
  103.2 2.3 %copy.24 = bf16[1,2880,128]{1,2,0:T(8,128)(2,1)} copy(bf16[1,2880,128]{2,1,0:T(8,128)(2,1)} %param.19) | data formatting | bytes 1474560 | tf_op jit(solution)/shard_map/optimization_barrier | solution.py:153
  105.5 1.4 fusion
  106.9 2.1 %copy-done.1 = f32[768,1280]{1,0:T(8,128)S(1)} copy-done((f32[768,1280]{1,0:T(8,128)S(1)}, f32[768,1280]{1,0:T(8,128)}, u32[]{:S(2)}) %copy-start.1) | copy-done | bytes 3932184
  109.1 1.4 copy-done.18
  110.5 1.2 copy-done.24
  111.6 4.2 %shard_map.116.refs_4_ = f32[768,1280]{1,0:T(8,128)S(1)} custom-call(bf16[4,768,180]{2,1,0:T(8,128)(2,1)S(1)} %copy-done.18, bf16[360,1280]{1,0:T(8,128)(2,1)} %collective-permute-done.8.refs_0_, bf16[360,1280]{1,0:T(8,128)(2,1)S(1)} %collective-permute-done.9.refs_1_, bf16[360,1280]{1,0:T(8,128)(2,1)S(1)} %copy-done.24, f32[768,1280]{1,0:T(8,128)S(1)} %copy-done.1), custom_call_target="tpu_custom_call" | custom-call | flops 1000 | bytes 1000 | tf_op jit(solution)/shard_map/pallas_call | solution.py:322
  115.9 1.6 add.77
  118.5 1.3 collective-permute-start.19
  120.6 5.6 %shard_map.117.q_ref = bf16[768,1280]{1,0:T(8,128)(2,1)S(1)} custom-call(bf16[4,768,180]{2,1,0:T(8,128)(2,1)S(1)} %copy-done.20, bf16[360,1280]{1,0:T(8,128)(2,1)S(1)} %collective-permute-done.6.refs_0_, bf16[360,1280]{1,0:T(8,128)(2,1)} %collective-permute-done.10.refs_1_, bf16[360,1280]{1,0:T(8,128)(2,1)S(1)} %copy-done.22, ...), custom_call_target="tpu_custom_call" | custom-call | flops 1000 | bytes 1000 | tf_op jit(solution)/shard_map/pallas_call | solution.py:322
  126.3 1.7 collective-permute-done.15.mate0_ref.mate1_ref
  128.1 3.2 %collective-permute-start.16 = (bf16[128,512]{1,0:T(8,128)(2,1)S(1)}, bf16[128,512]{1,0:T(8,128)(2,1)S(1)}, u32[]{:S(2)}, u32[]{:S(2)}) collective-permute-start(bf16[128,512]{1,0:T(8,128)(2,1)S(1)} %pad_maximum_fusion.1), channel_id=1, source_target_pairs={{0,2},{1,3},{2,4},{3,5},{4,6},{5,7},{6,8},{7,9},{8,10},{9,11},{10,... | collective-permute-start | bytes 393224 | tf_op jit(solution)/shard_map/ppermute | solution.py:507
  131.3 5.2 %collective-permute-done.19.refs_7_ = bf16[2880,128]{1,0:T(8,128)(2,1)S(1)} collective-permute-done((bf16[2880,128]{1,0:T(8,128)(2,1)}, bf16[2880,128]{1,0:T(8,128)(2,1)S(1)}, u32[]{:S(2)}, u32[]{:S(2)}) %collective-permute-start.19) | collective-permute-done | bytes 737312 | tf_op jit(solution)/shard_map/ppermute | solution.py:507
  136.5 2.4 %add.78 = bf16[2880,128]{1,0:T(8,128)(2,1)} add(bf16[2880,128]{1,0:T(8,128)(2,1)S(1)} %collective-permute-done.19.refs_7_, bf16[2880,128]{1,0:T(8,128)(2,1)} %collective-permute-done.7.refs_3_) | non-fusion elementwise | flops 368640 | bytes 2211840 | tf_op jit(solution)/shard_map/add | solution.py:623
  140.5 1.3 collective-permute-start.22
  141.8 1.3 collective-permute-start.23
  143.2 7.9 %shard_map.118.out_refs_0_ = bf16[1024,768]{1,0:T(8,128)(2,1)S(1)} custom-call(s32[1]{0:T(128)} %bitcast.2.core_ref, bf16[768,1280]{1,0:T(8,128)(2,1)S(1)} %shard_map.117.q_ref, bf16[768,256]{1,0:T(8,128)(2,1)S(1)} %slice.17.own0_ref.own1_ref, bf16[768,256]{1,0:T(8,128)(2,1)S(1)} %slice.17.own0_ref.own1_ref, ...), custom_call_target="tpu_custom_call" | custom-call | flops 1000 | bytes 1000 | tf_op jit(solution)/shard_map/pallas_call | solution.py:403
  154.1 1.5 shard_map.119
  155.8 5.5 %shard_map.120.refs_3_ = f32[2880,768]{1,0:T(8,128)S(1)} custom-call(s32[7]{0:T(128)S(1)} %concatenate.30.ids_ref, bf16[8,128,768]{2,1,0:T(8,128)(2,1)S(1)} %bitcast.27, bf16[2880,128]{1,0:T(8,128)(2,1)S(1)} %bitcast.39, bf16[2880,128]{1,0:T(8,128)(2,1)} %collective-permute-done.4.refs_1_, bf16[2880,128]{1,0:T(8,128)(2,1)} %collective-permute-done.2.refs_2_, ...), custom_call_target="tpu_custom_call" | custom-call | flops 1000 | bytes 1000 | tf_op jit(solution)/shard_map/pallas_call | solution.py:454
  161.4 3.1 %shard_map.121 = (f32[2880,384]{1,0:T(8,128)S(1)}, bf16[2880,384]{1,0:T(8,128)(2,1)S(1)}) custom-call(s32[3]{0:T(128)S(1)} %pad_add_fusion.1.ids_ref, bf16[8,128,768]{2,1,0:T(8,128)(2,1)S(1)} %bitcast.28, bf16[2880,128]{1,0:T(8,128)(2,1)S(1)} %copy-done.30, bf16[2880,128]{1,0:T(8,128)(2,1)} %collective-permute-done.22.refs_1_, ...), custom_call_target="tpu_custom_call" | custom-call | flops 1000 | bytes 1000 | tf_op jit(solution)/shard_map/pallas_call | solution.py:454
  164.6 4.3 %collective-permute-done.24.mate_ref = bf16[2880,384]{1,0:T(8,128)(2,1)S(1)} collective-permute-done((bf16[2880,384]{1,0:T(8,128)(2,1)S(1)}, bf16[2880,384]{1,0:T(8,128)(2,1)S(1)}, u32[]{:S(2)}, u32[]{:S(2)}) %collective-permute-start.24) | collective-permute-done | bytes 2211872 | tf_op jit(solution)/shard_map/ppermute | solution.py:507
  168.9 4.3 %shard_map.122 = (bf16[2880,384]{1,0:T(8,128)(2,1)}, bf16[384,128]{1,0:T(8,128)(2,1)S(1)}) custom-call(f32[2880,384]{1,0:T(8,128)S(1)} %get-tuple-element.65.own_ref, bf16[2880,384]{1,0:T(8,128)(2,1)S(1)} %collective-permute-done.24.mate_ref, bf16[2880,384]{1,0:T(8,128)(2,1)S(1)} %bitcast.33, f32[2880,3]{1,0:T(8,128)S(1)} %bitcast.30, ...), custom_call_target="tpu_custom_call" | custom-call | flops 1000 | bytes 1000 | tf_op jit(solution)/shard_map/pallas_call | solution.py:494
  173.2 1.5 collective-permute-start.25
  174.8 3.3 %collective-permute-done.25 = bf16[384,128]{1,0:T(8,128)(2,1)S(1)} collective-permute-done((bf16[384,128]{1,0:T(8,128)(2,1)S(1)}, bf16[384,128]{1,0:T(8,128)(2,1)S(1)}, u32[]{:S(2)}, u32[]{:S(2)}) %collective-permute-start.25) | collective-permute-done | bytes 98336 | tf_op jit(solution)/shard_map/ppermute | solution.py:638
  (117 shorter events, 20.9 us)
Async XLA Ops:
  0.6 29.2 %copy-start.35 = (f32[1,2880]{1,0:T(1,128)S(1)}, f32[1,2880]{1,0:T(1,128)}, u32[]{:S(2)}) copy-start(f32[1,2880]{1,0:T(1,128)} %param.18) | copy-start | bytes 34564
  0.6 29.2 %copy-start.36 = (f32[1,2880]{1,0:T(1,128)S(1)}, f32[1,2880]{1,0:T(1,128)}, u32[]{:S(2)}) copy-start(f32[1,2880]{1,0:T(1,128)} %param.17) | copy-start | bytes 34564
  0.7 29.2 %copy-start.37 = (f32[1,2880]{1,0:T(1,128)S(1)}, f32[1,2880]{1,0:T(1,128)}, u32[]{:S(2)}) copy-start(f32[1,2880]{1,0:T(1,128)} %param.12) | copy-start | bytes 34564
  0.7 8.2 %collective-permute-start = (bf16[2880,384]{1,0:T(8,128)(2,1)}, bf16[2880,384]{1,0:T(8,128)(2,1)S(1)}, u32[]{:S(2)}, u32[]{:S(2)}) collective-permute-start(bf16[2880,384]{1,0:T(8,128)(2,1)} %bitcast.31), channel_id=1, source_target_pairs={{0,1},{1,0},{2,3},{3,2},{4,5},{5,4},{6,7},{7,6},{8,9},{9,8},{10,11... | collective-permute-start | bytes 6635528 | tf_op jit(solution)/shard_map/ppermute | solution.py:507
  1.2 14.1 %collective-permute-start.7 = (bf16[2880,128]{1,0:T(8,128)(2,1)}, bf16[2880,128]{1,0:T(8,128)(2,1)}, u32[]{:S(2)}, u32[]{:S(2)}) collective-permute-start(bf16[2880,128]{1,0:T(8,128)(2,1)} %bitcast.36), channel_id=1, source_target_pairs={{4,8},{5,9},{6,10},{7,11},{8,4},{9,5},{10,6},{11,7},{20,24},{21,25... | collective-permute-start | bytes 2211848 | tf_op jit(solution)/shard_map/ppermute | solution.py:507
  2.7 20.0 %collective-permute-start.4 = (bf16[2880,128]{1,0:T(8,128)(2,1)}, bf16[2880,128]{1,0:T(8,128)(2,1)}, u32[]{:S(2)}, u32[]{:S(2)}) collective-permute-start(bf16[2880,128]{1,0:T(8,128)(2,1)} %bitcast.37), channel_id=1, source_target_pairs={{0,2},{1,3},{2,0},{3,1},{4,6},{5,7},{6,4},{7,5},{8,10},{9,11},{10,... | collective-permute-start | bytes 2211848 | tf_op jit(solution)/shard_map/ppermute | solution.py:507
  5.2 20.5 %collective-permute-start.2 = (bf16[2880,128]{1,0:T(8,128)(2,1)}, bf16[2880,128]{1,0:T(8,128)(2,1)}, u32[]{:S(2)}, u32[]{:S(2)}) collective-permute-start(bf16[2880,128]{1,0:T(8,128)(2,1)} %bitcast.38), channel_id=1, source_target_pairs={{0,4},{1,5},{2,6},{3,7},{4,0},{5,1},{6,2},{7,3},{8,12},{9,13},{10,... | collective-permute-start | bytes 2211848 | tf_op jit(solution)/shard_map/ppermute | solution.py:507
  13.3 1.9 %collective-permute-start.1 = (bf16[180,1280]{1,0:T(8,128)(2,1)S(1)}, bf16[180,1280]{1,0:T(8,128)(2,1)S(1)}, u32[]{:S(2)}, u32[]{:S(2)}) collective-permute-start(bf16[180,1280]{1,0:T(8,128)(2,1)S(1)} %get-tuple-element.40), channel_id=1, source_target_pairs={{0,1},{1,0},{2,3},{3,2},{4,5},{5,4},{6,7},{7,6},{8,9},{9,8},{10,11... | collective-permute-start | bytes 1382408 | tf_op jit(solution)/shard_map/ppermute | solution.py:507
  25.7 21.8 %collective-permute-start.3 = (bf16[360,1280]{1,0:T(8,128)(2,1)S(1)}, bf16[360,1280]{1,0:T(8,128)(2,1)}, u32[]{:S(2)}, u32[]{:S(2)}) collective-permute-start(bf16[360,1280]{1,0:T(8,128)(2,1)S(1)} %pad_maximum_fusion.refs_0_), channel_id=1, source_target_pairs={{0,4},{1,5},{2,6},{3,7},{4,0},{5,1},{6,2},{7,3},{8,12},{9,13},{10,... | collective-permute-start | bytes 2764808 | tf_op jit(solution)/shard_map/ppermute | solution.py:507
  27.5 21.2 %collective-permute-start.5 = (bf16[360,1280]{1,0:T(8,128)(2,1)S(1)}, bf16[360,1280]{1,0:T(8,128)(2,1)}, u32[]{:S(2)}, u32[]{:S(2)}) collective-permute-start(bf16[360,1280]{1,0:T(8,128)(2,1)S(1)} %pad_maximum_fusion.refs_0_), channel_id=1, source_target_pairs={{0,2},{1,3},{2,0},{3,1},{4,6},{5,7},{6,4},{7,5},{8,10},{9,11},{10,... | collective-permute-start | bytes 2764808 | tf_op jit(solution)/shard_map/ppermute | solution.py:507
  28.0 21.4 %collective-permute-start.8 = (bf16[360,1280]{1,0:T(8,128)(2,1)S(1)}, bf16[360,1280]{1,0:T(8,128)(2,1)}, u32[]{:S(2)}, u32[]{:S(2)}) collective-permute-start(bf16[360,1280]{1,0:T(8,128)(2,1)S(1)} %pad_maximum_fusion.refs_0_), channel_id=1, source_target_pairs={{4,8},{5,9},{6,10},{7,11},{8,4},{9,5},{10,6},{11,7},{20,24},{21,25... | collective-permute-start | bytes 2764808 | tf_op jit(solution)/shard_map/ppermute | solution.py:507
  30.4 12.8 %copy-start.2 = (f32[3,2880]{0,1:T(8,128)}, f32[3,2880]{0,1:T(8,128)S(1)}, u32[]{:S(2)}) copy-start(f32[3,2880]{0,1:T(8,128)S(1)} %copy.23) | copy-start | bytes 103684
  31.2 1.6 copy-start.6
  32.8 1.6 copy-start.16
  44.3 30.3 %copy-start.17 = (bf16[4,768,180]{2,1,0:T(8,128)(2,1)}, bf16[4,768,180]{2,1,0:T(8,128)(2,1)S(1)}, u32[]{:S(2)}) copy-start(bf16[4,768,180]{2,1,0:T(8,128)(2,1)S(1)} %get-tuple-element.54.chunks_ref) | copy-start | bytes 3317764
  48.7 2.7 %collective-permute-start.6 = (bf16[360,1280]{1,0:T(8,128)(2,1)}, bf16[360,1280]{1,0:T(8,128)(2,1)S(1)}, u32[]{:S(2)}, u32[]{:S(2)}) collective-permute-start(bf16[360,1280]{1,0:T(8,128)(2,1)} %collective-permute-done.3.refs_2_), channel_id=1, source_target_pairs={{4,8},{5,9},{6,10},{7,11},{8,4},{9,5},{10,6},{11,7},{20,24},{21,25... | collective-permute-start | bytes 2764808 | tf_op jit(solution)/shard_map/ppermute | solution.py:507
  49.4 22.9 %collective-permute-start.9 = (bf16[360,1280]{1,0:T(8,128)(2,1)}, bf16[360,1280]{1,0:T(8,128)(2,1)S(1)}, u32[]{:S(2)}, u32[]{:S(2)}) collective-permute-start(bf16[360,1280]{1,0:T(8,128)(2,1)} %collective-permute-done.8.refs_0_), channel_id=1, source_target_pairs={{4,0},{5,1},{6,2},{7,3},{8,12},{9,13},{10,14},{11,15},{20,16},{21,... | collective-permute-start | bytes 2764808 | tf_op jit(solution)/shard_map/ppermute | solution.py:507
  50.7 23.9 %collective-permute-start.12 = (bf16[360,1280]{1,0:T(8,128)(2,1)}, bf16[360,1280]{1,0:T(8,128)(2,1)S(1)}, u32[]{:S(2)}, u32[]{:S(2)}) collective-permute-start(bf16[360,1280]{1,0:T(8,128)(2,1)} %collective-permute-done.3.refs_2_), channel_id=1, source_target_pairs={{0,2},{1,3},{2,0},{3,1},{4,6},{5,7},{6,4},{7,5},{8,10},{9,11},{10,... | collective-permute-start | bytes 2764808 | tf_op jit(solution)/shard_map/ppermute | solution.py:507
  51.4 31.5 %collective-permute-start.11 = (bf16[360,1280]{1,0:T(8,128)(2,1)}, bf16[360,1280]{1,0:T(8,128)(2,1)S(1)}, u32[]{:S(2)}, u32[]{:S(2)}) collective-permute-start(bf16[360,1280]{1,0:T(8,128)(2,1)} %collective-permute-done.5.refs_1_), channel_id=1, source_target_pairs={{4,8},{5,9},{6,10},{7,11},{8,4},{9,5},{10,6},{11,7},{20,24},{21,25... | collective-permute-start | bytes 2764808 | tf_op jit(solution)/shard_map/ppermute | solution.py:507
  72.5 19.7 %collective-permute-start.13 = (bf16[360,1280]{1,0:T(8,128)(2,1)S(1)}, bf16[360,1280]{1,0:T(8,128)(2,1)S(1)}, u32[]{:S(2)}, u32[]{:S(2)}) collective-permute-start(bf16[360,1280]{1,0:T(8,128)(2,1)S(1)} %add.71), channel_id=1, source_target_pairs={{0,2},{1,3},{2,0},{3,1},{4,6},{5,7},{6,4},{7,5},{8,10},{9,11},{10,... | collective-permute-start | bytes 2764808 | tf_op jit(solution)/shard_map/ppermute | solution.py:507
  73.3 21.4 %collective-permute-start.10 = (bf16[360,1280]{1,0:T(8,128)(2,1)S(1)}, bf16[360,1280]{1,0:T(8,128)(2,1)}, u32[]{:S(2)}, u32[]{:S(2)}) collective-permute-start(bf16[360,1280]{1,0:T(8,128)(2,1)S(1)} %collective-permute-done.6.refs_0_), channel_id=1, source_target_pairs={{4,0},{5,1},{6,2},{7,3},{8,12},{9,13},{10,14},{11,15},{20,16},{21,... | collective-permute-start | bytes 2764808 | tf_op jit(solution)/shard_map/ppermute | solution.py:507
  80.9 1.9 %copy-start = (f32[768,1280]{1,0:T(8,128)}, f32[768,1280]{1,0:T(8,128)S(1)}, u32[]{:S(2)}) copy-start(f32[768,1280]{1,0:T(8,128)S(1)} %shard_map.115.refs_3_) | copy-start | bytes 11796484
  94.7 23.8 %collective-permute-start.14 = (bf16[360,1280]{1,0:T(8,128)(2,1)}, bf16[360,1280]{1,0:T(8,128)(2,1)}, u32[]{:S(2)}, u32[]{:S(2)}) collective-permute-start(bf16[360,1280]{1,0:T(8,128)(2,1)} %collective-permute-done.10.refs_1_), channel_id=1, source_target_pairs={{0,2},{1,3},{2,0},{3,1},{12,14},{13,15},{14,12},{15,13},{16,18},{1... | collective-permute-start | bytes 2764808 | tf_op jit(solution)/shard_map/ppermute | solution.py:507
  97.8 18.0 %collective-permute-start.18 = (bf16[2880,128]{1,0:T(8,128)(2,1)}, bf16[2880,128]{1,0:T(8,128)(2,1)}, u32[]{:S(2)}, u32[]{:S(2)}) collective-permute-start(bf16[2880,128]{1,0:T(8,128)(2,1)} %collective-permute-done.2.refs_2_), channel_id=1, source_target_pairs={{4,8},{5,9},{6,10},{7,11},{8,4},{9,5},{10,6},{11,7},{20,24},{21,25... | collective-permute-start | bytes 2211848 | tf_op jit(solution)/shard_map/ppermute | solution.py:507
  99.4 16.5 %collective-permute-start.20 = (bf16[2880,128]{1,0:T(8,128)(2,1)}, bf16[2880,128]{1,0:T(8,128)(2,1)S(1)}, u32[]{:S(2)}, u32[]{:S(2)}) collective-permute-start(bf16[2880,128]{1,0:T(8,128)(2,1)} %collective-permute-done.7.refs_3_), channel_id=1, source_target_pairs={{4,0},{5,1},{6,2},{7,3},{8,12},{9,13},{10,14},{11,15},{20,16},{21,... | collective-permute-start | bytes 2211848 | tf_op jit(solution)/shard_map/ppermute | solution.py:507
  100.7 16.8 %collective-permute-start.17 = (bf16[2880,128]{1,0:T(8,128)(2,1)}, bf16[2880,128]{1,0:T(8,128)(2,1)S(1)}, u32[]{:S(2)}, u32[]{:S(2)}) collective-permute-start(bf16[2880,128]{1,0:T(8,128)(2,1)} %collective-permute-done.2.refs_2_), channel_id=1, source_target_pairs={{4,6},{5,7},{6,4},{7,5},{8,10},{9,11},{10,8},{11,9},{20,22},{21,23... | collective-permute-start | bytes 2211848 | tf_op jit(solution)/shard_map/ppermute | solution.py:507
  106.9 2.1 %copy-start.1 = (f32[768,1280]{1,0:T(8,128)S(1)}, f32[768,1280]{1,0:T(8,128)}, u32[]{:S(2)}) copy-start(f32[768,1280]{1,0:T(8,128)} %copy-done) | copy-start | bytes 11796484
  111.6 8.9 %copy-start.22 = (bf16[360,1280]{1,0:T(8,128)(2,1)S(1)}, bf16[360,1280]{1,0:T(8,128)(2,1)}, u32[]{:S(2)}) copy-start(bf16[360,1280]{1,0:T(8,128)(2,1)} %copy-done.21) | copy-start | bytes 2764804
  115.8 4.7 %copy-start.20 = (bf16[4,768,180]{2,1,0:T(8,128)(2,1)S(1)}, bf16[4,768,180]{2,1,0:T(8,128)(2,1)}, u32[]{:S(2)}) copy-start(bf16[4,768,180]{2,1,0:T(8,128)(2,1)} %copy-done.19) | copy-start | bytes 3317764
  115.9 4.7 %copy-start.11 = (bf16[2880,128]{1,0:T(8,128)(2,1)}, bf16[2880,128]{1,0:T(8,128)(2,1)S(1)}, u32[]{:S(2)}) copy-start(bf16[2880,128]{1,0:T(8,128)(2,1)S(1)} %collective-permute-done.20.refs_4_) | copy-start | bytes 2211844
  118.5 18.0 %collective-permute-start.19 = (bf16[2880,128]{1,0:T(8,128)(2,1)}, bf16[2880,128]{1,0:T(8,128)(2,1)S(1)}, u32[]{:S(2)}, u32[]{:S(2)}) collective-permute-start(bf16[2880,128]{1,0:T(8,128)(2,1)} %collective-permute-done.18.refs_6_), channel_id=1, source_target_pairs={{4,0},{5,1},{6,2},{7,3},{8,12},{9,13},{10,14},{11,15},{20,16},{21,... | collective-permute-start | bytes 2211848 | tf_op jit(solution)/shard_map/ppermute | solution.py:507
  119.8 19.8 %collective-permute-start.21 = (bf16[2880,128]{1,0:T(8,128)(2,1)S(1)}, bf16[2880,128]{1,0:T(8,128)(2,1)S(1)}, u32[]{:S(2)}, u32[]{:S(2)}) collective-permute-start(bf16[2880,128]{1,0:T(8,128)(2,1)S(1)} %add.77), channel_id=1, source_target_pairs={{0,2},{1,3},{2,0},{3,1},{4,6},{5,7},{6,4},{7,5},{8,10},{9,11},{10,... | collective-permute-start | bytes 2211848 | tf_op jit(solution)/shard_map/ppermute | solution.py:507
  126.3 16.9 %copy-start.4 = (bf16[768,256]{1,0:T(8,128)(2,1)}, bf16[768,256]{1,0:T(8,128)(2,1)S(1)}, u32[]{:S(2)}) copy-start(bf16[768,256]{1,0:T(8,128)(2,1)S(1)} %slice.17.own0_ref.own1_ref) | copy-start | bytes 1179652
  126.3 1.8 %collective-permute-start.15 = (bf16[768,256]{1,0:T(8,128)(2,1)S(1)}, bf16[768,256]{1,0:T(8,128)(2,1)S(1)}, u32[]{:S(2)}, u32[]{:S(2)}) collective-permute-start(bf16[768,256]{1,0:T(8,128)(2,1)S(1)} %slice.17.own0_ref.own1_ref), channel_id=1, source_target_pairs={{0,1},{1,0},{2,3},{3,2},{4,5},{5,4},{6,7},{7,6},{8,9},{9,8},{10,11... | collective-permute-start | bytes 1179656 | tf_op jit(solution)/shard_map/ppermute | solution.py:507
  128.1 15.1 %copy-start.8 = (bf16[768,256]{1,0:T(8,128)(2,1)}, bf16[768,256]{1,0:T(8,128)(2,1)S(1)}, u32[]{:S(2)}) copy-start(bf16[768,256]{1,0:T(8,128)(2,1)S(1)} %collective-permute-done.15.mate0_ref.mate1_ref) | copy-start | bytes 1179652
  128.1 10.9 %collective-permute-start.16 = (bf16[128,512]{1,0:T(8,128)(2,1)S(1)}, bf16[128,512]{1,0:T(8,128)(2,1)S(1)}, u32[]{:S(2)}, u32[]{:S(2)}) collective-permute-start(bf16[128,512]{1,0:T(8,128)(2,1)S(1)} %pad_maximum_fusion.1), channel_id=1, source_target_pairs={{0,2},{1,3},{2,4},{3,5},{4,6},{5,7},{6,8},{7,9},{8,10},{9,11},{10,... | collective-permute-start | bytes 393224 | tf_op jit(solution)/shard_map/ppermute | solution.py:507
  136.5 6.6 %copy-start.13 = (bf16[2880,128]{1,0:T(8,128)(2,1)}, bf16[2880,128]{1,0:T(8,128)(2,1)S(1)}, u32[]{:S(2)}) copy-start(bf16[2880,128]{1,0:T(8,128)(2,1)S(1)} %collective-permute-done.19.refs_7_) | copy-start | bytes 2211844
  140.5 20.9 %collective-permute-start.22 = (bf16[2880,128]{1,0:T(8,128)(2,1)}, bf16[2880,128]{1,0:T(8,128)(2,1)}, u32[]{:S(2)}, u32[]{:S(2)}) collective-permute-start(bf16[2880,128]{1,0:T(8,128)(2,1)} %collective-permute-done.4.refs_1_), channel_id=1, source_target_pairs={{4,0},{5,1},{6,2},{7,3},{8,12},{9,13},{10,14},{11,15},{20,16},{21,... | collective-permute-start | bytes 2211848 | tf_op jit(solution)/shard_map/ppermute | solution.py:507
  141.8 19.6 %collective-permute-start.23 = (bf16[2880,128]{1,0:T(8,128)(2,1)}, bf16[2880,128]{1,0:T(8,128)(2,1)}, u32[]{:S(2)}, u32[]{:S(2)}) collective-permute-start(bf16[2880,128]{1,0:T(8,128)(2,1)} %add.78), channel_id=1, source_target_pairs={{0,2},{1,3},{2,0},{3,1},{4,6},{5,7},{6,4},{7,5},{8,10},{9,11},{10,... | collective-permute-start | bytes 2211848 | tf_op jit(solution)/shard_map/ppermute | solution.py:507
  154.0 1.5 copy-start.14
  154.0 1.6 copy-start.26
  154.1 1.8 copy-start.28
  155.8 5.6 %copy-start.30 = (bf16[2880,128]{1,0:T(8,128)(2,1)S(1)}, bf16[2880,128]{1,0:T(8,128)(2,1)}, u32[]{:S(2)}) copy-start(bf16[2880,128]{1,0:T(8,128)(2,1)} %copy-done.29) | copy-start | bytes 2211844
  161.4 7.6 %copy-start.3 = (f32[3,2880]{0,1:T(8,128)S(1)}, f32[3,2880]{0,1:T(8,128)}, u32[]{:S(2)}) copy-start(f32[3,2880]{0,1:T(8,128)} %copy-done.2) | copy-start | bytes 103684
  161.4 7.5 %copy-start.7 = (bf16[1,384,2880]{1,2,0:T(8,128)(2,1)S(1)}, bf16[1,384,2880]{1,2,0:T(8,128)(2,1)}, u32[]{:S(2)}) copy-start(bf16[1,384,2880]{1,2,0:T(8,128)(2,1)} %param.10) | copy-start | bytes 6635524
  161.4 7.5 %copy-start.10 = (bf16[1,2880,128]{1,2,0:T(8,128)(2,1)S(1)}, bf16[1,2880,128]{1,2,0:T(8,128)(2,1)}, u32[]{:S(2)}) copy-start(bf16[1,2880,128]{1,2,0:T(8,128)(2,1)} %copy.24) | copy-start | bytes 2211844
  164.5 4.4 %collective-permute-start.24 = (bf16[2880,384]{1,0:T(8,128)(2,1)S(1)}, bf16[2880,384]{1,0:T(8,128)(2,1)S(1)}, u32[]{:S(2)}, u32[]{:S(2)}) collective-permute-start(bf16[2880,384]{1,0:T(8,128)(2,1)S(1)} %get-tuple-element.66), channel_id=1, source_target_pairs={{0,1},{1,0},{2,3},{3,2},{4,5},{5,4},{6,7},{7,6},{8,9},{9,8},{10,11... | collective-permute-start | bytes 6635528 | tf_op jit(solution)/shard_map/ppermute | solution.py:507
  173.2 4.8 %collective-permute-start.25 = (bf16[384,128]{1,0:T(8,128)(2,1)S(1)}, bf16[384,128]{1,0:T(8,128)(2,1)S(1)}, u32[]{:S(2)}, u32[]{:S(2)}) collective-permute-start(bf16[384,128]{1,0:T(8,128)(2,1)S(1)} %get-tuple-element.69), channel_id=1, source_target_pairs={{0,16},{16,0},{1,17},{17,1},{2,18},{18,2},{3,19},{19,3},{4,20},{20... | collective-permute-start | bytes 294920 | tf_op jit(solution)/shard_map/ppermute | solution.py:638
  (16 other events, 16.8 us)

commit v6 on v5

--- a/solution.py
+++ b/solution.py
@@ -153,12 +153,12 @@
     return lax.optimization_barrier((value, *others))[0]
 
 
-def call(kernel, out_shape, vmem, **spec):
+def call(kernel, out_shape, vmem, flops=1000, **spec):
     return pl.pallas_call(
         kernel,
         out_shape=out_shape,
         compiler_params=pltpu.CompilerParams(vmem_limit_bytes=vmem * MIB),
-        cost_estimate=pl.CostEstimate(flops=1000, bytes_accessed=1000, transcendentals=0),
+        cost_estimate=pl.CostEstimate(flops=flops, bytes_accessed=1000, transcendentals=0),
         **spec,
     )
 
@@ -404,6 +404,7 @@
         attend_kernel,
         jax.ShapeDtypeStruct((q_wide, rows), jnp.bfloat16),
         12,
+        flops=steps * 1600000000,
         input_output_aliases=aliases,
         **scalars(
             1, (steps,), specs, pl.BlockSpec((q_wide, WINDOW), lambda m, c: (0, m + start))
@@ -411,15 +412,18 @@
     )(core, *operands)
 
 
-def out_kernel(shape, first, last, ids_ref, attended_ref, *refs):
+def out_kernel(shape, first, side, ids_ref, attended_ref, *refs):
     refs = list(refs)
     units = [[refs.pop(0) for _ in range(n)] for n in shape]
     acc_ref = None if first else refs.pop(0)
     wide = units[0][0].shape[0]
     half = attended_ref.shape[2] // CORES
     step = wide // 5
-    core = ids_ref[len(shape)]
-    x = jnp.concatenate([attended_ref[ids_ref[k]] for k in range(len(shape))], axis=0)
+    lanes = slice(None)
+    if side is not None:
+        core = ids_ref[len(shape)]
+        lanes = pl.ds(pl.multiple_of((core ^ side) * half, LANES), half)
+    x = jnp.concatenate([attended_ref[ids_ref[k], :, lanes] for k in range(len(shape))], axis=0)
     for low in range(0, wide, step):
         rows = slice(low, low + step)
         parts = []
@@ -430,33 +434,21 @@
             parts.append(w)
         total = jnp.dot(jnp.concatenate(parts, axis=1), x, preferred_element_type=jnp.float32)
         if not first:
-            total = total + acc_ref[rows, :]
-        if last:
-            left, right = total[:, :half], total[:, half:]
-            refs[0][rows, :] = jnp.where(core == 0, left, right)
-            refs[1][rows, :] = jnp.where(core == 0, right, left).astype(jnp.bfloat16)
-        else:
-            refs[0][rows, :] = total
-
-
-def project(indices, attended, units, acc, last):
+            total = total + acc_ref[rows, lanes]
+        refs[0][rows, :] = total.astype(refs[0].dtype)
+
+
+def project(indices, attended, units, acc, side, dtype):
     operands = [attended] + [part for unit in units for part in unit]
     if acc is not None:
         operands.append(acc)
     wide, rows = units[0][0].shape[0], attended.shape[2]
-    shape = (wide, rows // CORES)
-    out_shape = jax.ShapeDtypeStruct((wide, rows), jnp.float32)
-    if last:
-        out_shape = (
-            jax.ShapeDtypeStruct(shape, jnp.float32), jax.ShapeDtypeStruct(shape, jnp.bfloat16)
-        )
-    vmem = pl.BlockSpec(memory_space=pltpu.VMEM)
     return call(
-        functools.partial(out_kernel, [len(unit) for unit in units], acc is None, last),
-        out_shape,
+        functools.partial(out_kernel, [len(unit) for unit in units], acc is None, side),
+        jax.ShapeDtypeStruct((wide, rows if side is None else rows // CORES), dtype),
         14,
         in_specs=resident(len(operands)),
-        out_specs=(vmem, vmem) if last else vmem,
+        out_specs=pl.BlockSpec(memory_space=pltpu.VMEM),
     )(indices, *operands)
 
 
@@ -626,10 +618,13 @@
     attended = attended.reshape(shards // CORES, -1, chip_rows)
 
     units = [[unit_out], [o_side], [o_near], [o_inner, o_from_inner], [o_round], [o_far, o_from_far]]
-    acc = project(jnp.concatenate([ids[:3], ids[4:7], core]), attended, units, None, False)
+    acc = project(jnp.concatenate([ids[:3], ids[4:7], core]), attended, units, None, None, jnp.float32)
     units = [[o_x_near, o_z_side], [o_last]]
-    own, mate = project(jnp.concatenate([ids[3:4], ids[7:], core]), attended, units, acc, True)
-    updated, verdict = close(own, move(mate, p.mate), hidden_t, gains, judge_t)
+    order = jnp.concatenate([ids[3:4], ids[7:], core])
+    mate = project(order, attended, units, acc, 1, jnp.bfloat16)
+    mate_sum = move(mate, p.mate)
+    own = project(order, attended, units, tied(acc, mate), 0, jnp.float32)
+    updated, verdict = close(own, mate_sum, hidden_t, gains, judge_t)
 
     members = lax.axis_size("member")
     summed = verdict.astype(jnp.float32)

time: 180 us -> 179 us (level)
  starting transfers between devices: 34 us -> 38.7 us
  local copies, waits for them, and re-layouts: 26.7 us -> 22.1 us
  waiting for transfers between devices: 61.2 us -> 57.8 us
  Pallas kernels: 47.4 us -> 49.7 us
    ppermute x25, starting transfers between devices: 32.4 us -> 37.2 us  [move(): return lax.ppermute(block, 'seq', route)]
    unnamed x76 -> x64, local copies, waits for them, and re-layouts: 22.8 us -> 18.2 us
    ppermute x25, waiting for transfers between devices: 57.9 us -> 54.5 us  [move(): return lax.ppermute(block, 'seq', route)]
    pallas_call x2 -> x3, Pallas kernels: 8.6 us -> 10.2 us  [project(): call(functools.partial(out_kernel, [len(unit) for unit in units], acc is...]
  transfers between devices with their start and end apart: 26 -> 26, of which waited for: 12 -> 13; matrix products, arithmetic and copies ran while one was open for 6% -> 7% of each run, Pallas kernels for 22% -> 24%
where the time goes in v6:
time: 179 us; the launch traced here: 178 us
  waiting for transfers between devices  57.8 us (32%)
  Pallas kernels  49.7 us (28%)
  starting transfers between devices  38.7 us (22%)
  local copies, waits for them, and re-layouts  22.1 us (12%)
  other arithmetic  8.85 us (5%)
    ppermute x25, waiting for transfers between devices, move(): return lax.ppermute(block, 'seq', route)  54.5 us
    ppermute x25, starting transfers between devices, move(): return lax.ppermute(block, 'seq', route)  37.2 us
    unnamed x64, local copies, waits for them, and re-layouts  18.2 us
    pallas_call x3, Pallas kernels, qkv_group(): call(functools.partial(qkv_kernel, [len(unit) for unit in units], first,...  15.9 us
    pallas_call x2, Pallas kernels, attend(): call(attend_kernel, jax.ShapeDtypeStruct((q_wide, rows), jnp.bfloat16), 1...  10.4 us
    pallas_call x3, Pallas kernels, project(): call(functools.partial(out_kernel, [len(unit) for unit in units], acc is...  10.2 us
    pallas_call x1, Pallas kernels, prepare(): call(prepare_kernel, [jax.ShapeDtypeStruct((n, CORES * rows, depth), jnp....  8.68 us
    pallas_call x1, Pallas kernels, close(): call(close_kernel, (jax.ShapeDtypeStruct((width, half), jnp.bfloat16), ja...  4.32 us
  transfers between devices with their start and end apart: 26, of which 13 were waited for; matrix products, arithmetic and copies ran while one was open for 7% of the time, Pallas kernels for 24%

profile of v6, /device:TPU:0, one launch (start us, length us, event | category | flops | bytes accessed | tf_op | source)
XLA Modules:
  0.0 178.3 jit_solution(5508392730757591909)
XLA Ops:
  1.2 1.5 collective-permute-start.7
  2.7 2.5 %collective-permute-start.4 = (bf16[2880,128]{1,0:T(8,128)(2,1)}, bf16[2880,128]{1,0:T(8,128)(2,1)}, u32[]{:S(2)}, u32[]{:S(2)}) collective-permute-start(bf16[2880,128]{1,0:T(8,128)(2,1)} %bitcast.38), channel_id=1, source_target_pairs={{0,2},{1,3},{2,0},{3,1},{4,6},{5,7},{6,4},{7,5},{8,10},{9,11},{10,... | collective-permute-start | bytes 2211848 | tf_op jit(solution)/shard_map/ppermute | solution.py:499
  5.2 3.6 %collective-permute-start.2 = (bf16[2880,128]{1,0:T(8,128)(2,1)}, bf16[2880,128]{1,0:T(8,128)(2,1)}, u32[]{:S(2)}, u32[]{:S(2)}) collective-permute-start(bf16[2880,128]{1,0:T(8,128)(2,1)} %bitcast.39), channel_id=1, source_target_pairs={{0,4},{1,5},{2,6},{3,7},{4,0},{5,1},{6,2},{7,3},{8,12},{9,13},{10,... | collective-permute-start | bytes 2211848 | tf_op jit(solution)/shard_map/ppermute | solution.py:499
  8.8 1.4 copy-done.11
  13.5 1.7 collective-permute-done.1
  15.3 7.4 %collective-permute-done.4.refs_1_ = bf16[2880,128]{1,0:T(8,128)(2,1)} collective-permute-done((bf16[2880,128]{1,0:T(8,128)(2,1)}, bf16[2880,128]{1,0:T(8,128)(2,1)}, u32[]{:S(2)}, u32[]{:S(2)}) %collective-permute-start.4) | collective-permute-done | bytes 737312 | tf_op jit(solution)/shard_map/ppermute | solution.py:499
  22.7 3.1 %collective-permute-done.2.refs_2_ = bf16[2880,128]{1,0:T(8,128)(2,1)} collective-permute-done((bf16[2880,128]{1,0:T(8,128)(2,1)}, bf16[2880,128]{1,0:T(8,128)(2,1)}, u32[]{:S(2)}, u32[]{:S(2)}) %collective-permute-start.2) | collective-permute-done | bytes 737312 | tf_op jit(solution)/shard_map/ppermute | solution.py:499
  25.7 1.7 collective-permute-start.3
  28.0 1.7 collective-permute-start.8
  31.1 1.6 copy-done.2
  32.7 1.6 copy-done.12
  34.3 8.7 %shard_map.113 = (bf16[8,768,180]{2,1,0:T(8,128)(2,1)S(1)}, bf16[4,768,180]{2,1,0:T(8,128)(2,1)S(1)}, bf16[4,768,180]{2,1,0:T(8,128)(2,1)S(1)}) custom-call(s32[17]{0:T(128)S(1)} %pad_add_fusion.2.slots_ref, bf16[2880,384]{1,0:T(8,128)(2,1)S(1)} %bitcast.33, bf16[2880,384]{1,0:T(8,128)(2,1)S(1)} %copy-done.12, f32[2880,1]{1,0:T(8,128)S(1)} %bitcast.30), custom_call_target="tpu_custom_call" | custom-call | flops 1000 | bytes 1000 | tf_op jit(solution)/shard_map/pallas_call | solution.py:247
  44.2 3.4 %collective-permute-done.3.refs_2_ = bf16[360,1280]{1,0:T(8,128)(2,1)} collective-permute-done((bf16[360,1280]{1,0:T(8,128)(2,1)S(1)}, bf16[360,1280]{1,0:T(8,128)(2,1)}, u32[]{:S(2)}, u32[]{:S(2)}) %collective-permute-start.3) | collective-permute-done | bytes 921632 | tf_op jit(solution)/shard_map/ppermute | solution.py:499
  49.5 1.4 collective-permute-start.9
  52.3 20.1 %collective-permute-done.9.refs_1_ = bf16[360,1280]{1,0:T(8,128)(2,1)S(1)} collective-permute-done((bf16[360,1280]{1,0:T(8,128)(2,1)}, bf16[360,1280]{1,0:T(8,128)(2,1)S(1)}, u32[]{:S(2)}, u32[]{:S(2)}) %collective-permute-start.9) | collective-permute-done | bytes 921632 | tf_op jit(solution)/shard_map/ppermute | solution.py:499
  73.4 1.3 collective-permute-start.10
  74.8 6.1 %shard_map.115.refs_3_ = f32[768,1280]{1,0:T(8,128)S(1)} custom-call(bf16[8,768,180]{2,1,0:T(8,128)(2,1)S(1)} %get-tuple-element.42.chunks_ref, bf16[360,1280]{1,0:T(8,128)(2,1)S(1)} %pad_maximum_fusion.refs_0_, bf16[360,1280]{1,0:T(8,128)(2,1)S(1)} %copy-done.24, bf16[360,1280]{1,0:T(8,128)(2,1)} %collective-permute-done.3.refs_2_, ...), custom_call_target="tpu_custom_call" | custom-call | flops 1000 | bytes 1000 | tf_op jit(solution)/shard_map/pallas_call | solution.py:322
  80.9 1.9 %copy-done = f32[768,1280]{1,0:T(8,128)} copy-done((f32[768,1280]{1,0:T(8,128)}, f32[768,1280]{1,0:T(8,128)S(1)}, u32[]{:S(2)}) %copy-start) | copy-done | bytes 3932184
  83.6 8.8 %collective-permute-done.13.refs_2_ = bf16[360,1280]{1,0:T(8,128)(2,1)S(1)} collective-permute-done((bf16[360,1280]{1,0:T(8,128)(2,1)S(1)}, bf16[360,1280]{1,0:T(8,128)(2,1)S(1)}, u32[]{:S(2)}, u32[]{:S(2)}) %collective-permute-start.13) | collective-permute-done | bytes 921632 | tf_op jit(solution)/shard_map/ppermute | solution.py:499
  93.4 1.4 collective-permute-done.10.refs_1_
  94.8 3.3 %collective-permute-start.14 = (bf16[360,1280]{1,0:T(8,128)(2,1)}, bf16[360,1280]{1,0:T(8,128)(2,1)}, u32[]{:S(2)}, u32[]{:S(2)}) collective-permute-start(bf16[360,1280]{1,0:T(8,128)(2,1)} %collective-permute-done.10.refs_1_), channel_id=1, source_target_pairs={{0,2},{1,3},{2,0},{3,1},{12,14},{13,15},{14,12},{15,13},{16,18},{1... | collective-permute-start | bytes 2764808 | tf_op jit(solution)/shard_map/ppermute | solution.py:499
  98.1 1.5 collective-permute-start.18
  99.6 1.3 collective-permute-start.20
  100.9 1.5 collective-permute-start.17
  104.1 2.3 %copy.24 = bf16[1,2880,128]{1,2,0:T(8,128)(2,1)} copy(bf16[1,2880,128]{2,1,0:T(8,128)(2,1)} %param.19) | data formatting | bytes 1474560 | tf_op jit(solution)/shard_map/optimization_barrier | solution.py:153
  106.3 1.4 fusion
  107.8 2.1 %copy-done.1 = f32[768,1280]{1,0:T(8,128)S(1)} copy-done((f32[768,1280]{1,0:T(8,128)S(1)}, f32[768,1280]{1,0:T(8,128)}, u32[]{:S(2)}) %copy-start.1) | copy-done | bytes 3932184
  109.9 1.4 copy-done.14
  112.5 4.2 %shard_map.116.refs_4_ = f32[768,1280]{1,0:T(8,128)S(1)} custom-call(bf16[4,768,180]{2,1,0:T(8,128)(2,1)S(1)} %copy-done.14, bf16[360,1280]{1,0:T(8,128)(2,1)} %collective-permute-done.8.refs_0_, bf16[360,1280]{1,0:T(8,128)(2,1)S(1)} %collective-permute-done.9.refs_1_, bf16[360,1280]{1,0:T(8,128)(2,1)S(1)} %copy-done.22, f32[768,1280]{1,0:T(8,128)S(1)} %copy-done.1), custom_call_target="tpu_custom_call" | custom-call | flops 1000 | bytes 1000 | tf_op jit(solution)/shard_map/pallas_call | solution.py:322
  116.7 2.5 %add.77 = bf16[2880,128]{1,0:T(8,128)(2,1)} add(bf16[2880,128]{1,0:T(8,128)(2,1)S(1)} %collective-permute-done.20.refs_4_, bf16[2880,128]{1,0:T(8,128)(2,1)} %collective-permute-done.18.refs_6_) | non-fusion elementwise | flops 368640 | bytes 2211840 | tf_op jit(solution)/shard_map/add | solution.py:603
  119.2 1.3 collective-permute-start.19
  121.2 5.7 %shard_map.117.q_ref = bf16[768,1280]{1,0:T(8,128)(2,1)S(1)} custom-call(bf16[4,768,180]{2,1,0:T(8,128)(2,1)S(1)} %copy-done.18, bf16[360,1280]{1,0:T(8,128)(2,1)S(1)} %copy-done.5, bf16[360,1280]{1,0:T(8,128)(2,1)} %collective-permute-done.10.refs_1_, bf16[360,1280]{1,0:T(8,128)(2,1)S(1)} %copy-done.20, bf16[360,1280]{1,0:T(8,128)(2,1)} %collective-permute-done.14.refs_3_, ...), custom_call_target="tpu_custom_call" | custom-call | flops 1000 | bytes 1000 | tf_op jit(solution)/shard_map/pallas_call | solution.py:322
  127.0 1.7 collective-permute-done.15.mate0_ref.mate1_ref
  130.3 4.0 %collective-permute-start.16 = (bf16[128,512]{1,0:T(8,128)(2,1)}, bf16[128,512]{1,0:T(8,128)(2,1)}, u32[]{:S(2)}, u32[]{:S(2)}) collective-permute-start(bf16[128,512]{1,0:T(8,128)(2,1)} %pad_maximum_fusion.1), channel_id=1, source_target_pairs={{0,2},{1,3},{2,4},{3,5},{4,6},{5,7},{6,8},{7,9},{8,10},{9,11},{10,... | collective-permute-start | bytes 393224 | tf_op jit(solution)/shard_map/ppermute | solution.py:499
  134.4 2.1 %collective-permute-done.19.refs_7_ = bf16[2880,128]{1,0:T(8,128)(2,1)} collective-permute-done((bf16[2880,128]{1,0:T(8,128)(2,1)}, bf16[2880,128]{1,0:T(8,128)(2,1)}, u32[]{:S(2)}, u32[]{:S(2)}) %collective-permute-start.19) | collective-permute-done | bytes 737312 | tf_op jit(solution)/shard_map/ppermute | solution.py:499
  136.6 1.5 add.78
  138.1 1.3 collective-permute-start.22
  139.4 4.5 %collective-permute-start.23 = (bf16[2880,128]{1,0:T(8,128)(2,1)S(1)}, bf16[2880,128]{1,0:T(8,128)(2,1)S(1)}, u32[]{:S(2)}, u32[]{:S(2)}) collective-permute-start(bf16[2880,128]{1,0:T(8,128)(2,1)S(1)} %add.78), channel_id=1, source_target_pairs={{0,2},{1,3},{2,0},{3,1},{4,6},{5,7},{6,4},{7,5},{8,10},{9,11},{10,... | collective-permute-start | bytes 2211848 | tf_op jit(solution)/shard_map/ppermute | solution.py:499
  143.9 7.9 %shard_map.118.out_refs_0_ = bf16[1024,768]{1,0:T(8,128)(2,1)S(1)} custom-call(s32[1]{0:T(128)} %bitcast.2.core_ref, bf16[768,1280]{1,0:T(8,128)(2,1)S(1)} %shard_map.117.q_ref, bf16[768,256]{1,0:T(8,128)(2,1)S(1)} %copy-done.7, bf16[768,256]{1,0:T(8,128)(2,1)S(1)} %copy-done.7, bf16[768,256]{1,0:T(8,128)(2,1)S(1)} %copy-done.16, ...), custom_call_target="tpu_custom_call" | custom-call | flops 8000000000 | bytes 1000 | tf_op jit(solution)/shard_map/pallas_call | solution.py:403
  151.8 2.5 %shard_map.119 = bf16[1024,768]{1,0:T(8,128)(2,1)S(1)} custom-call(s32[1]{0:T(128)} %bitcast.2.core_ref, bf16[768,1280]{1,0:T(8,128)(2,1)S(1)} %shard_map.117.q_ref, bf16[128,512]{1,0:T(8,128)(2,1)} %collective-permute-done.16.own0_ref.mate0_ref, bf16[768,256]{1,0:T(8,128)(2,1)S(1)} %copy-done.7, ...), custom_call_target="tpu_custom_call", output_to_operand_aliasing={{}: (9, {})} | custom-call | flops 1600000000 | bytes 1000 | tf_op jit(solution)/shard_map/pallas_call | solution.py:403
  154.4 5.8 %shard_map.120.refs_3_ = f32[2880,768]{1,0:T(8,128)S(1)} custom-call(s32[7]{0:T(128)S(1)} %concatenate.30.ids_ref, bf16[8,128,768]{2,1,0:T(8,128)(2,1)S(1)} %bitcast.27, bf16[2880,128]{1,0:T(8,128)(2,1)S(1)} %bitcast.40, bf16[2880,128]{1,0:T(8,128)(2,1)} %collective-permute-done.4.refs_1_, bf16[2880,128]{1,0:T(8,128)(2,1)} %collective-permute-done.2.refs_2_, ...), custom_call_target="tpu_custom_call" | custom-call | flops 1000 | bytes 1000 | tf_op jit(solution)/shard_map/pallas_call | solution.py:446
  160.2 1.7 collective-permute-done.22.refs_1_
  161.9 2.1 %shard_map.121 = bf16[2880,384]{1,0:T(8,128)(2,1)S(1)} custom-call(s32[3]{0:T(128)S(1)} %pad_add_fusion.1.ids_ref, bf16[8,128,768]{2,1,0:T(8,128)(2,1)S(1)} %bitcast.28, bf16[2880,128]{1,0:T(8,128)(2,1)} %collective-permute-done.17.refs_0_, bf16[2880,128]{1,0:T(8,128)(2,1)S(1)} %collective-permute-done.22.refs_1_, ...), custom_call_target="tpu_custom_call" | custom-call | flops 1000 | bytes 1000 | tf_op jit(solution)/shard_map/pallas_call | solution.py:446
  164.2 2.2 %shard_map.122.own_ref = f32[2880,384]{1,0:T(8,128)S(1)} custom-call(s32[3]{0:T(128)S(1)} %pad_add_fusion.1.ids_ref, bf16[8,128,768]{2,1,0:T(8,128)(2,1)S(1)} %bitcast.29, bf16[2880,128]{1,0:T(8,128)(2,1)} %collective-permute-done.17.refs_0_, bf16[2880,128]{1,0:T(8,128)(2,1)S(1)} %collective-permute-done.22.refs_1_, ...), custom_call_target="tpu_custom_call" | custom-call | flops 1000 | bytes 1000 | tf_op jit(solution)/shard_map/pallas_call | solution.py:446
  166.4 2.1 %collective-permute-done.24.mate_ref = bf16[2880,384]{1,0:T(8,128)(2,1)S(1)} collective-permute-done((bf16[2880,384]{1,0:T(8,128)(2,1)S(1)}, bf16[2880,384]{1,0:T(8,128)(2,1)S(1)}, u32[]{:S(2)}, u32[]{:S(2)}) %collective-permute-start.24) | collective-permute-done | bytes 2211872 | tf_op jit(solution)/shard_map/ppermute | solution.py:499
  168.5 4.3 %shard_map.123 = (bf16[2880,384]{1,0:T(8,128)(2,1)}, bf16[384,128]{1,0:T(8,128)(2,1)S(1)}) custom-call(f32[2880,384]{1,0:T(8,128)S(1)} %shard_map.122.own_ref, bf16[2880,384]{1,0:T(8,128)(2,1)S(1)} %collective-permute-done.24.mate_ref, bf16[2880,384]{1,0:T(8,128)(2,1)S(1)} %bitcast.34, f32[2880,3]{1,0:T(8,128)S(1)} %bitcast.31, bf16[128,2880]{1,0:T(8,128)(2,1)S(1)} %bitcast.35), custom_call_target="tpu_custom_call" | custom-call | flops 1000 | bytes 1000 | tf_op jit(solution)/shard_map/pallas_call | solution.py:486
  172.8 1.5 collective-permute-start.25
  174.3 3.3 %collective-permute-done.25 = bf16[384,128]{1,0:T(8,128)(2,1)S(1)} collective-permute-done((bf16[384,128]{1,0:T(8,128)(2,1)S(1)}, bf16[384,128]{1,0:T(8,128)(2,1)S(1)}, u32[]{:S(2)}, u32[]{:S(2)}) %collective-permute-start.25) | collective-permute-done | bytes 98336 | tf_op jit(solution)/shard_map/ppermute | solution.py:633
  (106 shorter events, 19.2 us)
Async XLA Ops:
  0.6 29.2 %copy-start.29 = (f32[1,2880]{1,0:T(1,128)S(1)}, f32[1,2880]{1,0:T(1,128)}, u32[]{:S(2)}) copy-start(f32[1,2880]{1,0:T(1,128)} %param.18) | copy-start | bytes 34564
  0.6 29.2 %copy-start.30 = (f32[1,2880]{1,0:T(1,128)S(1)}, f32[1,2880]{1,0:T(1,128)}, u32[]{:S(2)}) copy-start(f32[1,2880]{1,0:T(1,128)} %param.17) | copy-start | bytes 34564
  0.7 29.2 %copy-start.31 = (f32[1,2880]{1,0:T(1,128)S(1)}, f32[1,2880]{1,0:T(1,128)}, u32[]{:S(2)}) copy-start(f32[1,2880]{1,0:T(1,128)} %param.12) | copy-start | bytes 34564
  0.7 8.2 %collective-permute-start = (bf16[2880,384]{1,0:T(8,128)(2,1)}, bf16[2880,384]{1,0:T(8,128)(2,1)S(1)}, u32[]{:S(2)}, u32[]{:S(2)}) collective-permute-start(bf16[2880,384]{1,0:T(8,128)(2,1)} %bitcast.32), channel_id=1, source_target_pairs={{0,1},{1,0},{2,3},{3,2},{4,5},{5,4},{6,7},{7,6},{8,9},{9,8},{10,11... | collective-permute-start | bytes 6635528 | tf_op jit(solution)/shard_map/ppermute | solution.py:499
  1.2 14.1 %collective-permute-start.7 = (bf16[2880,128]{1,0:T(8,128)(2,1)}, bf16[2880,128]{1,0:T(8,128)(2,1)}, u32[]{:S(2)}, u32[]{:S(2)}) collective-permute-start(bf16[2880,128]{1,0:T(8,128)(2,1)} %bitcast.37), channel_id=1, source_target_pairs={{4,8},{5,9},{6,10},{7,11},{8,4},{9,5},{10,6},{11,7},{20,24},{21,25... | collective-permute-start | bytes 2211848 | tf_op jit(solution)/shard_map/ppermute | solution.py:499
  2.7 20.0 %collective-permute-start.4 = (bf16[2880,128]{1,0:T(8,128)(2,1)}, bf16[2880,128]{1,0:T(8,128)(2,1)}, u32[]{:S(2)}, u32[]{:S(2)}) collective-permute-start(bf16[2880,128]{1,0:T(8,128)(2,1)} %bitcast.38), channel_id=1, source_target_pairs={{0,2},{1,3},{2,0},{3,1},{4,6},{5,7},{6,4},{7,5},{8,10},{9,11},{10,... | collective-permute-start | bytes 2211848 | tf_op jit(solution)/shard_map/ppermute | solution.py:499
  5.2 20.5 %collective-permute-start.2 = (bf16[2880,128]{1,0:T(8,128)(2,1)}, bf16[2880,128]{1,0:T(8,128)(2,1)}, u32[]{:S(2)}, u32[]{:S(2)}) collective-permute-start(bf16[2880,128]{1,0:T(8,128)(2,1)} %bitcast.39), channel_id=1, source_target_pairs={{0,4},{1,5},{2,6},{3,7},{4,0},{5,1},{6,2},{7,3},{8,12},{9,13},{10,... | collective-permute-start | bytes 2211848 | tf_op jit(solution)/shard_map/ppermute | solution.py:499
  8.8 1.4 copy-start.11
  13.3 1.9 %collective-permute-start.1 = (bf16[180,1280]{1,0:T(8,128)(2,1)S(1)}, bf16[180,1280]{1,0:T(8,128)(2,1)S(1)}, u32[]{:S(2)}, u32[]{:S(2)}) collective-permute-start(bf16[180,1280]{1,0:T(8,128)(2,1)S(1)} %get-tuple-element.39), channel_id=1, source_target_pairs={{0,1},{1,0},{2,3},{3,2},{4,5},{5,4},{6,7},{7,6},{8,9},{9,8},{10,11... | collective-permute-start | bytes 1382408 | tf_op jit(solution)/shard_map/ppermute | solution.py:499
  25.7 21.8 %collective-permute-start.3 = (bf16[360,1280]{1,0:T(8,128)(2,1)S(1)}, bf16[360,1280]{1,0:T(8,128)(2,1)}, u32[]{:S(2)}, u32[]{:S(2)}) collective-permute-start(bf16[360,1280]{1,0:T(8,128)(2,1)S(1)} %pad_maximum_fusion.refs_0_), channel_id=1, source_target_pairs={{0,4},{1,5},{2,6},{3,7},{4,0},{5,1},{6,2},{7,3},{8,12},{9,13},{10,... | collective-permute-start | bytes 2764808 | tf_op jit(solution)/shard_map/ppermute | solution.py:499
  27.5 21.1 %collective-permute-start.5 = (bf16[360,1280]{1,0:T(8,128)(2,1)S(1)}, bf16[360,1280]{1,0:T(8,128)(2,1)S(1)}, u32[]{:S(2)}, u32[]{:S(2)}) collective-permute-start(bf16[360,1280]{1,0:T(8,128)(2,1)S(1)} %pad_maximum_fusion.refs_0_), channel_id=1, source_target_pairs={{0,2},{1,3},{2,0},{3,1},{4,6},{5,7},{6,4},{7,5},{8,10},{9,11},{10,... | collective-permute-start | bytes 2764808 | tf_op jit(solution)/shard_map/ppermute | solution.py:499
  28.0 21.5 %collective-permute-start.8 = (bf16[360,1280]{1,0:T(8,128)(2,1)S(1)}, bf16[360,1280]{1,0:T(8,128)(2,1)}, u32[]{:S(2)}, u32[]{:S(2)}) collective-permute-start(bf16[360,1280]{1,0:T(8,128)(2,1)S(1)} %pad_maximum_fusion.refs_0_), channel_id=1, source_target_pairs={{4,8},{5,9},{6,10},{7,11},{8,4},{9,5},{10,6},{11,7},{20,24},{21,25... | collective-permute-start | bytes 2764808 | tf_op jit(solution)/shard_map/ppermute | solution.py:499
  31.1 1.6 copy-start.2
  32.7 1.6 copy-start.12
  44.2 30.6 %copy-start.13 = (bf16[4,768,180]{2,1,0:T(8,128)(2,1)}, bf16[4,768,180]{2,1,0:T(8,128)(2,1)S(1)}, u32[]{:S(2)}) copy-start(bf16[4,768,180]{2,1,0:T(8,128)(2,1)S(1)} %get-tuple-element.53.chunks_ref) | copy-start | bytes 3317764
  48.6 3.0 %collective-permute-start.6 = (bf16[360,1280]{1,0:T(8,128)(2,1)}, bf16[360,1280]{1,0:T(8,128)(2,1)S(1)}, u32[]{:S(2)}, u32[]{:S(2)}) collective-permute-start(bf16[360,1280]{1,0:T(8,128)(2,1)} %collective-permute-done.3.refs_2_), channel_id=1, source_target_pairs={{4,8},{5,9},{6,10},{7,11},{8,4},{9,5},{10,6},{11,7},{20,24},{21,25... | collective-permute-start | bytes 2764808 | tf_op jit(solution)/shard_map/ppermute | solution.py:499
  49.5 25.2 %copy-start.24 = (bf16[360,1280]{1,0:T(8,128)(2,1)S(1)}, bf16[360,1280]{1,0:T(8,128)(2,1)}, u32[]{:S(2)}) copy-start(bf16[360,1280]{1,0:T(8,128)(2,1)} %copy-done.23) | copy-start | bytes 2764804
  49.5 22.9 %collective-permute-start.9 = (bf16[360,1280]{1,0:T(8,128)(2,1)}, bf16[360,1280]{1,0:T(8,128)(2,1)S(1)}, u32[]{:S(2)}, u32[]{:S(2)}) collective-permute-start(bf16[360,1280]{1,0:T(8,128)(2,1)} %collective-permute-done.8.refs_0_), channel_id=1, source_target_pairs={{4,0},{5,1},{6,2},{7,3},{8,12},{9,13},{10,14},{11,15},{20,16},{21,... | collective-permute-start | bytes 2764808 | tf_op jit(solution)/shard_map/ppermute | solution.py:499
  50.9 23.8 %collective-permute-start.12 = (bf16[360,1280]{1,0:T(8,128)(2,1)}, bf16[360,1280]{1,0:T(8,128)(2,1)S(1)}, u32[]{:S(2)}, u32[]{:S(2)}) collective-permute-start(bf16[360,1280]{1,0:T(8,128)(2,1)} %collective-permute-done.3.refs_2_), channel_id=1, source_target_pairs={{0,2},{1,3},{2,0},{3,1},{4,6},{5,7},{6,4},{7,5},{8,10},{9,11},{10,... | collective-permute-start | bytes 2764808 | tf_op jit(solution)/shard_map/ppermute | solution.py:499
  51.6 29.2 %copy-start.4 = (bf16[360,1280]{1,0:T(8,128)(2,1)}, bf16[360,1280]{1,0:T(8,128)(2,1)S(1)}, u32[]{:S(2)}) copy-start(bf16[360,1280]{1,0:T(8,128)(2,1)S(1)} %collective-permute-done.6.refs_0_) | copy-start | bytes 2764804
  51.6 31.1 %collective-permute-start.11 = (bf16[360,1280]{1,0:T(8,128)(2,1)}, bf16[360,1280]{1,0:T(8,128)(2,1)S(1)}, u32[]{:S(2)}, u32[]{:S(2)}) collective-permute-start(bf16[360,1280]{1,0:T(8,128)(2,1)} %copy-done.23), channel_id=1, source_target_pairs={{4,8},{5,9},{6,10},{7,11},{8,4},{9,5},{10,6},{11,7},{20,24},{21,25... | collective-permute-start | bytes 2764808 | tf_op jit(solution)/shard_map/ppermute | solution.py:499
  72.7 19.8 %collective-permute-start.13 = (bf16[360,1280]{1,0:T(8,128)(2,1)S(1)}, bf16[360,1280]{1,0:T(8,128)(2,1)S(1)}, u32[]{:S(2)}, u32[]{:S(2)}) collective-permute-start(bf16[360,1280]{1,0:T(8,128)(2,1)S(1)} %add.71), channel_id=1, source_target_pairs={{0,2},{1,3},{2,0},{3,1},{4,6},{5,7},{6,4},{7,5},{8,10},{9,11},{10,... | collective-permute-start | bytes 2764808 | tf_op jit(solution)/shard_map/ppermute | solution.py:499
  73.4 21.3 %collective-permute-start.10 = (bf16[360,1280]{1,0:T(8,128)(2,1)S(1)}, bf16[360,1280]{1,0:T(8,128)(2,1)}, u32[]{:S(2)}, u32[]{:S(2)}) collective-permute-start(bf16[360,1280]{1,0:T(8,128)(2,1)S(1)} %collective-permute-done.6.refs_0_), channel_id=1, source_target_pairs={{4,0},{5,1},{6,2},{7,3},{8,12},{9,13},{10,14},{11,15},{20,16},{21,... | collective-permute-start | bytes 2764808 | tf_op jit(solution)/shard_map/ppermute | solution.py:499
  80.8 1.9 %copy-start = (f32[768,1280]{1,0:T(8,128)}, f32[768,1280]{1,0:T(8,128)S(1)}, u32[]{:S(2)}) copy-start(f32[768,1280]{1,0:T(8,128)S(1)} %shard_map.115.refs_3_) | copy-start | bytes 11796484
  94.8 24.5 %collective-permute-start.14 = (bf16[360,1280]{1,0:T(8,128)(2,1)}, bf16[360,1280]{1,0:T(8,128)(2,1)}, u32[]{:S(2)}, u32[]{:S(2)}) collective-permute-start(bf16[360,1280]{1,0:T(8,128)(2,1)} %collective-permute-done.10.refs_1_), channel_id=1, source_target_pairs={{0,2},{1,3},{2,0},{3,1},{12,14},{13,15},{14,12},{15,13},{16,18},{1... | collective-permute-start | bytes 2764808 | tf_op jit(solution)/shard_map/ppermute | solution.py:499
  98.1 18.6 %collective-permute-start.18 = (bf16[2880,128]{1,0:T(8,128)(2,1)}, bf16[2880,128]{1,0:T(8,128)(2,1)}, u32[]{:S(2)}, u32[]{:S(2)}) collective-permute-start(bf16[2880,128]{1,0:T(8,128)(2,1)} %collective-permute-done.2.refs_2_), channel_id=1, source_target_pairs={{4,8},{5,9},{6,10},{7,11},{8,4},{9,5},{10,6},{11,7},{20,24},{21,25... | collective-permute-start | bytes 2211848 | tf_op jit(solution)/shard_map/ppermute | solution.py:499
  99.6 17.1 %collective-permute-start.20 = (bf16[2880,128]{1,0:T(8,128)(2,1)}, bf16[2880,128]{1,0:T(8,128)(2,1)S(1)}, u32[]{:S(2)}, u32[]{:S(2)}) collective-permute-start(bf16[2880,128]{1,0:T(8,128)(2,1)} %collective-permute-done.7.refs_3_), channel_id=1, source_target_pairs={{4,0},{5,1},{6,2},{7,3},{8,12},{9,13},{10,14},{11,15},{20,16},{21,... | collective-permute-start | bytes 2211848 | tf_op jit(solution)/shard_map/ppermute | solution.py:499
  100.9 18.3 %collective-permute-start.17 = (bf16[2880,128]{1,0:T(8,128)(2,1)}, bf16[2880,128]{1,0:T(8,128)(2,1)}, u32[]{:S(2)}, u32[]{:S(2)}) collective-permute-start(bf16[2880,128]{1,0:T(8,128)(2,1)} %collective-permute-done.2.refs_2_), channel_id=1, source_target_pairs={{4,6},{5,7},{6,4},{7,5},{8,10},{9,11},{10,8},{11,9},{20,22},{21,23... | collective-permute-start | bytes 2211848 | tf_op jit(solution)/shard_map/ppermute | solution.py:499
  107.8 2.1 %copy-start.1 = (f32[768,1280]{1,0:T(8,128)S(1)}, f32[768,1280]{1,0:T(8,128)}, u32[]{:S(2)}) copy-start(f32[768,1280]{1,0:T(8,128)} %copy-done) | copy-start | bytes 11796484
  109.9 1.4 copy-start.14
  112.5 8.7 %copy-start.18 = (bf16[4,768,180]{2,1,0:T(8,128)(2,1)S(1)}, bf16[4,768,180]{2,1,0:T(8,128)(2,1)}, u32[]{:S(2)}) copy-start(bf16[4,768,180]{2,1,0:T(8,128)(2,1)} %copy-done.17) | copy-start | bytes 3317764
  116.7 4.5 %copy-start.5 = (bf16[360,1280]{1,0:T(8,128)(2,1)S(1)}, bf16[360,1280]{1,0:T(8,128)(2,1)}, u32[]{:S(2)}) copy-start(bf16[360,1280]{1,0:T(8,128)(2,1)} %copy-done.4) | copy-start | bytes 2764804
  116.7 4.5 %copy-start.20 = (bf16[360,1280]{1,0:T(8,128)(2,1)S(1)}, bf16[360,1280]{1,0:T(8,128)(2,1)}, u32[]{:S(2)}) copy-start(bf16[360,1280]{1,0:T(8,128)(2,1)} %copy-done.19) | copy-start | bytes 2764804
  116.7 4.4 %copy-start.9 = (bf16[2880,128]{1,0:T(8,128)(2,1)}, bf16[2880,128]{1,0:T(8,128)(2,1)S(1)}, u32[]{:S(2)}) copy-start(bf16[2880,128]{1,0:T(8,128)(2,1)S(1)} %collective-permute-done.20.refs_4_) | copy-start | bytes 2211844
  119.2 17.3 %collective-permute-start.19 = (bf16[2880,128]{1,0:T(8,128)(2,1)}, bf16[2880,128]{1,0:T(8,128)(2,1)}, u32[]{:S(2)}, u32[]{:S(2)}) collective-permute-start(bf16[2880,128]{1,0:T(8,128)(2,1)} %collective-permute-done.18.refs_6_), channel_id=1, source_target_pairs={{4,0},{5,1},{6,2},{7,3},{8,12},{9,13},{10,14},{11,15},{20,16},{21,... | collective-permute-start | bytes 2211848 | tf_op jit(solution)/shard_map/ppermute | solution.py:499
  120.5 17.6 %collective-permute-start.21 = (bf16[2880,128]{1,0:T(8,128)(2,1)}, bf16[2880,128]{1,0:T(8,128)(2,1)}, u32[]{:S(2)}, u32[]{:S(2)}) collective-permute-start(bf16[2880,128]{1,0:T(8,128)(2,1)} %add.77), channel_id=1, source_target_pairs={{0,2},{1,3},{2,0},{3,1},{4,6},{5,7},{6,4},{7,5},{8,10},{9,11},{10,... | collective-permute-start | bytes 2211848 | tf_op jit(solution)/shard_map/ppermute | solution.py:499
  126.9 1.8 %collective-permute-start.15 = (bf16[768,256]{1,0:T(8,128)(2,1)S(1)}, bf16[768,256]{1,0:T(8,128)(2,1)S(1)}, u32[]{:S(2)}, u32[]{:S(2)}) collective-permute-start(bf16[768,256]{1,0:T(8,128)(2,1)S(1)} %slice.17.own0_ref.own1_ref), channel_id=1, source_target_pairs={{0,1},{1,0},{2,3},{3,2},{4,5},{5,4},{6,7},{7,6},{8,9},{9,8},{10,11... | collective-permute-start | bytes 1179656 | tf_op jit(solution)/shard_map/ppermute | solution.py:499
  130.3 7.8 %collective-permute-start.16 = (bf16[128,512]{1,0:T(8,128)(2,1)}, bf16[128,512]{1,0:T(8,128)(2,1)}, u32[]{:S(2)}, u32[]{:S(2)}) collective-permute-start(bf16[128,512]{1,0:T(8,128)(2,1)} %pad_maximum_fusion.1), channel_id=1, source_target_pairs={{0,2},{1,3},{2,4},{3,5},{4,6},{5,7},{6,8},{7,9},{8,10},{9,11},{10,... | collective-permute-start | bytes 393224 | tf_op jit(solution)/shard_map/ppermute | solution.py:499
  134.4 9.6 %copy-start.7 = (bf16[768,256]{1,0:T(8,128)(2,1)S(1)}, bf16[768,256]{1,0:T(8,128)(2,1)}, u32[]{:S(2)}) copy-start(bf16[768,256]{1,0:T(8,128)(2,1)} %copy-done.6) | copy-start | bytes 1179652
  134.4 9.6 %copy-start.16 = (bf16[768,256]{1,0:T(8,128)(2,1)S(1)}, bf16[768,256]{1,0:T(8,128)(2,1)}, u32[]{:S(2)}) copy-start(bf16[768,256]{1,0:T(8,128)(2,1)} %copy-done.15) | copy-start | bytes 1179652
  138.1 23.8 %collective-permute-start.22 = (bf16[2880,128]{1,0:T(8,128)(2,1)}, bf16[2880,128]{1,0:T(8,128)(2,1)S(1)}, u32[]{:S(2)}, u32[]{:S(2)}) collective-permute-start(bf16[2880,128]{1,0:T(8,128)(2,1)} %collective-permute-done.4.refs_1_), channel_id=1, source_target_pairs={{4,0},{5,1},{6,2},{7,3},{8,12},{9,13},{10,14},{11,15},{20,16},{21,... | collective-permute-start | bytes 2211848 | tf_op jit(solution)/shard_map/ppermute | solution.py:499
  139.4 22.5 %collective-permute-start.23 = (bf16[2880,128]{1,0:T(8,128)(2,1)S(1)}, bf16[2880,128]{1,0:T(8,128)(2,1)S(1)}, u32[]{:S(2)}, u32[]{:S(2)}) collective-permute-start(bf16[2880,128]{1,0:T(8,128)(2,1)S(1)} %add.78), channel_id=1, source_target_pairs={{0,2},{1,3},{2,0},{3,1},{4,6},{5,7},{6,4},{7,5},{8,10},{9,11},{10,... | collective-permute-start | bytes 2211848 | tf_op jit(solution)/shard_map/ppermute | solution.py:499
  151.8 2.5 %copy-start.10 = (bf16[2880,128]{1,0:T(8,128)(2,1)S(1)}, bf16[2880,128]{1,0:T(8,128)(2,1)}, u32[]{:S(2)}) copy-start(bf16[2880,128]{1,0:T(8,128)(2,1)} %copy-done.9) | copy-start | bytes 2211844
  151.8 2.5 %copy-start.26 = (bf16[1,128,2880]{1,2,0:T(8,128)(2,1)S(1)}, bf16[1,128,2880]{1,2,0:T(8,128)(2,1)}, u32[]{:S(2)}) copy-start(bf16[1,128,2880]{1,2,0:T(8,128)(2,1)} %param.16) | copy-start | bytes 2211844
  164.1 4.4 %copy-start.3 = (bf16[1,384,2880]{1,2,0:T(8,128)(2,1)S(1)}, bf16[1,384,2880]{1,2,0:T(8,128)(2,1)}, u32[]{:S(2)}) copy-start(bf16[1,384,2880]{1,2,0:T(8,128)(2,1)} %param.10) | copy-start | bytes 6635524
  164.1 4.4 %copy-start.8 = (bf16[1,2880,128]{1,2,0:T(8,128)(2,1)S(1)}, bf16[1,2880,128]{1,2,0:T(8,128)(2,1)}, u32[]{:S(2)}) copy-start(bf16[1,2880,128]{1,2,0:T(8,128)(2,1)} %copy.24) | copy-start | bytes 2211844
  164.1 4.4 %collective-permute-start.24 = (bf16[2880,384]{1,0:T(8,128)(2,1)S(1)}, bf16[2880,384]{1,0:T(8,128)(2,1)S(1)}, u32[]{:S(2)}, u32[]{:S(2)}) collective-permute-start(bf16[2880,384]{1,0:T(8,128)(2,1)S(1)} %shard_map.121), channel_id=1, source_target_pairs={{0,1},{1,0},{2,3},{3,2},{4,5},{5,4},{6,7},{7,6},{8,9},{9,8},{10,11... | collective-permute-start | bytes 6635528 | tf_op jit(solution)/shard_map/ppermute | solution.py:499
  172.8 4.8 %collective-permute-start.25 = (bf16[384,128]{1,0:T(8,128)(2,1)S(1)}, bf16[384,128]{1,0:T(8,128)(2,1)S(1)}, u32[]{:S(2)}, u32[]{:S(2)}) collective-permute-start(bf16[384,128]{1,0:T(8,128)(2,1)S(1)} %get-tuple-element.67), channel_id=1, source_target_pairs={{0,16},{16,0},{1,17},{17,1},{2,18},{18,2},{3,19},{19,3},{4,20},{20... | collective-permute-start | bytes 294920 | tf_op jit(solution)/shard_map/ppermute | solution.py:633
  (10 other events, 9.6 us)
